TPU v7x, 128 devices: a whole 4x4x4 slice. The times are simulated.
128 devices in a mesh: gx: 16 (over z, x), gy: 8 (over y, core).
Axes of the slice: x: 4, y: 4, z: 4, core: 2. Of those that a mesh axis runs over, the one named last changes fastest.
Arguments:
- adj_fields: float32 [3, 8192, 4096], P(None, 'gx', 'gy'), may hold values from -6 to 6
- depth: float32 [8192, 4096], P('gx', 'gy'), may hold values from 0.2 to 1
- block_x: float32 [64, 128, 128], replicated
- reduced_x: float32 [128, 128], replicated
- block_y: float32 [32, 128, 128], replicated
- reduced_y: float32 [64, 64], replicated
- basis: float32 [4, 32, 128], replicated, may hold values from -0.09375 to 0.09375
- coef: float32 [2048, 8, 4], replicated, may hold values from -1 to 1
- footprint: int32 [2048, 8], replicated, may hold values from 0 to 8191, as said below
- owner: int32 [2048], replicated, may hold values from 0 to 2047, each once
- wet: int32 [256, 32], P('gx', 'gy'), may hold values 0 or 1
Outputs:
- adj_before: float32 [3, 8192, 4096], P(None, 'gx', 'gy')
- grad: float32 [2048], P(('gx', 'gy'))
Inputs may be any that keep to these rules, and one draw needn't show every extreme that they name: Each subfault's footprint is a patch of 2 x 4 neighbouring tiles, numbered tile row * 32 + tile column.
All inputs are finite; a program needn't handle non-finite values. No bound on the sum of `wet` on one device may be relied on, other than what follows from the above.
Results may differ from a plain program's by a relative error of at most 0.00021.
Values sent between devices are 32-bit elements; how exact they have to be, the bound alone decides.
No kernel may reach another device: no remote copies, remote signals or barrier semaphores. Data moves between devices by JAX's collectives and lax.ppermute only.
A program may use at most 128 MiB of HBM per device.

v0:
```python
import jax
import jax.numpy as jnp
from jax import lax
from jax.sharding import PartitionSpec as P

courant = 0.5


def shifted(block, axis, distance):
    devices = range(lax.axis_size(axis))
    route = [(i - distance, i) for i in devices if i - distance in devices]
    return lax.ppermute(block, axis, route)


def solve_last(lines, blocks, reduced):
    count = lines.shape[0]
    nblk = blocks.shape[0]
    width = blocks.shape[1]
    split = lines.reshape(count, nblk, width)
    inner = jnp.einsum("cjk,mck->mcj", blocks, split, precision=lax.Precision.HIGHEST)
    ends = jnp.stack((inner[:, :, 0], inner[:, :, width - 1]), axis=2).reshape(count, 2 * nblk)
    coupled = jnp.dot(ends, reduced.T, precision=lax.Precision.HIGHEST).reshape(count, nblk, 2)
    result = (
        inner
        + coupled[:, :, 0:1] * blocks[None, :, :, 0]
        + coupled[:, :, 1:2] * blocks[None, :, :, width - 1]
    )
    return result.reshape(count, nblk * width)


def solve_first(lines, blocks, reduced):
    length, count = lines.shape
    nblk = blocks.shape[0]
    width = blocks.shape[1]
    split = lines.reshape(nblk, width, count)
    inner = jnp.einsum("cjk,ckm->cjm", blocks, split, precision=lax.Precision.HIGHEST)
    ends = jnp.stack((inner[:, 0, :], inner[:, width - 1, :]), axis=1).reshape(2 * nblk, count)
    coupled = jnp.dot(reduced, ends, precision=lax.Precision.HIGHEST).reshape(nblk, 2, count)
    result = (
        inner
        + coupled[:, 0:1, :] * blocks[:, :, 0:1]
        + coupled[:, 1:2, :] * blocks[:, :, width - 1 : width]
    )
    return result.reshape(length, count)


def body(
    adj_fields, depth, block_x, reduced_x, block_y, reduced_y, basis, coef, footprint, owner, wet
):
    elev_in = adj_fields[0]
    row_flux = adj_fields[1]
    col_flux = adj_fields[2]
    rows_dev, cols_dev = row_flux.shape
    size_x = lax.axis_size("gx")
    size_y = lax.axis_size("gy")
    index_x = lax.axis_index("gx")
    index_y = lax.axis_index("gy")
    sectioned_x = row_flux.reshape(rows_dev, size_x, cols_dev // size_x)
    solved = solve_first(
        lax.all_to_all(sectioned_x, "gx", split_axis=1, concat_axis=0, tiled=True)[:, 0, :],
        block_x,
        reduced_x,
    )
    done_x = lax.all_to_all(solved[:, None, :], "gx", split_axis=0, concat_axis=1, tiled=True)
    flux_x = done_x.reshape(rows_dev, cols_dev)
    sectioned_y = col_flux.reshape(size_y, rows_dev // size_y, cols_dev)
    solved = solve_last(
        lax.all_to_all(sectioned_y, "gy", split_axis=0, concat_axis=2, tiled=True)[0],
        block_y,
        reduced_y,
    )
    done_y = lax.all_to_all(solved[None], "gy", split_axis=2, concat_axis=0, tiled=True)
    flux_y = done_y.reshape(rows_dev, cols_dev)
    weighted_x = depth * flux_x
    weighted_y = depth * flux_y
    below_row = shifted(weighted_x[rows_dev - 1 :], "gx", 1)
    below_col = shifted(weighted_y[:, cols_dev - 1 :], "gy", 1)
    back_x = weighted_x - jnp.concatenate([below_row, weighted_x[:-1]], axis=0)
    back_y = weighted_y - jnp.concatenate([below_col, weighted_y[:, :-1]], axis=1)
    elev = elev_in + courant * (back_x + back_y)
    above_row = shifted(elev[:1], "gx", -1)
    above_col = shifted(elev[:, :1], "gy", -1)
    fore_x = jnp.concatenate([elev[1:], above_row], axis=0) - elev
    fore_y = jnp.concatenate([elev[:, 1:], above_col], axis=1) - elev
    adj_before = jnp.stack([elev, flux_x + courant * fore_x, flux_y + courant * fore_y])
    modes, tile_h, tile_w = basis.shape
    tiles_x = rows_dev // tile_h
    tiles_y = cols_dev // tile_w
    tiled = elev.reshape(tiles_x, tile_h, tiles_y, tile_w)
    moments = jnp.einsum("ahbw,khw->abk", tiled, basis, precision=lax.Precision.HIGHEST)
    moments = moments * wet[:, :, None].astype(jnp.float32)
    faults = coef.shape[0]
    total_cols = tiles_y * size_y
    tile_row = footprint // total_cols
    tile_col = footprint % total_cols
    local_row = tile_row - index_x * tiles_x
    local_col = tile_col - index_y * tiles_y
    inside = (local_row >= 0) & (local_row < tiles_x) & (local_col >= 0) & (local_col < tiles_y)
    flat = jnp.where(inside, local_row * tiles_y + local_col, -1)
    numbers = jnp.arange(tiles_x * tiles_y, dtype=jnp.int32)
    matches = (flat[:, :, None] == numbers[None, None, :]).astype(jnp.float32)
    picked = jnp.einsum(
        "fpt,tb->fpb",
        matches,
        moments.reshape(tiles_x * tiles_y, modes),
        precision=lax.Precision.HIGHEST,
    )
    per_fault = jnp.sum(coef * picked, axis=(1, 2))
    placed = jnp.zeros((faults,), jnp.float32).at[owner].set(per_fault)
    grad = lax.psum_scatter(placed, ("gx", "gy"), scatter_dimension=0, tiled=True)
    return (adj_before, grad)


def solution(mesh):
    in_specs = (
        P(None, "gx", "gy"),
        P("gx", "gy"),
        P(),
        P(),
        P(),
        P(),
        P(),
        P(),
        P(),
        P(),
        P("gx", "gy"),
    )
    out_specs = (P(None, "gx", "gy"), P(("gx", "gy")))
    return jax.shard_map(body, mesh=mesh, in_specs=in_specs, out_specs=out_specs, check_vma=False)
```

profile of v0, /device:TPU:1, one launch (start us, length us, event | category | flops | bytes accessed | tf_op | source)
XLA Modules:
  0.0 300.0 jit_solution(7552683933710687464)
XLA Ops:
  0.6 3.6 %fusion.28 = (f32[1,512,512]{2,1,0:T(8,128)}, f32[1,512,512]{2,1,0:T(8,128)}, f32[1,512,512]{2,1,0:T(8,128)S(1)}) fusion(f32[3,512,512]{2,1,0:T(8,128)} %param.11), kind=kLoop, calls=%fused_computation.53 | loop fusion | bytes 6291456 | tf_op jit(solution)/shard_map/slice | solution.py:50
  4.2 6.0 %all-to-all-start.2 = ((f32[8,64,512]{2,1,0:T(8,128)}), f32[8,64,512]{2,1,0:T(8,128)S(1)}, u32[]{:S(2)}, u32[]{:S(2)}) async-start(f32[8,64,512]{2,1,0:T(8,128)} %bitcast.15), calls=%async_computation.2 | async-start | bytes 2097152 | tf_op jit(solution)/shard_map/all_to_all | solution.py:68
  11.5 8.0 %fusion.27 = (f32[64,128,1]{2,1,0:T(8,128)}, f32[64,128,1]{2,1,0:T(8,128)}) fusion(f32[64,128,128]{2,1,0:T(8,128)} %param.13), kind=kLoop, calls=%fused_computation.52 | loop fusion | bytes 131072 | tf_op jit(solution)/shard_map/slice | solution.py:41
  19.5 2.8 copy.151
  22.3 3.0 copy.150
  25.3 2.8 fusion.29
  30.3 2.2 copy.153
  32.5 8.2 %all-to-all-start = ((f32[512,16,32]{0,2,1:T(8,128)}), f32[512,16,32]{0,2,1:T(8,128)}, u32[]{:S(2)}, u32[]{:S(2)}) async-start(f32[512,16,32]{0,2,1:T(8,128)} %bitcast.1), calls=%async_computation | async-start | bytes 2097152 | tf_op jit(solution)/shard_map/all_to_all | solution.py:60
  42.3 2.3 reshape_squeeze.15
  44.6 5.4 %convolution_bitcast_fusion = f32[64,32,128]{2,0,1:T(8,128)S(1)} fusion(f32[32,128,128]{2,1,0:T(8,128)S(1)} %copy-done.2, f32[64,32,128]{2,1,0:T(8,128)} %reshape_squeeze.15), kind=kOutput, calls=%fused_computation.6 | convolution fusion | flops 402653184 | bytes 4194304 | tf_op jit(solution)/shard_map/cjk,mck->mcj/dot_general | solution.py:20
  55.3 19.3 %reduce = f32[4096,64]{1,0:T(8,128)} reduce(f32[4096,1,64]{2,1,0:T(1,128)S(1)} %bitcast.77, f32[]{:T(128)} %broadcast.28), dimensions={1}, to_apply=%bitcast.61.reduce_sub_computation | reduce | bytes 2097156
  74.7 3.3 %reshape.59 = f32[8,1,32768]{2,1,0:T(1,128)} reshape(f32[4096,64]{1,0:T(8,128)} %reduce) | data formatting | bytes 2097152
  78.0 5.3 %all-to-all-start.3 = ((f32[8,1,32768]{2,1,0:T(1,128)}), f32[8,1,32768]{2,1,0:T(1,128)S(1)}, u32[]{:S(2)}, u32[]{:S(2)}) async-start(f32[8,1,32768]{2,1,0:T(1,128)} %reshape.59), calls=%async_computation.3 | async-start | bytes 2097152 | tf_op jit(solution)/shard_map/all_to_all | solution.py:72
  85.2 8.8 %fusion.16 = f32[64,128,32]{1,2,0:T(8,128)S(1)} fusion(f32[64,128,128]{2,1,0:T(8,128)} %param.13, f32[64,128,32]{1,0,2:T(8,128)S(1)} %reshape_squeeze.13), kind=kOutput, calls=%fused_computation.29 | convolution fusion | flops 402653184 | bytes 6291456 | tf_op jit(solution)/shard_map/cjk,ckm->cjm/dot_general | solution.py:36
  96.3 2.7 copy.141
  99.0 38.4 %reduce.2 = f32[8192,32]{1,0:T(8,128)} reduce(f32[8192,1,32]{2,1,0:T(1,128)} %bitcast.73, f32[]{:T(128)} %broadcast.28), dimensions={1}, to_apply=%bitcast.11.reduce_sub_computation | reduce | bytes 2097156 | tf_op jit(solution)/shard_map/broadcast_in_dim;reshape | solution.py:64
  137.4 4.8 %reshape.61 = f32[16,1,16384]{2,1,0:T(1,128)} reshape(f32[8192,32]{1,0:T(8,128)} %reduce.2) | data formatting | bytes 2097152
  142.2 7.4 %all-to-all-start.1 = ((f32[16,1,16384]{2,1,0:T(1,128)}), f32[16,1,16384]{2,1,0:T(1,128)}, u32[]{:S(2)}, u32[]{:S(2)}) async-start(f32[16,1,16384]{2,1,0:T(1,128)} %reshape.61), calls=%async_computation.1 | async-start | bytes 2097152 | tf_op jit(solution)/shard_map/all_to_all | solution.py:64
  151.1 4.4 %reduce.1 = f32[8,32768]{1,0:T(8,128)S(1)} reduce(f32[8,1,32768]{2,1,0:T(1,128)} %copy-done.7, f32[]{:T(128)} %broadcast.28), dimensions={1}, to_apply=%all_to_all.53.reduce_sub_computation | reduce | bytes 2097156 | tf_op jit(solution)/shard_map/all_to_all | solution.py:72
  155.5 2.6 reshape.60
  159.9 7.3 %all-to-all-done.1 = f32[16,1,16384]{2,1,0:T(1,128)} async-done(((f32[16,1,16384]{2,1,0:T(1,128)}), f32[16,1,16384]{2,1,0:T(1,128)}, u32[]{:S(2)}, u32[]{:S(2)}) %all-to-all-start.1) | async-done | bytes 1048608 | tf_op jit(solution)/shard_map/all_to_all | solution.py:64
  167.2 4.4 %reduce.3 = f32[16,16384]{1,0:T(8,128)S(1)} reduce(f32[16,1,16384]{2,1,0:T(1,128)} %all-to-all-done.1, f32[]{:T(128)} %broadcast.28), dimensions={1}, to_apply=%all_to_all.47.reduce_sub_computation | reduce | bytes 2097156 | tf_op jit(solution)/shard_map/all_to_all | solution.py:64
  171.6 8.6 %reshape.62 = f32[8192,1,32]{2,1,0:T(1,128)} reshape(f32[16,16384]{1,0:T(8,128)S(1)} %reduce.3) | data formatting | bytes 2097152
  180.2 3.0 %copy.142 = f32[16,512,1,32]{1,0,3,2:T(8,128)S(1)} copy(f32[16,512,1,32]{3,1,0,2:T(8,128)} %bitcast.72) | data formatting | bytes 2097152 | tf_op jit(solution)/shard_map/all_to_all | solution.py:64
  187.4 4.9 %collective-permute-start.1 = (f32[512,1]{0,1:T(1,128)S(1)}, f32[512,1]{0,1:T(1,128)S(1)}, u32[]{:S(2)}, u32[]{:S(2)}) collective-permute-start(f32[512,1]{0,1:T(1,128)S(1)} %slice.102), channel_id=1, source_target_pairs={{0,1},{1,2},{2,3},{3,4},{4,5},{5,6},{6,7},{8,9},{9,10},{10,11},{11... | collective-permute-start | bytes 6152 | tf_op jit(solution)/shard_map/ppermute | solution.py:12
  192.9 2.5 copy.148
  205.6 2.5 reshape.41
  208.1 5.1 %fusion.4 = f32[16,4,4]{0,2,1:T(4,128)S(1)} fusion(f32[16,32,4,128]{3,2,1,0:T(4,128)} %reshape.41, f32[4,32,128]{2,1,0:T(8,128)S(1)} %copy-done.9, f32[16,4]{0,1:T(4,128)S(1)} %convert_element_type.5), kind=kOutput, calls=%fused_computation.10 | convolution fusion | flops 12583168 | bytes 1115392 | tf_op jit(solution)/shard_map/ahbw,khw->abk/dot_general | solution.py:90
  213.5 2.3 fusion.3
  215.8 8.2 %scatter_custom_fusion = f32[2048]{0:T(1024)S(1)} fusion(s32[2048]{0:T(1024)} %compare_select_fusion, f32[2048]{0:T(1024)S(1)} %fusion.3, f32[]{:T(128)} %constant.40.clone.1), kind=kCustom, calls=%fused_computation.50 | custom fusion | bytes 8704 | tf_op jit(solution)/shard_map/scatter | solution.py:109
  224.0 67.2 %all-reduce = f32[2048]{0:T(1024)S(1)} all-reduce(f32[2048]{0:T(1024)S(1)} %scatter_custom_fusion), channel_id=2, replica_groups=mesh['gx'=16,'gy'=8] {'gx','gy'}, use_global_device_ids=true, to_apply=%region_2.3.clone | all-reduce | flops 2048 | bytes 16384
  295.9 3.5 %copy.138 = f32[3,512,512]{2,1,0:T(8,128)} copy(f32[3,512,512]{1,2,0:T(8,128)} %pad_maximum_fusion) | data formatting | bytes 6291456
  (80 shorter events, 37.5 us)
Async XLA Ops:
  0.6 94.5 %copy-start = (f32[128,128]{1,0:T(8,128)S(1)}, f32[128,128]{1,0:T(8,128)}, u32[]{:S(2)}) copy-start(f32[128,128]{1,0:T(8,128)} %param.14) | copy-start | bytes 196612
  4.2 28.3 %all-to-all-start.2 = ((f32[8,64,512]{2,1,0:T(8,128)}), f32[8,64,512]{2,1,0:T(8,128)S(1)}, u32[]{:S(2)}, u32[]{:S(2)}) async-start(f32[8,64,512]{2,1,0:T(8,128)} %bitcast.15), calls=%async_computation.2 | async-start | bytes 2097152 | tf_op jit(solution)/shard_map/all_to_all | solution.py:68
  22.3 3.0 %copy-start.2 = (f32[32,128,128]{2,1,0:T(8,128)S(1)}, f32[32,128,128]{2,1,0:T(8,128)}, u32[]{:S(2)}) copy-start(f32[32,128,128]{2,1,0:T(8,128)} %param.15) | copy-start | bytes 6291460
  32.5 45.5 %all-to-all-start = ((f32[512,16,32]{0,2,1:T(8,128)}), f32[512,16,32]{0,2,1:T(8,128)}, u32[]{:S(2)}, u32[]{:S(2)}) async-start(f32[512,16,32]{0,2,1:T(8,128)} %bitcast.1), calls=%async_computation | async-start | bytes 2097152 | tf_op jit(solution)/shard_map/all_to_all | solution.py:60
  50.4 0.8 copy-start.11
  78.0 64.2 %all-to-all-start.3 = ((f32[8,1,32768]{2,1,0:T(1,128)}), f32[8,1,32768]{2,1,0:T(1,128)S(1)}, u32[]{:S(2)}, u32[]{:S(2)}) async-start(f32[8,1,32768]{2,1,0:T(1,128)} %reshape.59), calls=%async_computation.3 | async-start | bytes 2097152 | tf_op jit(solution)/shard_map/all_to_all | solution.py:72
  137.4 12.3 %copy-start.8 = (f32[512,512]{1,0:T(8,128)S(1)}, f32[512,512]{1,0:T(8,128)}, u32[]{:S(2)}) copy-start(f32[512,512]{1,0:T(8,128)} %param.12) | copy-start | bytes 3145732
  142.2 8.8 %copy-start.10 = (s32[2048,8]{0,1:T(8,128)S(1)}, s32[2048,8]{0,1:T(8,128)}, u32[]{:S(2)}) copy-start(s32[2048,8]{0,1:T(8,128)} %param.19) | copy-start | bytes 196612
  142.2 8.8 %copy-start.7 = (f32[8,1,32768]{2,1,0:T(1,128)}, f32[8,1,32768]{2,1,0:T(1,128)S(1)}, u32[]{:S(2)}) copy-start(f32[8,1,32768]{2,1,0:T(1,128)S(1)} %all-to-all-done.3) | copy-start | bytes 3145732
  142.2 25.0 %all-to-all-start.1 = ((f32[16,1,16384]{2,1,0:T(1,128)}), f32[16,1,16384]{2,1,0:T(1,128)}, u32[]{:S(2)}, u32[]{:S(2)}) async-start(f32[16,1,16384]{2,1,0:T(1,128)} %reshape.61), calls=%async_computation.1 | async-start | bytes 2097152 | tf_op jit(solution)/shard_map/all_to_all | solution.py:64
  159.9 23.9 %copy-start.3 = (f32[512,512]{0,1:T(8,128)}, f32[512,512]{0,1:T(8,128)S(1)}, u32[]{:S(2)}) copy-start(f32[512,512]{0,1:T(8,128)S(1)} %copy.132) | copy-start | bytes 3145732
  183.9 2.0 copy-start.5
  183.9 8.4 %copy-start.12 = (s32[2048]{0:T(1024)S(1)}, s32[2048]{0:T(1024)}, u32[]{:S(2)}) copy-start(s32[2048]{0:T(1024)} %param.20) | copy-start | bytes 24580
  183.9 11.5 %copy-start.13 = (s32[16,4]{0,1:T(4,128)S(1)}, s32[16,4]{0,1:T(4,128)}, u32[]{:S(2)}) copy-start(s32[16,4]{0,1:T(4,128)} %param.21) | copy-start | bytes 772
  186.0 9.5 %collective-permute-start = (f32[1,512]{0,1:T(8,128)S(1)}, f32[1,512]{0,1:T(8,128)S(1)}, u32[]{:S(2)}, u32[]{:S(2)}) collective-permute-start(f32[1,512]{0,1:T(8,128)S(1)} %slice.96), channel_id=1, source_target_pairs={{0,8},{8,16},{16,24},{24,32},{32,40},{40,48},{48,56},{56,64},{64,7... | collective-permute-start | bytes 6152 | tf_op jit(solution)/shard_map/ppermute | solution.py:12
  187.4 8.0 %collective-permute-start.1 = (f32[512,1]{0,1:T(1,128)S(1)}, f32[512,1]{0,1:T(1,128)S(1)}, u32[]{:S(2)}, u32[]{:S(2)}) collective-permute-start(f32[512,1]{0,1:T(1,128)S(1)} %slice.102), channel_id=1, source_target_pairs={{0,1},{1,2},{2,3},{3,4},{4,5},{5,6},{6,7},{8,9},{9,10},{10,11},{11... | collective-permute-start | bytes 6152 | tf_op jit(solution)/shard_map/ppermute | solution.py:12
  198.6 9.5 %copy-start.9 = (f32[4,32,128]{2,1,0:T(8,128)S(1)}, f32[4,32,128]{2,1,0:T(8,128)}, u32[]{:S(2)}) copy-start(f32[4,32,128]{2,1,0:T(8,128)} %param.17) | copy-start | bytes 196612
  201.0 90.8 %copy-start.4 = (f32[512,512]{0,1:T(8,128)S(1)}, f32[512,512]{0,1:T(8,128)}, u32[]{:S(2)}) copy-start(f32[512,512]{0,1:T(8,128)} %copy-done.3) | copy-start | bytes 3145732
  201.0 90.8 %copy-start.6 = (f32[512,16,1,32]{0,3,1,2:T(8,128)S(1)}, f32[512,16,1,32]{0,3,1,2:T(8,128)}, u32[]{:S(2)}) copy-start(f32[512,16,1,32]{0,3,1,2:T(8,128)} %copy-done.5) | copy-start | bytes 3145732
  202.4 89.5 %collective-permute-start.2 = (f32[1,512]{0,1:T(8,128)}, f32[1,512]{0,1:T(8,128)S(1)}, u32[]{:S(2)}, u32[]{:S(2)}) collective-permute-start(f32[1,512]{0,1:T(8,128)} %slice.105), channel_id=1, source_target_pairs={{8,0},{16,8},{24,16},{32,24},{40,32},{48,40},{56,48},{64,56},{72,6... | collective-permute-start | bytes 6152 | tf_op jit(solution)/shard_map/ppermute | solution.py:12
  203.7 88.2 %collective-permute-start.3 = (f32[512,1]{0,1:T(1,128)}, f32[512,1]{0,1:T(1,128)S(1)}, u32[]{:S(2)}, u32[]{:S(2)}) collective-permute-start(f32[512,1]{0,1:T(1,128)} %slice.107), channel_id=1, source_target_pairs={{1,0},{2,1},{3,2},{4,3},{5,4},{6,5},{7,6},{9,8},{10,9},{11,10},{12... | collective-permute-start | bytes 6152 | tf_op jit(solution)/shard_map/ppermute | solution.py:12
  294.0 5.5 %copy-start.1 = (f32[128,128]{1,0:T(8,128)S(1)}, f32[128,128]{1,0:T(8,128)}, u32[]{:S(2)}) copy-start(f32[128,128]{1,0:T(8,128)} %param.14) | copy-start | bytes 196612
where the time goes:
time: 305 us; the launch traced here: 300 us
  local copies, waits for them, and re-layouts  87.4 us (29%)
  other arithmetic  78.1 us (26%)
  blocking collectives  67.2 us (22%)
  starting transfers between devices  36.4 us (12%)
  matrix products  22.1 us (7%)
  waiting for transfers between devices  7.3 us (2%)
    unnamed x1, blocking collectives  67.2 us
    unnamed x42, local copies, waits for them, and re-layouts  39.5 us
    another operation x1, other arithmetic, body(): solved[:, None, :]  38.4 us
    unnamed x1, other arithmetic  19.3 us
    ppermute x4, starting transfers between devices, shifted(): return lax.ppermute(block, axis, route)  9.48 us
    dot_general x1, matrix products, solve_first(): jnp.einsum('cjk,ckm->cjm', blocks, split, precision=lax.Precision.HIGHEST)  8.76 us
    all_to_all x1, starting transfers between devices, body(): lax.all_to_all(sectioned_x, 'gx', split_axis=1, concat_axis=0, tiled=True)  8.2 us
    scatter x1, local copies, waits for them, and re-layouts, body(): placed = jnp.zeros((faults,), jnp.float32).at[owner].set(per_fault)  8.19 us
  transfers between devices with their start and end apart: 8, of which 1 were waited for; matrix products, arithmetic and copies ran while one was open for 50% of the time, Pallas kernels for 0%

commit v1 on v0

v1 whole, which is shorter than its diff:
```python
import jax
import jax.numpy as jnp
from jax import lax
from jax.experimental import pallas as pl
from jax.experimental.pallas import tpu as pltpu
from jax.sharding import PartitionSpec as P

courant = 0.5
f32 = jnp.float32
bf16 = jnp.bfloat16
K = 128
EXTRA = 128

NN = (((1,), (0,)), ((), ()))
NT = (((1,), (1,)), ((), ()))
TN = (((0,), (0,)), ((), ()))


def halves(x):
    high = x.astype(bf16)
    return high, (x - high.astype(f32)).astype(bf16)


def mm(a, b, dims):
    return lax.dot_general(a, b, dims, preferred_element_type=f32)


def mm3(a, b, dims):
    ah, al = a
    bh, bl = b
    return mm(ah, bh, dims) + (mm(ah, bl, dims) + mm(al, bh, dims))


def exact(a, b, dims):
    return lax.dot_general(a, b, dims, precision=lax.Precision.HIGHEST, preferred_element_type=f32)


def iota(shape, dim):
    return lax.broadcasted_iota(jnp.int32, shape, dim)


def any_spec():
    return pl.BlockSpec(memory_space=pl.ANY)


def vmem_spec():
    return pl.BlockSpec(memory_space=pltpu.VMEM)


def cost(flops, nbytes):
    return pl.CostEstimate(flops=flops, bytes_accessed=nbytes, transcendentals=0)


def ends_kernel(
    adj, depth, block_x, block_y, px, py, vx, vy, wx0, wx1, wy0, wy1, drow, dcol, sems
):
    u = lax.axis_index("gx")
    v = lax.axis_index("gy")
    rows, cols = vx.shape
    nbx = wx0.shape[0]
    nby = wy0.shape[0]
    small = [
        pltpu.make_async_copy(block_x.at[pl.ds(u * nbx, nbx), pl.ds(0, 8), :], wx0, sems.at[0]),
        pltpu.make_async_copy(block_x.at[pl.ds(u * nbx, nbx), pl.ds(K - 8, 8), :], wx1, sems.at[1]),
        pltpu.make_async_copy(block_y.at[pl.ds(v * nby, nby), pl.ds(0, 8), :], wy0, sems.at[2]),
        pltpu.make_async_copy(block_y.at[pl.ds(v * nby, nby), pl.ds(K - 8, 8), :], wy1, sems.at[3]),
        pltpu.make_async_copy(depth.at[pl.ds(rows - 8, 8), :], drow, sems.at[4]),
        pltpu.make_async_copy(depth.at[:, pl.ds(cols - K, K)], dcol, sems.at[5]),
    ]
    for copy in small:
        copy.start()
    big = []
    for c in range(nbx):
        here = pl.ds(c * K, K)
        big.append(pltpu.make_async_copy(adj.at[2, here, :], vy.at[here, :], sems.at[6 + c]))
    for c in range(nbx):
        here = pl.ds(c * K, K)
        big.append(pltpu.make_async_copy(adj.at[1, here, :], vx.at[here, :], sems.at[6 + nbx + c]))
    for copy in big:
        copy.start()
    for copy in small:
        copy.wait()
    ends_y = [halves(jnp.concatenate([wy0[c, 0:1, :], wy1[c, 7:8, :]], axis=0)) for c in range(nby)]
    ends_x = [halves(jnp.concatenate([wx0[c, 0:1, :], wx1[c, 7:8, :]], axis=0)) for c in range(nbx)]
    for part in range(cols // K):
        px[0, part : part + 1, cols:] = drow[7:8, part * K : (part + 1) * K]
    px[0, cols // K :, cols:] = jnp.zeros((8 - cols // K, EXTRA), f32)
    last = (iota((8, K), 1) == K - 1).astype(f32)
    side = exact(last, dcol[...], NT)
    for part in range(rows // K):
        py[part : part + 1, rows:] = side[0:1, part * K : (part + 1) * K]
    py[rows // K :, rows:] = jnp.zeros((8 - rows // K, EXTRA), f32)
    for r in range(nbx):
        big[r].wait()
        for c in range(nby):
            part = halves(vy[r * K : (r + 1) * K, c * K : (c + 1) * K])
            py[2 * c : 2 * c + 2, r * K : (r + 1) * K] = mm3(ends_y[c], part, NT)
    for c in range(nbx):
        big[nbx + c].wait()
        part = halves(vx[c * K : (c + 1) * K, :])
        px[0, 2 * c : 2 * c + 2, :cols] = mm3(ends_x[c], part, NN)
    for d in range(1, px.shape[0]):
        px[d] = px[0]


def ends(adj, depth, block_x, block_y, size_x, size_y):
    rows, cols = depth.shape
    nbx = block_x.shape[0] // size_x
    nby = block_y.shape[0] // size_y
    return pl.pallas_call(
        ends_kernel,
        out_shape=(
            jax.ShapeDtypeStruct((size_x, 2 * nbx, cols + EXTRA), f32),
            jax.ShapeDtypeStruct((2 * nby, rows + EXTRA), f32),
        ),
        in_specs=[any_spec()] * 4,
        out_specs=(vmem_spec(), vmem_spec()),
        scratch_shapes=[
            pltpu.VMEM((rows, cols), f32),
            pltpu.VMEM((rows, cols), f32),
            pltpu.VMEM((nbx, 8, K), f32),
            pltpu.VMEM((nbx, 8, K), f32),
            pltpu.VMEM((nby, 8, K), f32),
            pltpu.VMEM((nby, 8, K), f32),
            pltpu.VMEM((8, cols), f32),
            pltpu.VMEM((rows, K), f32),
            pltpu.SemaphoreType.DMA((6 + 2 * nbx,)),
        ],
        compiler_params=pltpu.CompilerParams(vmem_limit_bytes=16 << 20),
        cost_estimate=cost(2 * rows * cols * 32, 3 << 20),
        name="ends",
    )(adj, depth, block_x, block_y)


def local_kernel(
    adj, block_x, block_y, reduced_x, reduced_y,
    yx, yy, gxh, gxl, gyh, gyl, gside, vx, vy, wx, wy, wpx, wpy, sems,
):
    u = lax.axis_index("gx")
    v = lax.axis_index("gy")
    rows, cols = vx.shape
    nbx = wx.shape[0]
    nby = wy.shape[0]
    before_x = jnp.maximum(u * nbx - 1, 0)
    before_y = jnp.maximum(v * nby - 1, 0)
    copies = [
        pltpu.make_async_copy(block_x.at[pl.ds(u * nbx, nbx)], wx, sems.at[0]),
        pltpu.make_async_copy(block_y.at[pl.ds(v * nby, nby)], wy, sems.at[1]),
        pltpu.make_async_copy(block_x.at[before_x, pl.ds(K - 8, 8), :], wpx, sems.at[2]),
        pltpu.make_async_copy(block_y.at[before_y, pl.ds(K - 8, 8), :], wpy, sems.at[3]),
        pltpu.make_async_copy(adj.at[1], vx, sems.at[4]),
        pltpu.make_async_copy(adj.at[2], vy, sems.at[5]),
    ]
    for copy in copies:
        copy.start()
    for copy in copies[:4]:
        copy.wait()
    own_x = reduced_x[pl.ds(pl.multiple_of(u * 8, 8), 8), :]
    own_y = reduced_y[pl.ds(pl.multiple_of(v * 8, 8), 8), :]
    prev_x = reduced_x[pl.ds(pl.multiple_of(jnp.maximum(u - 1, 0) * 8, 8), 8), :]
    prev_y = reduced_y[pl.ds(pl.multiple_of(jnp.maximum(v - 1, 0) * 8, 8), 8), :]
    for c in range(nbx):
        w = wx[c]
        g = w[:, 0:1] * own_x[2 * c : 2 * c + 1, :] + w[:, K - 1 : K] * own_x[2 * c + 1 : 2 * c + 2, :]
        high, low = halves(g)
        gxh[c * K : (c + 1) * K, :] = high
        gxl[c * K : (c + 1) * K, :] = low
    row = iota((8, K), 0)
    lane = iota((8, K), 1)
    for c in range(nby):
        pick = (((row == 2 * c) & (lane == 0)) | ((row == 2 * c + 1) & (lane == K - 1))).astype(f32)
        across = exact(pick, wy[c], NT)
        high, low = halves(exact(own_y, across, TN))
        gyh[:, c * K : (c + 1) * K] = high
        gyl[:, c * K : (c + 1) * K] = low

    def side(w, prev, index):
        width = prev.shape[1]
        g = w[7:8, 0:1] * prev[6:7, :] + w[7:8, K - 1 : K] * prev[7:8, :]
        g = g + (iota((1, width), 1) == index * 8 - 1).astype(f32)
        return jnp.where(index > 0, g, 0.0)

    gside[...] = jnp.zeros(gside.shape, f32)
    gside[0:1, :] = side(wpx[...], prev_x, u)
    gside[1:2, : reduced_y.shape[1]] = side(wpy[...], prev_y, v)
    copies[4].wait()
    for c in range(nbx):
        yx[c * K : (c + 1) * K, :] = mm3(halves(wx[c]), halves(vx[c * K : (c + 1) * K, :]), NN)
    copies[5].wait()
    for c in range(nby):
        yy[:, c * K : (c + 1) * K] = mm3(halves(vy[:, c * K : (c + 1) * K]), halves(wy[c]), NT)


def local(adj, block_x, block_y, reduced_x, reduced_y, size_x, size_y):
    _, rows, cols = adj.shape
    nbx = block_x.shape[0] // size_x
    nby = block_y.shape[0] // size_y
    field = jax.ShapeDtypeStruct((rows, cols), f32)
    return pl.pallas_call(
        local_kernel,
        out_shape=(
            field,
            field,
            jax.ShapeDtypeStruct((rows, reduced_x.shape[0]), bf16),
            jax.ShapeDtypeStruct((rows, reduced_x.shape[0]), bf16),
            jax.ShapeDtypeStruct((reduced_y.shape[0], cols), bf16),
            jax.ShapeDtypeStruct((reduced_y.shape[0], cols), bf16),
            jax.ShapeDtypeStruct((8, reduced_x.shape[0]), f32),
        ),
        in_specs=[any_spec()] * 3 + [vmem_spec()] * 2,
        out_specs=(vmem_spec(),) * 7,
        scratch_shapes=[
            pltpu.VMEM((rows, cols), f32),
            pltpu.VMEM((rows, cols), f32),
            pltpu.VMEM((nbx, K, K), f32),
            pltpu.VMEM((nby, K, K), f32),
            pltpu.VMEM((8, K), f32),
            pltpu.VMEM((8, K), f32),
            pltpu.SemaphoreType.DMA((6,)),
        ],
        compiler_params=pltpu.CompilerParams(vmem_limit_bytes=24 << 20),
        cost_estimate=cost(12 * rows * cols * K, 5 << 20),
        name="local",
    )(adj, block_x, block_y, reduced_x, reduced_y)


def faults_kernel(wet, coef, footprint, owner, weights, high_of, low_of, dist, coef8):
    u = lax.axis_index("gx")
    v = lax.axis_index("gy")
    tiles_x, tiles_y = wet.shape
    total_cols = tiles_y * lax.axis_size("gy")
    shift = total_cols.bit_length() - 1
    count = footprint.shape[1]
    places = footprint.shape[0]
    sub = iota((8, count), 0)
    for f in range(places):
        tile = footprint[f : f + 1, :]
        row = lax.shift_right_logical(tile, shift) - u * tiles_x
        col = (tile & (total_cols - 1)) - v * tiles_y
        inside = (row >= 0) & (row < tiles_x) & (col >= 0) & (col < tiles_y)
        flat = jnp.where(inside, col * tiles_x + row, -1000)
        dist[f] = flat - lax.shift_right_logical(sub, 2)
        four = coef[4 * f : 4 * f + 4, :]
        coef8[f] = jnp.concatenate([four, four], axis=0)

    def group(g, carry):
        acc = jnp.zeros((8, count), f32)
        for f in range(places):
            acc = acc + jnp.where(dist[f] == 2 * g, coef8[f], 0.0)
        col = (2 * g) // tiles_x
        row = 2 * g - col * tiles_x
        keep = jnp.where(sub < 4, wet[row, col].astype(f32), wet[row + 1, col].astype(f32))
        weights[pl.ds(pl.multiple_of(g * 8, 8), 8), :] = acc * keep
        return carry

    lax.fori_loop(0, tiles_x * tiles_y // 2, group, 0)
    own = owner[...]
    slots = low_of.shape[0]
    bits = slots.bit_length() - 1
    high_of[...] = (iota(high_of.shape, 0) == lax.shift_right_logical(own, bits)).astype(f32).astype(bf16)
    low_of[...] = (iota(low_of.shape, 0) == (own & (slots - 1))).astype(f32)


def faults(wet, coef, footprint, owner, devices):
    tiles_x, tiles_y = wet.shape
    subf, places, modes = coef.shape
    slots = subf // devices
    return pl.pallas_call(
        faults_kernel,
        out_shape=(
            jax.ShapeDtypeStruct((tiles_x * tiles_y * modes, subf), f32),
            jax.ShapeDtypeStruct((devices, subf), bf16),
            jax.ShapeDtypeStruct((slots, subf), f32),
        ),
        in_specs=[pl.BlockSpec(memory_space=pltpu.SMEM)] + [vmem_spec()] * 3,
        out_specs=(vmem_spec(),) * 3,
        scratch_shapes=[
            pltpu.VMEM((places, 8, subf), jnp.int32),
            pltpu.VMEM((places, 8, subf), f32),
        ],
        compiler_params=pltpu.CompilerParams(vmem_limit_bytes=16 << 20),
        cost_estimate=cost(40 << 20, 3 << 20),
        name="faults",
    )(
        wet,
        coef.reshape(subf, places * modes).T,
        footprint.T,
        owner.reshape(1, subf),
    )


def elev_kernel(
    tx, ta, tb, yx, yy, gxh, gxl, gyh, gyl, gside, adj, depth, basis, weights, high_of, low_of,
    elev, fx, fy, erow, ecol, parts, dep, a0, tyn, mom, sems,
):
    u = lax.axis_index("gx")
    v = lax.axis_index("gy")
    rows, cols = dep.shape
    steps = rows // K
    copies = []
    for r in range(steps):
        here = pl.ds(r * K, K)
        copies.append(
            (
                pltpu.make_async_copy(depth.at[here, :], dep.at[here, :], sems.at[2 * r]),
                pltpu.make_async_copy(adj.at[0, here, :], a0.at[here, :], sems.at[2 * r + 1]),
            )
        )
    for pair in copies:
        for copy in pair:
            copy.start()
    nx = tx.shape[0]
    half = ta.shape[0]
    tx_all = jnp.concatenate([tx[d][:, :cols] for d in range(nx)], axis=0)
    for j in range(2 * half):
        k = j ^ v
        first = ta[k & (half - 1)]
        second = tb[k & (half - 1)]
        tyn[j * 8 : (j + 1) * 8, :] = jnp.where(k < half, first, second)
    ty_all = tyn[:, :rows]
    txs = halves(tx_all)
    tys = halves(ty_all)
    up = jnp.maximum(u - 1, 0)
    left = jnp.maximum(v - 1, 0)
    gs = gside[...]
    edge_x = exact(gs, tx_all, NN)[0:1, :]
    edge_y = exact(gs[:, : ty_all.shape[0]], ty_all, NN)[1:2, :]
    drow = tx[up][:, cols:]
    drow = jnp.concatenate([drow[p : p + 1, :] for p in range(cols // K)], axis=1)
    dcol = tyn[pl.ds(pl.multiple_of(left * 8, 8), 8), rows:]
    dcol = jnp.concatenate([dcol[p : p + 1, :] for p in range(rows // K)], axis=1)
    carry = edge_x * drow
    side = jnp.broadcast_to(edge_y * dcol, (8, rows))
    row = iota((K, cols), 0)
    lane = iota((K, cols), 1)
    first_lane = (iota((8, K), 1) == 0) & (iota((8, K), 0) == 0)
    first_lane = first_lane.astype(f32)
    modes, tile_h, tile_w = basis.shape
    per = K // tile_h
    wide = [jnp.concatenate([basis[b]] * (cols // tile_w), axis=1) for b in range(modes)]
    for r in range(steps):
        here = slice(r * K, (r + 1) * K)
        for copy in copies[r]:
            copy.wait()
        d = dep[here, :]
        flux_x = yx[here, :] + mm3((gxh[here, :], gxl[here, :]), txs, NN)
        part = (tys[0][:, here], tys[1][:, here])
        flux_y = yy[here, :] + mm3(part, (gyh[...], gyl[...]), TN)
        fx[here, :] = flux_x
        fy[here, :] = flux_y
        weighted_x = d * flux_x
        weighted_y = d * flux_y
        before_x = jnp.where(row == 0, carry, pltpu.roll(weighted_x, 1, 0))
        carry = weighted_x[K - 1 : K, :]
        edge = exact(side[:, here], first_lane, TN)
        edge = jnp.concatenate([edge, jnp.zeros((K, cols - K), f32)], axis=1)
        before_y = jnp.where(lane == 0, edge, pltpu.roll(weighted_y, 1, 1))
        e = a0[here, :] + courant * ((weighted_x - before_x) + (weighted_y - before_y))
        elev[here, :] = e
        if r == 0:
            erow[...] = e[0:1, :]
        ecol[:, here] = exact(first_lane, e[:, :K], NT)[0:1, :]
        for a in range(per):
            tile = e[a * tile_h : (a + 1) * tile_h, :]
            for b in range(modes):
                at = (r * per + a) * modes + b
                mom[at : at + 1, :] = jnp.sum(tile * wide[b], axis=0, keepdims=True)
    total = None
    group = mom.shape[0]
    for w in range(cols // tile_w):
        m = jnp.sum(mom[:, w * tile_w : (w + 1) * tile_w], axis=1, keepdims=True)
        term = jnp.sum(weights[w * group : (w + 1) * group, :] * m, axis=0, keepdims=True)
        total = term if total is None else total + term
    high, low = halves(low_of[...] * total)
    sums = mm(high_of[...], high, NT) + mm(high_of[...], low, NT)
    parts[...] = jnp.zeros(parts.shape, f32)
    parts[:, : sums.shape[1]] = sums


def elevation(tx, ta, tb, solved, adj, depth, basis, weights, high_of, low_of):
    rows, cols = depth.shape
    field = jax.ShapeDtypeStruct((rows, cols), f32)
    modes, tile_h, tile_w = basis.shape
    return pl.pallas_call(
        elev_kernel,
        out_shape=(
            field,
            field,
            field,
            jax.ShapeDtypeStruct((1, cols), f32),
            jax.ShapeDtypeStruct((1, rows), f32),
            jax.ShapeDtypeStruct((high_of.shape[0], K), f32),
        ),
        in_specs=[vmem_spec()] * 10 + [any_spec()] * 2 + [vmem_spec()] * 4,
        out_specs=(vmem_spec(),) * 6,
        scratch_shapes=[
            pltpu.VMEM((rows, cols), f32),
            pltpu.VMEM((rows, cols), f32),
            pltpu.VMEM((2 * ta.shape[0] * 8, rows + EXTRA), f32),
            pltpu.VMEM((rows // tile_h * modes, cols), f32),
            pltpu.SemaphoreType.DMA((2 * (rows // K),)),
        ],
        compiler_params=pltpu.CompilerParams(vmem_limit_bytes=32 << 20),
        cost_estimate=cost(12 * rows * cols * K, 10 << 20),
        name="elevation",
    )(tx, ta, tb, *solved, adj, depth, basis, weights, high_of, low_of)


def fluxes_kernel(elev, fx, fy, hrow, hcol, out, e, x, y, sems):
    rows, cols = e.shape
    steps = rows // K
    reads = []
    for r in range(steps):
        here = pl.ds(r * K, K)
        reads.append(
            (
                pltpu.make_async_copy(elev.at[here, :], e.at[here, :], sems.at[r, 0]),
                pltpu.make_async_copy(fx.at[here, :], x.at[here, :], sems.at[r, 1]),
                pltpu.make_async_copy(fy.at[here, :], y.at[here, :], sems.at[r, 2]),
            )
        )
    for group in reads:
        for copy in group:
            copy.start()
    last_lane = ((iota((8, K), 1) == K - 1) & (iota((8, K), 0) == 0)).astype(f32)
    side = jnp.broadcast_to(hcol[...], (8, rows))
    row = iota((K, cols), 0)
    lane = iota((K, cols), 1)
    writes = []
    for copy in reads[0]:
        copy.wait()
    for r in range(steps):
        here = slice(r * K, (r + 1) * K)
        if r + 1 < steps:
            for copy in reads[r + 1]:
                copy.wait()
            after = e[(r + 1) * K : (r + 1) * K + 1, :]
        else:
            after = hrow[...]
        now = e[here, :]
        edge = exact(side[:, here], last_lane, TN)
        edge = jnp.concatenate([jnp.zeros((K, cols - K), f32), edge], axis=1)
        below = jnp.where(row == K - 1, after, pltpu.roll(now, K - 1, 0))
        right = jnp.where(lane == cols - 1, edge, pltpu.roll(now, cols - 1, 1))
        x[here, :] = x[here, :] + courant * (below - now)
        y[here, :] = y[here, :] + courant * (right - now)
        where = pl.ds(r * K, K)
        group = (
            pltpu.make_async_copy(e.at[where, :], out.at[0, where, :], sems.at[r, 3]),
            pltpu.make_async_copy(x.at[where, :], out.at[1, where, :], sems.at[r, 4]),
            pltpu.make_async_copy(y.at[where, :], out.at[2, where, :], sems.at[r, 5]),
        )
        for copy in group:
            copy.start()
        writes.append(group)
    for group in writes:
        for copy in group:
            copy.wait()


def fluxes(elev, fx, fy, hrow, hcol):
    rows, cols = elev.shape
    return pl.pallas_call(
        fluxes_kernel,
        out_shape=jax.ShapeDtypeStruct((3, rows, cols), f32),
        in_specs=[any_spec()] * 3 + [vmem_spec()] * 2,
        out_specs=any_spec(),
        scratch_shapes=[
            pltpu.VMEM((rows, cols), f32),
            pltpu.VMEM((rows, cols), f32),
            pltpu.VMEM((rows, cols), f32),
            pltpu.SemaphoreType.DMA((rows // K, 6)),
        ],
        compiler_params=pltpu.CompilerParams(vmem_limit_bytes=16 << 20),
        cost_estimate=cost(10 * rows * cols, 6 << 20),
        name="fluxes",
    )(elev, fx, fy, hrow, hcol)


def partner(axis, bit):
    return [(i, i ^ bit) for i in range(lax.axis_size(axis))]


def previous(axis):
    return [(i, i - 1) for i in range(1, lax.axis_size(axis))]


def body(
    adj_fields, depth, block_x, reduced_x, block_y, reduced_y, basis, coef, footprint, owner, wet
):
    size_x = lax.axis_size("gx")
    size_y = lax.axis_size("gy")
    px, py = ends(adj_fields, depth, block_x, block_y, size_x, size_y)
    tx = lax.all_to_all(px, "gx", split_axis=0, concat_axis=0, tiled=True)
    ty = py[None]
    bit = 1
    while 2 * bit < size_y:
        ty = jnp.concatenate([ty, lax.ppermute(ty, "gy", partner("gy", bit))], axis=0)
        bit *= 2
    ty_far = lax.ppermute(ty, "gy", partner("gy", bit))
    solved = local(adj_fields, block_x, block_y, reduced_x, reduced_y, size_x, size_y)
    chosen = faults(wet, coef, footprint, owner, size_x * size_y)
    elev, fx, fy, erow, ecol, parts = elevation(
        tx, ty, ty_far, solved, adj_fields, depth, basis, *chosen
    )
    devices, width = parts.shape
    sums = lax.all_to_all(
        parts.reshape(devices, 1, width), ("gx", "gy"), split_axis=0, concat_axis=0, tiled=True
    )
    hrow = lax.ppermute(erow, "gx", previous("gx"))
    hcol = lax.ppermute(ecol, "gy", previous("gy"))
    adj_before = fluxes(elev, fx, fy, hrow, hcol)
    slots = owner.shape[0] // devices
    grad = jnp.sum(sums[:, 0, :slots], axis=0)
    return adj_before, grad


def solution(mesh):
    in_specs = (
        P(None, "gx", "gy"),
        P("gx", "gy"),
        P(),
        P(),
        P(),
        P(),
        P(),
        P(),
        P(),
        P(),
        P("gx", "gy"),
    )
    out_specs = (P(None, "gx", "gy"), P(("gx", "gy")))
    return jax.shard_map(body, mesh=mesh, in_specs=in_specs, out_specs=out_specs, check_vma=False)
```

time: 305 us -> 99.8 us (0.33)
  the two profiles are of different devices: /device:TPU:1 before, /device:TPU:33 now
where the time goes in v1:
time: 99.8 us; the launch traced here: 98.4 us
  local copies, waits for them, and re-layouts  47.8 us (48%)
  starting transfers between devices  28.1 us (28%)
  Pallas kernels  16.2 us (16%)
  waiting for transfers between devices  4.11 us (4%)
  other arithmetic  1.42 us (1%)
    unnamed x95, local copies, waits for them, and re-layouts  46 us
    all_to_all x1, starting transfers between devices, body(): lax.all_to_all(parts.reshape(devices, 1, width), ('gx', 'gy'), split_axis...  9.05 us
    all_to_all x1, starting transfers between devices, body(): tx = lax.all_to_all(px, 'gx', split_axis=0, concat_axis=0, tiled=True)  7.34 us
    pallas_call x1, Pallas kernels, elevation(): pl.pallas_call(elev_kernel, out_shape=(field, field, field, jax.ShapeDtyp...  5.54 us
    ppermute x1, starting transfers between devices, body(): hrow = lax.ppermute(erow, 'gx', previous('gx'))  4.18 us
    pallas_call x1, Pallas kernels, local(): pl.pallas_call(local_kernel, out_shape=(field, field, jax.ShapeDtypeStruc...  2.92 us
    ppermute x1, starting transfers between devices, body(): ty_far = lax.ppermute(ty, 'gy', partner('gy', bit))  2.91 us
    pallas_call x1, Pallas kernels, faults(): pl.pallas_call(faults_kernel, out_shape=(jax.ShapeDtypeStruct((tiles_x *...  2.74 us
  transfers between devices with their start and end apart: 7, of which 2 were waited for; matrix products, arithmetic and copies ran while one was open for 4% of the time, Pallas kernels for 8%

profile of v1, /device:TPU:33, one launch (start us, length us, event | category | flops | bytes accessed | tf_op | source)
XLA Modules:
  0.0 98.4 jit_solution(2784893805332465401)
XLA Ops:
  0.6 1.9 %copy-done = f32[3,512,512]{2,1,0:T(8,128)S(1)} copy-done((f32[3,512,512]{2,1,0:T(8,128)S(1)}, f32[3,512,512]{2,1,0:T(8,128)}, u32[]{:S(2)}) %copy-start) | copy-done | bytes 3145752
  2.5 2.2 %copy-done.2 = f32[64,128,128]{2,1,0:T(8,128)S(1)} copy-done((f32[64,128,128]{2,1,0:T(8,128)S(1)}, f32[64,128,128]{2,1,0:T(8,128)}, u32[]{:S(2)}) %copy-start.2) | copy-done | bytes 4194328
  4.7 1.6 %copy-done.4 = f32[32,128,128]{2,1,0:T(8,128)S(1)} copy-done((f32[32,128,128]{2,1,0:T(8,128)S(1)}, f32[32,128,128]{2,1,0:T(8,128)}, u32[]{:S(2)}) %copy-start.4) | copy-done | bytes 2097176
  6.3 1.2 %copy-done.6 = f32[512,512]{1,0:T(8,128)S(1)} copy-done((f32[512,512]{1,0:T(8,128)S(1)}, f32[512,512]{1,0:T(8,128)}, u32[]{:S(2)}) %copy-start.6) | copy-done | bytes 1048600
  7.5 2.7 %ends.1 = (f32[16,8,640]{2,1,0:T(8,128)S(1)}, f32[8,640]{1,0:T(8,128)S(1)}) custom-call(f32[3,512,512]{2,1,0:T(8,128)S(1)} %copy-done, f32[512,512]{1,0:T(8,128)S(1)} %copy-done.6, f32[64,128,128]{2,1,0:T(8,128)S(1)} %copy-done.2, f32[32,128,128]{2,1,0:T(8,128)S(1)} %copy-done.4), custom_call_target="tpu_custom_call" | custom-call | flops 16777216 | bytes 3145728 | tf_op jit(solution)/shard_map/ends/pallas_call | solution.py:110
  11.6 7.3 %all-to-all-start = ((f32[16,8,640]{2,1,0:T(8,128)}), f32[16,8,640]{2,1,0:T(8,128)S(1)}, u32[]{:S(2)}, u32[]{:S(2)}) async-start(f32[16,8,640]{2,1,0:T(8,128)} %copy-done.23), calls=%async_computation | async-start | bytes 655360 | tf_op jit(solution)/shard_map/all_to_all | solution.py:494
  19.0 1.4 %collective-permute-start.1 = (f32[2,8,640]{2,1,0:T(8,128)S(1)}, f32[2,8,640]{2,1,0:T(8,128)S(1)}, u32[]{:S(2)}, u32[]{:S(2)}) collective-permute-start(f32[2,8,640]{2,1,0:T(8,128)S(1)} %pad_maximum_fusion.1), channel_id=1, source_target_pairs={{0,2},{1,3},{2,0},{3,1},{4,6},{5,7},{6,4},{7,5},{8,10},{9,11},{10,... | collective-permute-start | bytes 122888 | tf_op jit(solution)/shard_map/ppermute | solution.py:498
  20.3 1.6 %collective-permute-done.1 = f32[2,8,640]{2,1,0:T(8,128)S(1)} collective-permute-done((f32[2,8,640]{2,1,0:T(8,128)S(1)}, f32[2,8,640]{2,1,0:T(8,128)S(1)}, u32[]{:S(2)}, u32[]{:S(2)}) %collective-permute-start.1) | collective-permute-done | bytes 40992 | tf_op jit(solution)/shard_map/ppermute | solution.py:498
  22.6 2.9 %collective-permute-start.2 = (f32[4,8,640]{2,1,0:T(8,128)S(1)}, f32[4,8,640]{2,1,0:T(8,128)}, u32[]{:S(2)}, u32[]{:S(2)}) collective-permute-start(f32[4,8,640]{2,1,0:T(8,128)S(1)} %pad_maximum_fusion.ta), channel_id=1, source_target_pairs={{0,4},{1,5},{2,6},{3,7},{4,0},{5,1},{6,2},{7,3},{8,12},{9,13},{10,... | collective-permute-start | bytes 245768 | tf_op jit(solution)/shard_map/ppermute | solution.py:500
  25.6 1.4 %copy.14.wet = s32[16,4]{1,0:T(8,128)} copy(s32[16,4]{0,1:T(4,128)} %param.21) | data formatting | bytes 512 | tf_op args[10]
  26.9 1.7 %reshape.13 = f32[2048,32]{0,1:T(8,128)} reshape(f32[2048,8,4]{0,2,1:T(4,128)} %param.18) | data formatting | bytes 524288 | tf_op jit(solution)/shard_map/reshape | solution.py:286
  31.8 2.7 %faults.1 = (f32[256,2048]{1,0:T(8,128)S(1)}, bf16[128,2048]{1,0:T(8,128)(2,1)S(1)}, f32[16,2048]{1,0:T(8,128)S(1)}) custom-call(s32[16,4]{1,0:T(8,128)S(1)} %copy-done.40, f32[32,2048]{1,0:T(8,128)S(1)} %bitcast.9, s32[8,2048]{1,0:T(8,128)S(1)} %bitcast.14, s32[1,2048]{1,0:T(1,128)S(1)} %bitcast.15), custom_call_target="tpu_custom_call" | custom-call | flops 41943040 | bytes 3145728 | tf_op jit(solution)/shard_map/faults/pallas_call | solution.py:268
  34.6 1.3 %copy-done.8 = f32[256,2048]{1,0:T(8,128)} copy-done((f32[256,2048]{1,0:T(8,128)}, f32[256,2048]{1,0:T(8,128)S(1)}, u32[]{:S(2)}) %copy-start.8) | copy-done | bytes 2097176
  37.4 2.2 %copy-done.3 = f32[64,128,128]{2,1,0:T(8,128)S(1)} copy-done((f32[64,128,128]{2,1,0:T(8,128)S(1)}, f32[64,128,128]{2,1,0:T(8,128)}, u32[]{:S(2)}) %copy-start.3) | copy-done | bytes 4194328
  39.5 1.6 %copy-done.5 = f32[32,128,128]{2,1,0:T(8,128)S(1)} copy-done((f32[32,128,128]{2,1,0:T(8,128)S(1)}, f32[32,128,128]{2,1,0:T(8,128)}, u32[]{:S(2)}) %copy-start.5) | copy-done | bytes 2097176
  42.7 2.9 %local.1 = (f32[512,512]{1,0:T(8,128)S(1)}, f32[512,512]{1,0:T(8,128)S(1)}, bf16[512,128]{1,0:T(8,128)(2,1)S(1)}, bf16[512,128]{1,0:T(8,128)(2,1)S(1)}, bf16[64,...) custom-call(f32[3,512,512]{2,1,0:T(8,128)S(1)} %copy-done.1, ...), custom_call_target="tpu_custom_call" | custom-call | flops 402653184 | bytes 5242880 | tf_op jit(solution)/shard_map/local/pallas_call | solution.py:199
  45.7 1.0 %copy-done.10 = f32[512,512]{1,0:T(8,128)} copy-done((f32[512,512]{1,0:T(8,128)}, f32[512,512]{1,0:T(8,128)S(1)}, u32[]{:S(2)}) %copy-start.10) | copy-done | bytes 1048600
  50.8 1.2 %copy-done.7 = f32[512,512]{1,0:T(8,128)S(1)} copy-done((f32[512,512]{1,0:T(8,128)S(1)}, f32[512,512]{1,0:T(8,128)}, u32[]{:S(2)}) %copy-start.7) | copy-done | bytes 1048600
  52.0 1.6 %copy-done.9 = f32[256,2048]{1,0:T(8,128)S(1)} copy-done((f32[256,2048]{1,0:T(8,128)S(1)}, f32[256,2048]{1,0:T(8,128)}, u32[]{:S(2)}) %copy-start.9) | copy-done | bytes 2097176
  53.6 1.2 %copy-done.11 = f32[512,512]{1,0:T(8,128)S(1)} copy-done((f32[512,512]{1,0:T(8,128)S(1)}, f32[512,512]{1,0:T(8,128)}, u32[]{:S(2)}) %copy-start.11) | copy-done | bytes 1048600
  54.8 1.2 %copy-done.13 = f32[512,512]{1,0:T(8,128)S(1)} copy-done((f32[512,512]{1,0:T(8,128)S(1)}, f32[512,512]{1,0:T(8,128)}, u32[]{:S(2)}) %copy-start.13) | copy-done | bytes 1048600
  56.1 1.0 %copy-done.22 = bf16[128,2048]{1,0:T(8,128)(2,1)S(1)} copy-done((bf16[128,2048]{1,0:T(8,128)(2,1)S(1)}, bf16[128,2048]{1,0:T(8,128)(2,1)}, u32[]{:S(2)}) %copy-start.22) | copy-done | bytes 524312
  63.0 5.5 %elevation.1 = (f32[512,512]{1,0:T(8,128)S(1)}, f32[512,512]{1,0:T(8,128)S(1)}, f32[512,512]{1,0:T(8,128)S(1)}, f32[1,512]{1,0:T(1,128)S(1)}, f32[1,512]{1,0:T(1,128)S(1)}, /*index=5*/f32[128,128]{1,0:T(8,128)S(1)}) custom-call(f32[16,8,640]{2,1,0:T(8,128)S(1)} %all-to-all-done.tx, f32[4,8,640]{2,1,0:T(8,128)S(1)} %pad_maximum_fusion.ta, ...), custom_call_target="tpu_custom_call" | custom-call | flops 402653184 | bytes 10485760 | tf_op jit(solution)/shard_map/elevation/pallas_call | solution.py:384
  69.5 1.0 %copy-done.17 = f32[512,512]{1,0:T(8,128)} copy-done((f32[512,512]{1,0:T(8,128)}, f32[512,512]{1,0:T(8,128)S(1)}, u32[]{:S(2)}) %copy-start.17) | copy-done | bytes 1048600
  73.3 9.0 %all-to-all-start.1 = ((f32[128,1,128]{2,1,0:T(1,128)}), f32[128,1,128]{2,1,0:T(1,128)S(1)}, u32[]{:S(2)}, u32[]{:S(2)}) async-start(f32[128,1,128]{2,1,0:T(1,128)} %bitcast.13), calls=%async_computation.1 | async-start | bytes 131072 | tf_op jit(solution)/shard_map/all_to_all | solution.py:507
  82.4 4.2 %collective-permute-start.3 = (f32[1,512]{1,0:T(1,128)}, f32[1,512]{1,0:T(1,128)S(1)}, u32[]{:S(2)}, u32[]{:S(2)}) collective-permute-start(f32[1,512]{1,0:T(1,128)} %copy-done.45), channel_id=1, source_target_pairs={{8,0},{16,8},{24,16},{32,24},{40,32},{48,40},{56,48},{64,56},{72,6... | collective-permute-start | bytes 6152 | tf_op jit(solution)/shard_map/ppermute | solution.py:510
  86.6 2.5 %collective-permute-start.4 = (f32[1,512]{1,0:T(1,128)}, f32[1,512]{1,0:T(1,128)S(1)}, u32[]{:S(2)}, u32[]{:S(2)}) collective-permute-start(f32[1,512]{1,0:T(1,128)} %copy-done.44), channel_id=1, source_target_pairs={{1,0},{2,1},{3,2},{4,3},{5,4},{6,5},{7,6},{9,8},{10,9},{11,10},{12... | collective-permute-start | bytes 6152 | tf_op jit(solution)/shard_map/ppermute | solution.py:511
  89.1 2.5 %collective-permute-done.4.hcol = f32[1,512]{1,0:T(1,128)S(1)} collective-permute-done((f32[1,512]{1,0:T(1,128)}, f32[1,512]{1,0:T(1,128)S(1)}, u32[]{:S(2)}, u32[]{:S(2)}) %collective-permute-start.4) | collective-permute-done | bytes 2080 | tf_op jit(solution)/shard_map/ppermute | solution.py:511
  91.7 1.2 %copy-done.16 = f32[512,512]{1,0:T(8,128)S(1)} copy-done((f32[512,512]{1,0:T(8,128)S(1)}, f32[512,512]{1,0:T(8,128)}, u32[]{:S(2)}) %copy-start.16) | copy-done | bytes 1048600
  92.9 1.2 %copy-done.18 = f32[512,512]{1,0:T(8,128)S(1)} copy-done((f32[512,512]{1,0:T(8,128)S(1)}, f32[512,512]{1,0:T(8,128)}, u32[]{:S(2)}) %copy-start.18) | copy-done | bytes 1048600
  94.1 1.2 %copy-done.20 = f32[512,512]{1,0:T(8,128)S(1)} copy-done((f32[512,512]{1,0:T(8,128)S(1)}, f32[512,512]{1,0:T(8,128)}, u32[]{:S(2)}) %copy-start.20) | copy-done | bytes 1048600
  95.4 2.3 %fluxes.1 = f32[3,512,512]{2,1,0:T(8,128)} custom-call(f32[512,512]{1,0:T(8,128)S(1)} %copy-done.16, f32[512,512]{1,0:T(8,128)S(1)} %copy-done.18, f32[512,512]{1,0:T(8,128)S(1)} %copy-done.20, f32[1,512]{1,0:T(1,128)S(1)} %collective-permute-done.3.hrow, f32[1,512]{1,0:T(1,128)S(1)} %collective-permute-done.4.hcol), custom_call_target="tpu_custom_call" | custom-call | flops 2621440 | bytes 6291456 | tf_op jit(solution)/shard_map/fluxes/pallas_call | solution.py:463
  (86 shorter events, 22.8 us)
Async XLA Ops:
  0.6 1.9 %copy-start = (f32[3,512,512]{2,1,0:T(8,128)S(1)}, f32[3,512,512]{2,1,0:T(8,128)}, u32[]{:S(2)}) copy-start(f32[3,512,512]{2,1,0:T(8,128)} %adj.5) | copy-start | bytes 9437188
  2.5 2.2 %copy-start.2 = (f32[64,128,128]{2,1,0:T(8,128)S(1)}, f32[64,128,128]{2,1,0:T(8,128)}, u32[]{:S(2)}) copy-start(f32[64,128,128]{2,1,0:T(8,128)} %block_x.3) | copy-start | bytes 12582916
  4.7 1.6 %copy-start.4 = (f32[32,128,128]{2,1,0:T(8,128)S(1)}, f32[32,128,128]{2,1,0:T(8,128)}, u32[]{:S(2)}) copy-start(f32[32,128,128]{2,1,0:T(8,128)} %block_y.3) | copy-start | bytes 6291460
  6.3 1.2 %copy-start.6 = (f32[512,512]{1,0:T(8,128)S(1)}, f32[512,512]{1,0:T(8,128)}, u32[]{:S(2)}) copy-start(f32[512,512]{1,0:T(8,128)} %depth.3) | copy-start | bytes 3145732
  7.5 29.8 %copy-start.1 = (f32[3,512,512]{2,1,0:T(8,128)S(1)}, f32[3,512,512]{2,1,0:T(8,128)}, u32[]{:S(2)}) copy-start(f32[3,512,512]{2,1,0:T(8,128)} %adj.5) | copy-start | bytes 9437188
  10.9 9.4 %copy-start.30 = (f32[8,640]{1,0:T(8,128)}, f32[8,640]{1,0:T(8,128)S(1)}, u32[]{:S(2)}) copy-start(f32[8,640]{1,0:T(8,128)S(1)} %get-tuple-element.21) | copy-start | bytes 61444
  10.9 8.0 %collective-permute-start = (f32[1,8,640]{2,1,0:T(8,128)S(1)}, f32[1,8,640]{2,1,0:T(8,128)S(1)}, u32[]{:S(2)}, u32[]{:S(2)}) collective-permute-start(f32[1,8,640]{2,1,0:T(8,128)S(1)} %bitcast.10), channel_id=1, source_target_pairs={{0,1},{1,0},{2,3},{3,2},{4,5},{5,4},{6,7},{7,6},{8,9},{9,8},{10,11... | collective-permute-start | bytes 61448 | tf_op jit(solution)/shard_map/ppermute | solution.py:498
  11.6 39.2 %all-to-all-start = ((f32[16,8,640]{2,1,0:T(8,128)}), f32[16,8,640]{2,1,0:T(8,128)S(1)}, u32[]{:S(2)}, u32[]{:S(2)}) async-start(f32[16,8,640]{2,1,0:T(8,128)} %copy-done.23), calls=%async_computation | async-start | bytes 655360 | tf_op jit(solution)/shard_map/all_to_all | solution.py:494
  18.9 1.4 %copy-start.46 = (f32[1,8,640]{2,1,0:T(8,128)}, f32[1,8,640]{2,1,0:T(8,128)S(1)}, u32[]{:S(2)}) copy-start(f32[1,8,640]{2,1,0:T(8,128)S(1)} %collective-permute-done) | copy-start | bytes 61444
  19.0 2.9 %collective-permute-start.1 = (f32[2,8,640]{2,1,0:T(8,128)S(1)}, f32[2,8,640]{2,1,0:T(8,128)S(1)}, u32[]{:S(2)}, u32[]{:S(2)}) collective-permute-start(f32[2,8,640]{2,1,0:T(8,128)S(1)} %pad_maximum_fusion.1), channel_id=1, source_target_pairs={{0,2},{1,3},{2,0},{3,1},{4,6},{5,7},{6,4},{7,5},{8,10},{9,11},{10,... | collective-permute-start | bytes 122888 | tf_op jit(solution)/shard_map/ppermute | solution.py:498
  22.6 28.2 %collective-permute-start.2 = (f32[4,8,640]{2,1,0:T(8,128)S(1)}, f32[4,8,640]{2,1,0:T(8,128)}, u32[]{:S(2)}, u32[]{:S(2)}) collective-permute-start(f32[4,8,640]{2,1,0:T(8,128)S(1)} %pad_maximum_fusion.ta), channel_id=1, source_target_pairs={{0,4},{1,5},{2,6},{3,7},{4,0},{5,1},{6,2},{7,3},{8,12},{9,13},{10,... | collective-permute-start | bytes 245768 | tf_op jit(solution)/shard_map/ppermute | solution.py:500
  28.7 0.9 copy-start.14
  34.6 1.3 %copy-start.8 = (f32[256,2048]{1,0:T(8,128)}, f32[256,2048]{1,0:T(8,128)S(1)}, u32[]{:S(2)}) copy-start(f32[256,2048]{1,0:T(8,128)S(1)} %get-tuple-element.29.weights) | copy-start | bytes 6291460
  37.4 2.2 %copy-start.3 = (f32[64,128,128]{2,1,0:T(8,128)S(1)}, f32[64,128,128]{2,1,0:T(8,128)}, u32[]{:S(2)}) copy-start(f32[64,128,128]{2,1,0:T(8,128)} %block_x.3) | copy-start | bytes 12582916
  39.5 1.6 %copy-start.5 = (f32[32,128,128]{2,1,0:T(8,128)S(1)}, f32[32,128,128]{2,1,0:T(8,128)}, u32[]{:S(2)}) copy-start(f32[32,128,128]{2,1,0:T(8,128)} %block_y.3) | copy-start | bytes 6291460
  45.7 1.0 %copy-start.10 = (f32[512,512]{1,0:T(8,128)}, f32[512,512]{1,0:T(8,128)S(1)}, u32[]{:S(2)}) copy-start(f32[512,512]{1,0:T(8,128)S(1)} %get-tuple-element.22.yx) | copy-start | bytes 3145732
  46.7 1.0 copy-start.12
  50.8 1.2 %copy-start.7 = (f32[512,512]{1,0:T(8,128)S(1)}, f32[512,512]{1,0:T(8,128)}, u32[]{:S(2)}) copy-start(f32[512,512]{1,0:T(8,128)} %depth.3) | copy-start | bytes 3145732
  52.0 1.6 %copy-start.9 = (f32[256,2048]{1,0:T(8,128)S(1)}, f32[256,2048]{1,0:T(8,128)}, u32[]{:S(2)}) copy-start(f32[256,2048]{1,0:T(8,128)} %copy-done.8) | copy-start | bytes 6291460
  53.6 1.2 %copy-start.11 = (f32[512,512]{1,0:T(8,128)S(1)}, f32[512,512]{1,0:T(8,128)}, u32[]{:S(2)}) copy-start(f32[512,512]{1,0:T(8,128)} %copy-done.10) | copy-start | bytes 3145732
  54.8 1.2 %copy-start.13 = (f32[512,512]{1,0:T(8,128)S(1)}, f32[512,512]{1,0:T(8,128)}, u32[]{:S(2)}) copy-start(f32[512,512]{1,0:T(8,128)} %copy-done.12) | copy-start | bytes 3145732
  56.1 1.0 %copy-start.22 = (bf16[128,2048]{1,0:T(8,128)(2,1)S(1)}, bf16[128,2048]{1,0:T(8,128)(2,1)}, u32[]{:S(2)}) copy-start(bf16[128,2048]{1,0:T(8,128)(2,1)} %copy-done.21) | copy-start | bytes 1572868
  57.1 0.9 copy-start.25
  68.6 1.0 copy-start.15
  69.5 1.0 %copy-start.17 = (f32[512,512]{1,0:T(8,128)}, f32[512,512]{1,0:T(8,128)S(1)}, u32[]{:S(2)}) copy-start(f32[512,512]{1,0:T(8,128)S(1)} %get-tuple-element.33.fx) | copy-start | bytes 3145732
  70.6 1.0 copy-start.19
  73.3 24.4 %all-to-all-start.1 = ((f32[128,1,128]{2,1,0:T(1,128)}), f32[128,1,128]{2,1,0:T(1,128)S(1)}, u32[]{:S(2)}, u32[]{:S(2)}) async-start(f32[128,1,128]{2,1,0:T(1,128)} %bitcast.13), calls=%async_computation.1 | async-start | bytes 131072 | tf_op jit(solution)/shard_map/all_to_all | solution.py:507
  82.4 6.7 %collective-permute-start.3 = (f32[1,512]{1,0:T(1,128)}, f32[1,512]{1,0:T(1,128)S(1)}, u32[]{:S(2)}, u32[]{:S(2)}) collective-permute-start(f32[1,512]{1,0:T(1,128)} %copy-done.45), channel_id=1, source_target_pairs={{8,0},{16,8},{24,16},{32,24},{40,32},{48,40},{56,48},{64,56},{72,6... | collective-permute-start | bytes 6152 | tf_op jit(solution)/shard_map/ppermute | solution.py:510
  86.6 5.1 %collective-permute-start.4 = (f32[1,512]{1,0:T(1,128)}, f32[1,512]{1,0:T(1,128)S(1)}, u32[]{:S(2)}, u32[]{:S(2)}) collective-permute-start(f32[1,512]{1,0:T(1,128)} %copy-done.44), channel_id=1, source_target_pairs={{1,0},{2,1},{3,2},{4,3},{5,4},{6,5},{7,6},{9,8},{10,9},{11,10},{12... | collective-permute-start | bytes 6152 | tf_op jit(solution)/shard_map/ppermute | solution.py:511
  91.7 1.2 %copy-start.16 = (f32[512,512]{1,0:T(8,128)S(1)}, f32[512,512]{1,0:T(8,128)}, u32[]{:S(2)}) copy-start(f32[512,512]{1,0:T(8,128)} %copy-done.15) | copy-start | bytes 3145732
  92.9 1.2 %copy-start.18 = (f32[512,512]{1,0:T(8,128)S(1)}, f32[512,512]{1,0:T(8,128)}, u32[]{:S(2)}) copy-start(f32[512,512]{1,0:T(8,128)} %copy-done.17) | copy-start | bytes 3145732
  94.1 1.2 %copy-start.20 = (f32[512,512]{1,0:T(8,128)S(1)}, f32[512,512]{1,0:T(8,128)}, u32[]{:S(2)}) copy-start(f32[512,512]{1,0:T(8,128)} %copy-done.19) | copy-start | bytes 3145732
  (22 other events, 15.9 us)

commit v2 on v1

v2 whole, which is shorter than its diff:
```python
import jax
import jax.numpy as jnp
from jax import lax
from jax.experimental import pallas as pl
from jax.experimental.pallas import tpu as pltpu
from jax.sharding import PartitionSpec as P

courant = 0.5
f32 = jnp.float32
bf16 = jnp.bfloat16
K = 128
EXTRA = 128

NN = (((1,), (0,)), ((), ()))
NT = (((1,), (1,)), ((), ()))
TN = (((0,), (0,)), ((), ()))


def halves(x):
    high = x.astype(bf16)
    return high, (x - high.astype(f32)).astype(bf16)


def mm(a, b, dims):
    return lax.dot_general(a, b, dims, preferred_element_type=f32)


def mm3(a, b, dims):
    ah, al = a
    bh, bl = b
    return mm(ah, bh, dims) + (mm(ah, bl, dims) + mm(al, bh, dims))


def exact(a, b, dims):
    return lax.dot_general(a, b, dims, precision=lax.Precision.HIGHEST, preferred_element_type=f32)


def iota(shape, dim):
    return lax.broadcasted_iota(jnp.int32, shape, dim)


def hbm_spec():
    return pl.BlockSpec(memory_space=pltpu.HBM)


def vmem_spec():
    return pl.BlockSpec(memory_space=pltpu.VMEM)


def in_hbm(*arrays):
    return tuple(pltpu.with_memory_space_constraint(a, pltpu.HBM) for a in arrays)


def in_vmem(*arrays):
    return tuple(pltpu.with_memory_space_constraint(a, pltpu.VMEM) for a in arrays)


def cost(flops, nbytes):
    return pl.CostEstimate(flops=flops, bytes_accessed=nbytes, transcendentals=0)


def ends_kernel(
    adj, depth, block_x, block_y, px_hbm, py, vx, vy, wx0, wx1, wy0, wy1, drow, dcol, px, sems, out_sems
):
    u = lax.axis_index("gx")
    v = lax.axis_index("gy")
    rows, cols = vx.shape
    nbx = wx0.shape[0]
    nby = wy0.shape[0]
    small = [
        pltpu.make_async_copy(block_x.at[pl.ds(u * nbx, nbx), pl.ds(0, 8), :], wx0, sems.at[0]),
        pltpu.make_async_copy(block_x.at[pl.ds(u * nbx, nbx), pl.ds(K - 8, 8), :], wx1, sems.at[1]),
        pltpu.make_async_copy(block_y.at[pl.ds(v * nby, nby), pl.ds(0, 8), :], wy0, sems.at[2]),
        pltpu.make_async_copy(block_y.at[pl.ds(v * nby, nby), pl.ds(K - 8, 8), :], wy1, sems.at[3]),
        pltpu.make_async_copy(depth.at[pl.ds(rows - 8, 8), :], drow, sems.at[4]),
        pltpu.make_async_copy(depth.at[:, pl.ds(cols - K, K)], dcol, sems.at[5]),
    ]
    for copy in small:
        copy.start()
    big = []
    for c in range(nbx):
        here = pl.ds(c * K, K)
        big.append(pltpu.make_async_copy(adj.at[1, here, :], vx.at[here, :], sems.at[6 + c]))
    for c in range(nbx):
        here = pl.ds(c * K, K)
        big.append(pltpu.make_async_copy(adj.at[2, here, :], vy.at[here, :], sems.at[6 + nbx + c]))
    for copy in big:
        copy.start()
    for copy in small:
        copy.wait()

    def stacked(first, last, c):
        high, low = halves(jnp.concatenate([first[c, 0:1, :], last[c, 7:8, :]], axis=0))
        return jnp.concatenate([high, low], axis=0)

    def product(weights, high, low, dims):
        both = mm(weights, high, dims)
        return both[0:2] + both[2:4] + mm(weights[0:2], low, dims)

    ends_x = [stacked(wx0, wx1, c) for c in range(nbx)]
    ends_y = [stacked(wy0, wy1, c) for c in range(nby)]
    for part in range(cols // K):
        px[part : part + 1, cols:] = drow[7:8, part * K : (part + 1) * K]
    px[cols // K :, cols:] = jnp.zeros((8 - cols // K, EXTRA), f32)
    for c in range(nbx):
        big[c].wait()
        high, low = halves(vx[c * K : (c + 1) * K, :])
        px[2 * c : 2 * c + 2, :cols] = product(ends_x[c], high, low, NN)
    outs = [pltpu.make_async_copy(px, px_hbm.at[d], out_sems.at[d]) for d in range(px_hbm.shape[0])]
    for copy in outs:
        copy.start()
    last = (iota((8, K), 1) == K - 1).astype(f32).astype(bf16)
    high, low = halves(dcol[...])
    side = mm(last, high, NT) + mm(last, low, NT)
    for part in range(rows // K):
        py[part : part + 1, rows:] = side[0:1, part * K : (part + 1) * K]
    py[rows // K :, rows:] = jnp.zeros((8 - rows // K, EXTRA), f32)
    for r in range(nbx):
        big[nbx + r].wait()
        for c in range(nby):
            high, low = halves(vy[r * K : (r + 1) * K, c * K : (c + 1) * K])
            py[2 * c : 2 * c + 2, r * K : (r + 1) * K] = product(ends_y[c], high, low, NT)
    for copy in outs:
        copy.wait()


def ends(adj, depth, block_x, block_y, size_x, size_y):
    rows, cols = depth.shape
    nbx = block_x.shape[0] // size_x
    nby = block_y.shape[0] // size_y
    return pl.pallas_call(
        ends_kernel,
        out_shape=(
            pltpu.HBM((size_x, 2 * nbx, cols + EXTRA), f32),
            jax.ShapeDtypeStruct((2 * nby, rows + EXTRA), f32),
        ),
        in_specs=[hbm_spec()] * 4,
        out_specs=(hbm_spec(), vmem_spec()),
        scratch_shapes=[
            pltpu.VMEM((rows, cols), f32),
            pltpu.VMEM((rows, cols), f32),
            pltpu.VMEM((nbx, 8, K), f32),
            pltpu.VMEM((nbx, 8, K), f32),
            pltpu.VMEM((nby, 8, K), f32),
            pltpu.VMEM((nby, 8, K), f32),
            pltpu.VMEM((8, cols), f32),
            pltpu.VMEM((rows, K), f32),
            pltpu.VMEM((2 * nbx, cols + EXTRA), f32),
            pltpu.SemaphoreType.DMA((6 + 2 * nbx,)),
            pltpu.SemaphoreType.DMA((size_x,)),
        ],
        compiler_params=pltpu.CompilerParams(vmem_limit_bytes=16 << 20),
        cost_estimate=cost(2 * rows * cols * 32, 3 << 20),
        name="ends",
    )(*in_hbm(adj, depth, block_x, block_y))


def local_kernel(
    adj, block_x, block_y, reduced_x_hbm, reduced_y_hbm,
    yx_hbm, yy_hbm, gxh_hbm, gxl_hbm, gyh_hbm, gyl_hbm, gside_hbm,
    yx, yy, gxh, gxl, gyh, gyl, gside, vx, vy, wx, wy, wpx, wpy, reduced_x, reduced_y, sems, out_sems,
):
    u = lax.axis_index("gx")
    v = lax.axis_index("gy")
    rows, cols = vx.shape
    nbx = wx.shape[0]
    nby = wy.shape[0]
    before_x = jnp.maximum(u * nbx - 1, 0)
    before_y = jnp.maximum(v * nby - 1, 0)
    copies = [
        pltpu.make_async_copy(block_x.at[pl.ds(u * nbx, nbx)], wx, sems.at[0]),
        pltpu.make_async_copy(block_y.at[pl.ds(v * nby, nby)], wy, sems.at[1]),
        pltpu.make_async_copy(block_x.at[before_x, pl.ds(K - 8, 8), :], wpx, sems.at[2]),
        pltpu.make_async_copy(block_y.at[before_y, pl.ds(K - 8, 8), :], wpy, sems.at[3]),
        pltpu.make_async_copy(reduced_x_hbm, reduced_x, sems.at[4]),
        pltpu.make_async_copy(reduced_y_hbm, reduced_y, sems.at[5]),
        pltpu.make_async_copy(adj.at[1], vx, sems.at[6]),
        pltpu.make_async_copy(adj.at[2], vy, sems.at[7]),
    ]
    for copy in copies:
        copy.start()
    for copy in copies[:6]:
        copy.wait()
    own_x = reduced_x[pl.ds(pl.multiple_of(u * 8, 8), 8), :]
    own_y = reduced_y[pl.ds(pl.multiple_of(v * 8, 8), 8), :]
    prev_x = reduced_x[pl.ds(pl.multiple_of(jnp.maximum(u - 1, 0) * 8, 8), 8), :]
    prev_y = reduced_y[pl.ds(pl.multiple_of(jnp.maximum(v - 1, 0) * 8, 8), 8), :]
    for c in range(nbx):
        w = wx[c]
        g = w[:, 0:1] * own_x[2 * c : 2 * c + 1, :] + w[:, K - 1 : K] * own_x[2 * c + 1 : 2 * c + 2, :]
        high, low = halves(g)
        gxh[c * K : (c + 1) * K, :] = high
        gxl[c * K : (c + 1) * K, :] = low
    row = iota((8, K), 0)
    lane = iota((8, K), 1)
    for c in range(nby):
        pick = (((row == 2 * c) & (lane == 0)) | ((row == 2 * c + 1) & (lane == K - 1))).astype(f32)
        across = exact(pick, wy[c], NT)
        high, low = halves(exact(own_y, across, TN))
        gyh[:, c * K : (c + 1) * K] = high
        gyl[:, c * K : (c + 1) * K] = low

    def side(w, prev, index):
        width = prev.shape[1]
        g = w[7:8, 0:1] * prev[6:7, :] + w[7:8, K - 1 : K] * prev[7:8, :]
        g = g + (iota((1, width), 1) == index * 8 - 1).astype(f32)
        return jnp.where(index > 0, g, 0.0)

    gside[...] = jnp.zeros(gside.shape, f32)
    gside[0:1, :] = side(wpx[...], prev_x, u)
    gside[1:2, : reduced_y.shape[1]] = side(wpy[...], prev_y, v)
    outs = [
        pltpu.make_async_copy(gxh, gxh_hbm, out_sems.at[2]),
        pltpu.make_async_copy(gxl, gxl_hbm, out_sems.at[3]),
        pltpu.make_async_copy(gyh, gyh_hbm, out_sems.at[4]),
        pltpu.make_async_copy(gyl, gyl_hbm, out_sems.at[5]),
        pltpu.make_async_copy(gside, gside_hbm, out_sems.at[6]),
    ]
    for copy in outs:
        copy.start()
    copies[6].wait()
    for c in range(nbx):
        yx[c * K : (c + 1) * K, :] = mm3(halves(wx[c]), halves(vx[c * K : (c + 1) * K, :]), NN)
    outs.append(pltpu.make_async_copy(yx, yx_hbm, out_sems.at[0]))
    outs[-1].start()
    copies[7].wait()
    for c in range(nby):
        yy[:, c * K : (c + 1) * K] = mm3(halves(vy[:, c * K : (c + 1) * K]), halves(wy[c]), NT)
    outs.append(pltpu.make_async_copy(yy, yy_hbm, out_sems.at[1]))
    outs[-1].start()
    for copy in outs:
        copy.wait()


def local(adj, block_x, block_y, reduced_x, reduced_y, size_x, size_y):
    _, rows, cols = adj.shape
    nbx = block_x.shape[0] // size_x
    nby = block_y.shape[0] // size_y
    results = [
        ((rows, cols), f32),
        ((rows, cols), f32),
        ((rows, reduced_x.shape[0]), bf16),
        ((rows, reduced_x.shape[0]), bf16),
        ((reduced_y.shape[0], cols), bf16),
        ((reduced_y.shape[0], cols), bf16),
        ((8, reduced_x.shape[0]), f32),
    ]
    return pl.pallas_call(
        local_kernel,
        out_shape=tuple(pltpu.HBM(*result) for result in results),
        in_specs=[hbm_spec()] * 5,
        out_specs=(hbm_spec(),) * 7,
        scratch_shapes=[pltpu.VMEM(*result) for result in results]
        + [
            pltpu.VMEM((rows, cols), f32),
            pltpu.VMEM((rows, cols), f32),
            pltpu.VMEM((nbx, K, K), f32),
            pltpu.VMEM((nby, K, K), f32),
            pltpu.VMEM((8, K), f32),
            pltpu.VMEM((8, K), f32),
            pltpu.VMEM(reduced_x.shape, f32),
            pltpu.VMEM(reduced_y.shape, f32),
            pltpu.SemaphoreType.DMA((8,)),
            pltpu.SemaphoreType.DMA((7,)),
        ],
        compiler_params=pltpu.CompilerParams(vmem_limit_bytes=16 << 20),
        cost_estimate=cost(12 * rows * cols * K, 5 << 20),
        name="local",
    )(*in_hbm(adj, block_x, block_y, reduced_x, reduced_y))


def faults_kernel(
    wet_hbm, coef_hbm, footprint_hbm, owner_hbm,
    weights_hbm, high_hbm, low_hbm,
    weights, high_of, low_of, dist, coef8, wet, coef, footprint, owner, sems, out_sems,
):
    copies = [
        pltpu.make_async_copy(wet_hbm, wet, sems.at[0]),
        pltpu.make_async_copy(coef_hbm, coef, sems.at[1]),
        pltpu.make_async_copy(footprint_hbm, footprint, sems.at[2]),
        pltpu.make_async_copy(owner_hbm, owner, sems.at[3]),
    ]
    for copy in copies:
        copy.start()
    for copy in copies:
        copy.wait()
    u = lax.axis_index("gx")
    v = lax.axis_index("gy")
    tiles_y, tiles_x = wet.shape
    total_cols = tiles_y * lax.axis_size("gy")
    shift = total_cols.bit_length() - 1
    count = footprint.shape[1]
    places = footprint.shape[0]
    sub = iota((8, count), 0)
    for f in range(places):
        tile = footprint[f : f + 1, :]
        row = lax.shift_right_logical(tile, shift) - u * tiles_x
        col = (tile & (total_cols - 1)) - v * tiles_y
        inside = (row >= 0) & (row < tiles_x) & (col >= 0) & (col < tiles_y)
        flat = jnp.where(inside, col * tiles_x + row, -1000)
        dist[f] = flat - lax.shift_right_logical(sub, 2)
        four = coef[f]
        coef8[f] = jnp.concatenate([four, four], axis=0)

    def group(g, carry):
        acc = jnp.zeros((8, count), f32)
        for f in range(places):
            acc = acc + jnp.where(dist[f] == 2 * g, coef8[f], 0.0)
        col = (2 * g) // tiles_x
        row = 2 * g - col * tiles_x
        keep = jnp.where(sub < 4, wet[col, row].astype(f32), wet[col, row + 1].astype(f32))
        weights[pl.ds(pl.multiple_of(g * 8, 8), 8), :] = acc * keep
        return carry

    lax.fori_loop(0, tiles_x * tiles_y // 2, group, 0)
    own = owner[...]
    slots = low_of.shape[0]
    bits = slots.bit_length() - 1
    high_of[...] = (iota(high_of.shape, 0) == lax.shift_right_logical(own, bits)).astype(f32).astype(bf16)
    low_of[...] = (iota(low_of.shape, 0) == (own & (slots - 1))).astype(f32)
    outs = [
        pltpu.make_async_copy(weights, weights_hbm, out_sems.at[0]),
        pltpu.make_async_copy(high_of, high_hbm, out_sems.at[1]),
        pltpu.make_async_copy(low_of, low_hbm, out_sems.at[2]),
    ]
    for copy in outs:
        copy.start()
    for copy in outs:
        copy.wait()


def faults(wet, coef, footprint, owner, devices):
    tiles_x, tiles_y = wet.shape
    subf, places, modes = coef.shape
    slots = subf // devices
    results = [
        ((tiles_x * tiles_y * modes, subf), f32),
        ((devices, subf), bf16),
        ((slots, subf), f32),
    ]
    return pl.pallas_call(
        faults_kernel,
        out_shape=tuple(pltpu.HBM(*result) for result in results),
        in_specs=[hbm_spec()] * 4,
        out_specs=(hbm_spec(),) * 3,
        scratch_shapes=[pltpu.VMEM(*result) for result in results]
        + [
            pltpu.VMEM((places, 8, subf), jnp.int32),
            pltpu.VMEM((places, 8, subf), f32),
            pltpu.SMEM((tiles_y, tiles_x), jnp.int32),
            pltpu.VMEM((places, modes, subf), f32),
            pltpu.VMEM((places, subf), jnp.int32),
            pltpu.VMEM((1, subf), jnp.int32),
            pltpu.SemaphoreType.DMA((4,)),
            pltpu.SemaphoreType.DMA((3,)),
        ],
        compiler_params=pltpu.CompilerParams(vmem_limit_bytes=16 << 20),
        cost_estimate=cost(40 << 20, 3 << 20),
        name="faults",
    )(*in_hbm(wet.T, coef.transpose(1, 2, 0), footprint.T, owner.reshape(1, subf)))


def elev_kernel(
    tx_in, ta_in, tb_in, yx_in, yy_in, gxh_in, gxl_in, gyh_in, gyl_in, gside_in, adj, depth, basis_in,
    weights_in, high_in, low_in,
    elev_out, fx_out, fy_out, parts_out,
    tx, ty, yx, yy, gxh, gxl, gyh, gyl, gside, a0, dep, basis, weights, high_of, low_of,
    elev, fx, fy, tyn, mom, parts, sems, row_sems, out_sems,
):
    u = lax.axis_index("gx")
    v = lax.axis_index("gy")
    rows, cols = dep.shape
    steps = rows // K
    half = ta_in.shape[0]
    first = [
        pltpu.make_async_copy(tx_in, tx, sems.at[0]),
        pltpu.make_async_copy(ta_in, ty.at[pl.ds(0, half)], sems.at[1]),
        pltpu.make_async_copy(tb_in, ty.at[pl.ds(half, half)], sems.at[2]),
        pltpu.make_async_copy(gside_in, gside, sems.at[3]),
        pltpu.make_async_copy(gxh_in, gxh, sems.at[4]),
        pltpu.make_async_copy(gxl_in, gxl, sems.at[5]),
        pltpu.make_async_copy(gyh_in, gyh, sems.at[6]),
        pltpu.make_async_copy(gyl_in, gyl, sems.at[7]),
        pltpu.make_async_copy(basis_in, basis, sems.at[8]),
    ]
    last = [
        pltpu.make_async_copy(weights_in, weights, sems.at[9]),
        pltpu.make_async_copy(high_in, high_of, sems.at[10]),
        pltpu.make_async_copy(low_in, low_of, sems.at[11]),
    ]
    fields = []
    for r in range(steps):
        here = pl.ds(r * K, K)
        fields.append(
            [
                pltpu.make_async_copy(yx_in.at[here, :], yx.at[here, :], row_sems.at[r, 0]),
                pltpu.make_async_copy(yy_in.at[here, :], yy.at[here, :], row_sems.at[r, 1]),
                pltpu.make_async_copy(depth.at[here, :], dep.at[here, :], row_sems.at[r, 2]),
                pltpu.make_async_copy(adj.at[0, here, :], a0.at[here, :], row_sems.at[r, 3]),
            ]
        )
    for group in [first, *fields, last]:
        for copy in group:
            copy.start()
    for copy in first:
        copy.wait()
    nx = tx.shape[0]
    tx_all = jnp.concatenate([tx[d][:, :cols] for d in range(nx)], axis=0)
    for j in range(2 * half):
        tyn[j * 8 : (j + 1) * 8, :] = ty[j ^ v]
    ty_all = tyn[:, :rows]
    txs = halves(tx_all)
    tys = halves(ty_all)
    up = jnp.maximum(u - 1, 0)
    left = jnp.maximum(v - 1, 0)
    gs = gside[...]
    edge_x = mm3(halves(gs), txs, NN)[0:1, :]
    edge_y = mm3(halves(gs[:, : ty_all.shape[0]]), tys, NN)[1:2, :]
    drow = tx[up][:, cols:]
    drow = jnp.concatenate([drow[p : p + 1, :] for p in range(cols // K)], axis=1)
    dcol = tyn[pl.ds(pl.multiple_of(left * 8, 8), 8), rows:]
    dcol = jnp.concatenate([dcol[p : p + 1, :] for p in range(rows // K)], axis=1)
    carry = edge_x * drow
    side = halves(jnp.broadcast_to(edge_y * dcol, (8, rows)))
    row = iota((K, cols), 0)
    lane = iota((K, cols), 1)
    corner = ((iota((8, K), 1) == 0) & (iota((8, K), 0) == 0)).astype(f32).astype(bf16)
    modes, tile_h, tile_w = basis.shape
    per = K // tile_h
    wide = [jnp.concatenate([basis[b]] * (cols // tile_w), axis=1) for b in range(modes)]
    outs = []
    firsts = []
    for r in range(steps):
        here = slice(r * K, (r + 1) * K)
        for copy in fields[r]:
            copy.wait()
        d = dep[here, :]
        flux_x = yx[here, :] + mm3((gxh[here, :], gxl[here, :]), txs, NN)
        part = (tys[0][:, here], tys[1][:, here])
        flux_y = yy[here, :] + mm3(part, (gyh[...], gyl[...]), TN)
        fx[here, :] = flux_x
        fy[here, :] = flux_y
        weighted_x = d * flux_x
        weighted_y = d * flux_y
        before_x = jnp.where(row == 0, carry, pltpu.roll(weighted_x, 1, 0))
        carry = weighted_x[K - 1 : K, :]
        edge = mm(side[0][:, here], corner, TN) + mm(side[1][:, here], corner, TN)
        edge = jnp.concatenate([edge, jnp.zeros((K, cols - K), f32)], axis=1)
        before_y = jnp.where(lane == 0, edge, pltpu.roll(weighted_y, 1, 1))
        e = a0[here, :] + courant * ((weighted_x - before_x) + (weighted_y - before_y))
        elev[here, :] = e
        where = pl.ds(r * K, K)
        for i, (source, target) in enumerate(((elev, elev_out), (fx, fx_out), (fy, fy_out))):
            copy = pltpu.make_async_copy(source.at[where, :], target.at[where, :], out_sems.at[r, i])
            copy.start()
            outs.append(copy)
        if r == 0:
            top = e[0:1, :]
        eh, el = halves(e[:, :K])
        firsts.append((mm(corner, eh, NT) + mm(corner, el, NT))[0:1, :])
        for a in range(per):
            tile = e[a * tile_h : (a + 1) * tile_h, :]
            for b in range(modes):
                at = (r * per + a) * modes + b
                mom[at : at + 1, :] = jnp.sum(tile * wide[b], axis=0, keepdims=True)
    for copy in last:
        copy.wait()
    total = None
    group = mom.shape[0]
    for w in range(cols // tile_w):
        m = jnp.sum(mom[:, w * tile_w : (w + 1) * tile_w], axis=1, keepdims=True)
        term = jnp.sum(weights[w * group : (w + 1) * group, :] * m, axis=0, keepdims=True)
        total = term if total is None else total + term
    high, low = halves(low_of[...] * total)
    sums = mm(high_of[...], high, NT) + mm(high_of[...], low, NT)
    devices, slots = sums.shape
    parts[...] = jnp.zeros(parts.shape, f32)
    parts[pl.ds(0, devices, stride=8), :] = jnp.concatenate(
        [sums, jnp.zeros((devices, K - slots), f32)], axis=1
    )
    size_y = lax.axis_size("gy")

    def put(device, line):
        at = pl.ds(pl.multiple_of(device * 8, 8), 8)
        below = jnp.concatenate(
            [jnp.zeros((4, K), f32)] + [line[:, p * K : (p + 1) * K] for p in range(4)], axis=0
        )
        parts[at, :] = parts[at, :] + below

    @pl.when(u > 0)
    def _():
        put((u - 1) * size_y + v, top)

    @pl.when(v > 0)
    def _():
        put(u * size_y + v - 1, jnp.concatenate(firsts, axis=1))

    outs.append(pltpu.make_async_copy(parts, parts_out, sems.at[12]))
    outs[-1].start()
    for copy in outs:
        copy.wait()


def elevation(tx, ta, tb, solved, adj, depth, basis, weights, high_of, low_of):
    rows, cols = depth.shape
    modes, tile_h, tile_w = basis.shape
    devices = high_of.shape[0]
    steps = rows // K
    field = ((rows, cols), f32)
    far = (2 * ta.shape[0], 8, rows + EXTRA)
    parts = ((devices * 8, K), f32)
    like = lambda a: pltpu.VMEM(a.shape, a.dtype)
    return pl.pallas_call(
        elev_kernel,
        out_shape=(pltpu.HBM(*field),) * 3 + (pltpu.HBM(*parts),),
        in_specs=[pl.BlockSpec(memory_space=pl.ANY)] * 3 + [hbm_spec()] * 13,
        out_specs=(hbm_spec(),) * 4,
        scratch_shapes=[like(tx), pltpu.VMEM(far, f32)]
        + [like(a) for a in solved]
        + [pltpu.VMEM(*field)] * 2
        + [like(a) for a in (basis, weights, high_of, low_of)]
        + [pltpu.VMEM(*field)] * 3
        + [
            pltpu.VMEM((far[0] * 8, far[2]), f32),
            pltpu.VMEM((rows // tile_h * modes, cols), f32),
            pltpu.VMEM(*parts),
            pltpu.SemaphoreType.DMA((13,)),
            pltpu.SemaphoreType.DMA((steps, 4)),
            pltpu.SemaphoreType.DMA((steps, 3)),
        ],
        compiler_params=pltpu.CompilerParams(vmem_limit_bytes=32 << 20),
        cost_estimate=cost(12 * rows * cols * K, 10 << 20),
        name="elevation",
    )(tx, ta, tb, *in_hbm(*solved, adj, depth, basis, weights, high_of, low_of))


def fluxes_kernel(elev_in, fx_in, fy_in, out, e, x, y, sems, out_sems):
    rows, cols = e.shape
    steps = rows // K
    reads = []
    for r in range(steps):
        here = pl.ds(r * K, K)
        pairs = ((elev_in, e), (fx_in, x), (fy_in, y))
        reads.append(
            [
                pltpu.make_async_copy(source.at[here, :], target.at[here, :], sems.at[r, i])
                for i, (source, target) in enumerate(pairs)
            ]
        )
    for group in reads:
        for copy in group:
            copy.start()
    row = iota((K, cols), 0)
    lane = iota((K, cols), 1)
    writes = []
    for copy in reads[0]:
        copy.wait()
    for r in range(steps):
        here = slice(r * K, (r + 1) * K)
        after = 0.0
        if r + 1 < steps:
            for copy in reads[r + 1]:
                copy.wait()
            after = e[(r + 1) * K : (r + 1) * K + 1, :]
        now = e[here, :]
        below = jnp.where(row == K - 1, after, pltpu.roll(now, K - 1, 0))
        right = jnp.where(lane == cols - 1, 0.0, pltpu.roll(now, cols - 1, 1))
        x[here, :] = x[here, :] + courant * (below - now)
        y[here, :] = y[here, :] + courant * (right - now)
        where = pl.ds(r * K, K)
        for i, source in enumerate((e, x, y)):
            copy = pltpu.make_async_copy(source.at[where, :], out.at[i, where, :], out_sems.at[r, i])
            copy.start()
            writes.append(copy)
    for copy in writes:
        copy.wait()


def fluxes(elev, fx, fy):
    rows, cols = elev.shape
    return pl.pallas_call(
        fluxes_kernel,
        out_shape=pltpu.HBM((3, rows, cols), f32),
        in_specs=[hbm_spec()] * 3,
        out_specs=hbm_spec(),
        scratch_shapes=[
            pltpu.VMEM((rows, cols), f32),
            pltpu.VMEM((rows, cols), f32),
            pltpu.VMEM((rows, cols), f32),
            pltpu.SemaphoreType.DMA((rows // K, 3)),
            pltpu.SemaphoreType.DMA((rows // K, 3)),
        ],
        compiler_params=pltpu.CompilerParams(vmem_limit_bytes=16 << 20),
        cost_estimate=cost(10 * rows * cols, 6 << 20),
        name="fluxes",
    )(*in_hbm(elev, fx, fy))


def finish_kernel(fields_in, sums_in, fields, grad, sums, bottom, edge, sems, out_sems):
    u = lax.axis_index("gx")
    v = lax.axis_index("gy")
    size_x = lax.axis_size("gx")
    size_y = lax.axis_size("gy")
    rows, cols = fields.shape[1:]
    reads = [
        pltpu.make_async_copy(sums_in, sums, sems.at[0]),
        pltpu.make_async_copy(fields.at[1, pl.ds(rows - 8, 8), :], bottom, sems.at[1]),
        pltpu.make_async_copy(fields.at[2, :, pl.ds(cols - K, K)], edge, sems.at[2]),
    ]
    for copy in reads:
        copy.start()
    for copy in reads:
        copy.wait()

    def line(device):
        part = sums[pl.ds(pl.multiple_of(device * 8, 8), 8), :]
        return jnp.concatenate([part[4 + p : 5 + p, :] for p in range(4)], axis=1)

    below = line(jnp.minimum(u + 1, size_x - 1) * size_y + v) * jnp.where(u + 1 < size_x, courant, 0.0)
    right = line(u * size_y + jnp.minimum(v + 1, size_y - 1)) * jnp.where(v + 1 < size_y, courant, 0.0)
    bottom[7:8, :] = bottom[7:8, :] + below
    corner = ((iota((8, K), 1) == K - 1) & (iota((8, K), 0) == 0)).astype(f32).astype(bf16)
    high, low = halves(jnp.broadcast_to(right, (8, rows)))
    edge[...] = edge[...] + (mm(high, corner, TN) + mm(low, corner, TN))
    writes = [
        pltpu.make_async_copy(bottom, fields.at[1, pl.ds(rows - 8, 8), :], out_sems.at[0]),
        pltpu.make_async_copy(edge, fields.at[2, :, pl.ds(cols - K, K)], out_sems.at[1]),
    ]
    for copy in writes:
        copy.start()
    devices = sums.shape[0] // 8
    grad[...] = jnp.sum(sums[pl.ds(0, devices, stride=8), :], axis=0, keepdims=True)
    for copy in writes:
        copy.wait()


def finish(fields, sums):
    _, rows, cols = fields.shape
    return pl.pallas_call(
        finish_kernel,
        out_shape=(pltpu.HBM(fields.shape, f32), jax.ShapeDtypeStruct((1, K), f32)),
        in_specs=[hbm_spec(), pl.BlockSpec(memory_space=pl.ANY)],
        out_specs=(hbm_spec(), vmem_spec()),
        input_output_aliases={0: 0},
        scratch_shapes=[
            pltpu.VMEM(sums.shape, f32),
            pltpu.VMEM((8, cols), f32),
            pltpu.VMEM((rows, K), f32),
            pltpu.SemaphoreType.DMA((3,)),
            pltpu.SemaphoreType.DMA((2,)),
        ],
        compiler_params=pltpu.CompilerParams(vmem_limit_bytes=16 << 20),
        cost_estimate=cost(1 << 20, 1 << 20),
        name="finish",
    )(*in_hbm(fields), sums)


def partner(axis, bit):
    return [(i, i ^ bit) for i in range(lax.axis_size(axis))]


def body(
    adj_fields, depth, block_x, reduced_x, block_y, reduced_y, basis, coef, footprint, owner, wet
):
    size_x = lax.axis_size("gx")
    size_y = lax.axis_size("gy")
    px, py = ends(adj_fields, depth, block_x, block_y, size_x, size_y)
    tx = lax.all_to_all(px, "gx", split_axis=0, concat_axis=0, tiled=True)
    ty = py[None]
    bit = 1
    while 2 * bit < size_y:
        ty = jnp.concatenate([ty, lax.ppermute(ty, "gy", partner("gy", bit))], axis=0)
        bit *= 2
    ty_far = lax.ppermute(ty, "gy", partner("gy", bit))
    solved = local(adj_fields, block_x, block_y, reduced_x, reduced_y, size_x, size_y)
    chosen = faults(wet, coef, footprint, owner, size_x * size_y)
    elev, fx, fy, parts = elevation(tx, ty, ty_far, solved, adj_fields, depth, basis, *chosen)
    devices = size_x * size_y
    sums = lax.all_to_all(
        parts.reshape(devices, 8, K), ("gx", "gy"), split_axis=0, concat_axis=0, tiled=True
    )
    adj_before, grad = finish(fluxes(elev, fx, fy), sums.reshape(parts.shape))
    return adj_before, grad[0, : owner.shape[0] // devices]


def solution(mesh):
    in_specs = (
        P(None, "gx", "gy"),
        P("gx", "gy"),
        P(),
        P(),
        P(),
        P(),
        P(),
        P(),
        P(),
        P(),
        P("gx", "gy"),
    )
    out_specs = (P(None, "gx", "gy"), P(("gx", "gy")))
    return jax.shard_map(body, mesh=mesh, in_specs=in_specs, out_specs=out_specs, check_vma=False)
```

time: 99.8 us -> 60.8 us (0.61)
  the two profiles are of different devices: /device:TPU:33 before, /device:TPU:1 now
where the time goes in v2:
time: 60.8 us; the launch traced here: 60.4 us
  Pallas kernels  24.9 us (41%)
  starting transfers between devices  22.4 us (37%)
  waiting for transfers between devices  11.9 us (20%)
  between operations  0.73 us (1%)
    all_to_all x1, waiting for transfers between devices, body(): lax.all_to_all(parts.reshape(devices, 8, K), ('gx', 'gy'), split_axis=0,...  10.3 us
    all_to_all x1, starting transfers between devices, body(): lax.all_to_all(parts.reshape(devices, 8, K), ('gx', 'gy'), split_axis=0,...  8.93 us
    all_to_all x1, starting transfers between devices, body(): tx = lax.all_to_all(px, 'gx', split_axis=0, concat_axis=0, tiled=True)  7.68 us
    pallas_call x1, Pallas kernels, elevation(): pl.pallas_call(elev_kernel, out_shape=(pltpu.HBM(*field),) * 3 + (pltpu.H...  7.2 us
    pallas_call x1, Pallas kernels, local(): pl.pallas_call(local_kernel, out_shape=tuple((pltpu.HBM(*result) for resu...  4.86 us
    pallas_call x1, Pallas kernels, faults(): pl.pallas_call(faults_kernel, out_shape=tuple((pltpu.HBM(*result) for res...  4.51 us
    pallas_call x1, Pallas kernels, fluxes(): pl.pallas_call(fluxes_kernel, out_shape=pltpu.HBM((3, rows, cols), f32),...  3.2 us
    pallas_call x1, Pallas kernels, ends(): pl.pallas_call(ends_kernel, out_shape=(pltpu.HBM((size_x, 2 * nbx, cols +...  3.13 us
  transfers between devices with their start and end apart: 5, of which 2 were waited for; matrix products, arithmetic and copies ran while one was open for 0% of the time, Pallas kernels for 21%

profile of v2, /device:TPU:1, one launch (start us, length us, event | category | flops | bytes accessed | tf_op | source)
XLA Modules:
  0.0 60.4 jit_solution(5946148297856558774)
XLA Ops:
  0.6 3.1 %ends.1 = (f32[16,8,640]{2,1,0:T(8,128)}, f32[8,640]{1,0:T(8,128)S(1)}) custom-call(f32[3,512,512]{2,1,0:T(8,128)} %adj.5, f32[512,512]{1,0:T(8,128)} %depth.3, f32[64,128,128]{2,1,0:T(8,128)} %block_x.3, f32[32,128,128]{2,1,0:T(8,128)} %block_y.3), custom_call_target="tpu_custom_call" | custom-call | flops 16777216 | bytes 3145728 | tf_op jit(solution)/shard_map/ends/pallas_call | solution.py:131
  3.8 1.5 %collective-permute-start = (f32[1,8,640]{2,1,0:T(8,128)S(1)}, f32[1,8,640]{2,1,0:T(8,128)S(1)}, u32[]{:S(2)}, u32[]{:S(2)}) collective-permute-start(f32[1,8,640]{2,1,0:T(8,128)S(1)} %bitcast.10), channel_id=1, source_target_pairs={{0,1},{1,0},{2,3},{3,2},{4,5},{5,4},{6,7},{7,6},{8,9},{9,8},{10,11... | collective-permute-start | bytes 61448 | tf_op jit(solution)/shard_map/ppermute | solution.py:672
  5.3 7.7 %all-to-all-start = ((f32[16,8,640]{2,1,0:T(8,128)}), f32[16,8,640]{2,1,0:T(8,128)S(1)}, u32[]{:S(2)}, u32[]{:S(2)}) async-start(f32[16,8,640]{2,1,0:T(8,128)} %get-tuple-element.20), calls=%async_computation | async-start | bytes 655360 | tf_op jit(solution)/shard_map/all_to_all | solution.py:668
  13.0 0.0 collective-permute-done
  13.0 1.4 %collective-permute-start.1 = (f32[2,8,640]{2,1,0:T(8,128)S(1)}, f32[2,8,640]{2,1,0:T(8,128)S(1)}, u32[]{:S(2)}, u32[]{:S(2)}) collective-permute-start(f32[2,8,640]{2,1,0:T(8,128)S(1)} %pad_maximum_fusion.1), channel_id=1, source_target_pairs={{0,2},{1,3},{2,0},{3,1},{4,6},{5,7},{6,4},{7,5},{8,10},{9,11},{10,... | collective-permute-start | bytes 122888 | tf_op jit(solution)/shard_map/ppermute | solution.py:672
  14.4 1.6 %collective-permute-done.1 = f32[2,8,640]{2,1,0:T(8,128)S(1)} collective-permute-done((f32[2,8,640]{2,1,0:T(8,128)S(1)}, f32[2,8,640]{2,1,0:T(8,128)S(1)}, u32[]{:S(2)}, u32[]{:S(2)}) %collective-permute-start.1) | collective-permute-done | bytes 40992 | tf_op jit(solution)/shard_map/ppermute | solution.py:672
  15.9 2.9 %collective-permute-start.2 = (f32[4,8,640]{2,1,0:T(8,128)S(1)}, f32[4,8,640]{2,1,0:T(8,128)S(1)}, u32[]{:S(2)}, u32[]{:S(2)}) collective-permute-start(f32[4,8,640]{2,1,0:T(8,128)S(1)} %pad_maximum_fusion.ta_in), channel_id=1, source_target_pairs={{0,4},{1,5},{2,6},{3,7},{4,0},{5,1},{6,2},{7,3},{8,12},{9,13},{10,... | collective-permute-start | bytes 245768 | tf_op jit(solution)/shard_map/ppermute | solution.py:674
  18.8 4.5 %faults.1 = (f32[256,2048]{1,0:T(8,128)}, bf16[128,2048]{1,0:T(8,128)(2,1)}, f32[16,2048]{1,0:T(8,128)}) custom-call(s32[4,16]{1,0:T(4,128)} %bitcast.17, f32[8,4,2048]{2,1,0:T(4,128)} %bitcast.14, s32[8,2048]{1,0:T(8,128)} %bitcast.15, s32[1,2048]{1,0:T(1,128)} %bitcast.16), custom_call_target="tpu_custom_call" | custom-call | flops 41943040 | bytes 3145728 | tf_op jit(solution)/shard_map/faults/pallas_call | solution.py:341
  23.3 4.9 %local.1 = (f32[512,512]{1,0:T(8,128)}, f32[512,512]{1,0:T(8,128)}, bf16[512,128]{1,0:T(8,128)(2,1)}, bf16[512,128]{1,0:T(8,128)(2,1)}, bf16[64,512]{1,0:T(8,128...) custom-call(f32[3,512,512]{2,1,0:T(8,128)} %adj.5, f32[64,128,128]{2,1,0:T(8,128)} %block_x.3, ...), custom_call_target="tpu_custom_call" | custom-call | flops 402653184 | bytes 5242880 | tf_op jit(solution)/shard_map/local/pallas_call | solution.py:248
  28.2 0.0 collective-permute-done.2.tb_in
  28.2 0.0 all-to-all-done.tx_in
  28.2 7.2 %elevation.1 = (f32[512,512]{1,0:T(8,128)}, f32[512,512]{1,0:T(8,128)}, f32[512,512]{1,0:T(8,128)}, f32[1024,128]{1,0:T(8,128)}) custom-call(f32[16,8,640]{2,1,0:T(8,128)S(1)} %all-to-all-done.tx_in, f32[4,8,640]{2,1,0:T(8,128)S(1)} %pad_maximum_fusion.ta_in, f32[4,8,640]{2,1,0:T(8,128)S(1)} %collective-permute-done.2.tb_in, ...), custom_call_target="tpu_custom_call" | custom-call | flops 402653184 | bytes 10485760 | tf_op jit(solution)/shard_map/elevation/pallas_call | solution.py:513
  35.4 8.9 %all-to-all-start.1 = ((f32[128,8,128]{2,1,0:T(8,128)}), f32[128,8,128]{2,1,0:T(8,128)S(1)}, u32[]{:S(2)}, u32[]{:S(2)}) async-start(f32[128,8,128]{2,1,0:T(8,128)} %bitcast.13), calls=%async_computation.1 | async-start | bytes 1048576 | tf_op jit(solution)/shard_map/all_to_all | solution.py:679
  44.4 3.2 %fluxes.1.fields_in = f32[3,512,512]{2,1,0:T(8,128)} custom-call(f32[512,512]{1,0:T(8,128)} %get-tuple-element.32.elev_in, f32[512,512]{1,0:T(8,128)} %get-tuple-element.33.fx_in, f32[512,512]{1,0:T(8,128)} %get-tuple-element.34.fy_in), custom_call_target="tpu_custom_call" | custom-call | flops 2621440 | bytes 6291456 | tf_op jit(solution)/shard_map/fluxes/pallas_call | solution.py:581
  47.6 10.3 %all-to-all-done.1 = f32[128,8,128]{2,1,0:T(8,128)S(1)} async-done(((f32[128,8,128]{2,1,0:T(8,128)}), f32[128,8,128]{2,1,0:T(8,128)S(1)}, u32[]{:S(2)}, u32[]{:S(2)}) %all-to-all-start.1) | async-done | bytes 524320 | tf_op jit(solution)/shard_map/all_to_all | solution.py:679
  57.9 2.0 %finish.1 = (f32[3,512,512]{2,1,0:T(8,128)}, f32[1,128]{1,0:T(1,128)S(1)}) custom-call(f32[3,512,512]{2,1,0:T(8,128)} %fluxes.1.fields_in, f32[1024,128]{1,0:T(8,128)S(1)} %bitcast.9), custom_call_target="tpu_custom_call", output_to_operand_aliasing={{0}: (0, {})} | custom-call | flops 1048576 | bytes 1048576 | tf_op jit(solution)/shard_map/finish/pallas_call | solution.py:639
  59.9 0.5 slice_bitcast_fusion
  (2 shorter events, 0.0 us)
Async XLA Ops:
  3.8 9.2 %collective-permute-start = (f32[1,8,640]{2,1,0:T(8,128)S(1)}, f32[1,8,640]{2,1,0:T(8,128)S(1)}, u32[]{:S(2)}, u32[]{:S(2)}) collective-permute-start(f32[1,8,640]{2,1,0:T(8,128)S(1)} %bitcast.10), channel_id=1, source_target_pairs={{0,1},{1,0},{2,3},{3,2},{4,5},{5,4},{6,7},{7,6},{8,9},{9,8},{10,11... | collective-permute-start | bytes 61448 | tf_op jit(solution)/shard_map/ppermute | solution.py:672
  5.3 23.0 %all-to-all-start = ((f32[16,8,640]{2,1,0:T(8,128)}), f32[16,8,640]{2,1,0:T(8,128)S(1)}, u32[]{:S(2)}, u32[]{:S(2)}) async-start(f32[16,8,640]{2,1,0:T(8,128)} %get-tuple-element.20), calls=%async_computation | async-start | bytes 655360 | tf_op jit(solution)/shard_map/all_to_all | solution.py:668
  13.0 2.9 %collective-permute-start.1 = (f32[2,8,640]{2,1,0:T(8,128)S(1)}, f32[2,8,640]{2,1,0:T(8,128)S(1)}, u32[]{:S(2)}, u32[]{:S(2)}) collective-permute-start(f32[2,8,640]{2,1,0:T(8,128)S(1)} %pad_maximum_fusion.1), channel_id=1, source_target_pairs={{0,2},{1,3},{2,0},{3,1},{4,6},{5,7},{6,4},{7,5},{8,10},{9,11},{10,... | collective-permute-start | bytes 122888 | tf_op jit(solution)/shard_map/ppermute | solution.py:672
  15.9 12.3 %collective-permute-start.2 = (f32[4,8,640]{2,1,0:T(8,128)S(1)}, f32[4,8,640]{2,1,0:T(8,128)S(1)}, u32[]{:S(2)}, u32[]{:S(2)}) collective-permute-start(f32[4,8,640]{2,1,0:T(8,128)S(1)} %pad_maximum_fusion.ta_in), channel_id=1, source_target_pairs={{0,4},{1,5},{2,6},{3,7},{4,0},{5,1},{6,2},{7,3},{8,12},{9,13},{10,... | collective-permute-start | bytes 245768 | tf_op jit(solution)/shard_map/ppermute | solution.py:674
  35.4 22.4 %all-to-all-start.1 = ((f32[128,8,128]{2,1,0:T(8,128)}), f32[128,8,128]{2,1,0:T(8,128)S(1)}, u32[]{:S(2)}, u32[]{:S(2)}) async-start(f32[128,8,128]{2,1,0:T(8,128)} %bitcast.13), calls=%async_computation.1 | async-start | bytes 1048576 | tf_op jit(solution)/shard_map/all_to_all | solution.py:679

commit v3 on v2

v3 whole, which is shorter than its diff:
```python
import jax
import jax.numpy as jnp
from jax import lax
from jax.experimental import pallas as pl
from jax.experimental.pallas import tpu as pltpu
from jax.sharding import PartitionSpec as P

courant = 0.5
f32 = jnp.float32
bf16 = jnp.bfloat16
K = 128
EXTRA = 128

NN = (((1,), (0,)), ((), ()))
NT = (((1,), (1,)), ((), ()))
TN = (((0,), (0,)), ((), ()))


def halves(x):
    high = x.astype(bf16)
    return high, (x - high.astype(f32)).astype(bf16)


def mm(a, b, dims):
    return lax.dot_general(a, b, dims, preferred_element_type=f32)


def mm3(a, b, dims):
    ah, al = a
    bh, bl = b
    return mm(ah, bh, dims) + (mm(ah, bl, dims) + mm(al, bh, dims))


def exact(a, b, dims):
    return lax.dot_general(a, b, dims, precision=lax.Precision.HIGHEST, preferred_element_type=f32)


def iota(shape, dim):
    return lax.broadcasted_iota(jnp.int32, shape, dim)


def hbm_spec():
    return pl.BlockSpec(memory_space=pltpu.HBM)


def vmem_spec():
    return pl.BlockSpec(memory_space=pltpu.VMEM)


def in_hbm(*arrays):
    return tuple(pltpu.with_memory_space_constraint(a, pltpu.HBM) for a in arrays)


def in_vmem(*arrays):
    return tuple(pltpu.with_memory_space_constraint(a, pltpu.VMEM) for a in arrays)


def cost(flops, nbytes):
    return pl.CostEstimate(flops=flops, bytes_accessed=nbytes, transcendentals=0)


def stacked(first, last, c):
    high, low = halves(jnp.concatenate([first[c, 0:1, :], last[c, 7:8, :]], axis=0))
    return jnp.concatenate([high, low], axis=0)


def two_rows(weights, field, dims):
    high, low = halves(field)
    both = mm(weights, high, dims)
    return both[0:2] + both[2:4] + mm(weights[0:2], low, dims)


def block_ends(blocks, index, first, last, sems):
    here = pl.ds(index * first.shape[0], first.shape[0])
    return [
        pltpu.make_async_copy(blocks.at[here, pl.ds(0, 8), :], first, sems.at[0]),
        pltpu.make_async_copy(blocks.at[here, pl.ds(K - 8, 8), :], last, sems.at[1]),
    ]


def ends_x_kernel(adj, depth, block_x, px_hbm, vx, first, last, drow, px, sems, row_sems, out_sems):
    rows, cols = vx.shape
    count = first.shape[0]
    small = block_ends(block_x, lax.axis_index("gx"), first, last, sems)
    small.append(pltpu.make_async_copy(depth.at[pl.ds(rows - 8, 8), :], drow, sems.at[2]))
    big = []
    for c in range(count):
        here = pl.ds(c * K, K)
        big.append(pltpu.make_async_copy(adj.at[1, here, :], vx.at[here, :], row_sems.at[c]))
    for copy in small + big:
        copy.start()
    for copy in small:
        copy.wait()
    for part in range(cols // K):
        px[part : part + 1, cols:] = drow[7:8, part * K : (part + 1) * K]
    px[cols // K :, cols:] = jnp.zeros((8 - cols // K, EXTRA), f32)
    weights = [stacked(first, last, c) for c in range(count)]
    for c in range(count):
        big[c].wait()
        px[2 * c : 2 * c + 2, :cols] = two_rows(weights[c], vx[c * K : (c + 1) * K, :], NN)
    outs = [pltpu.make_async_copy(px, px_hbm.at[d], out_sems.at[d]) for d in range(px_hbm.shape[0])]
    for copy in outs:
        copy.start()
    for copy in outs:
        copy.wait()


def ends_x(adj, depth, block_x, size_x):
    rows, cols = depth.shape
    count = block_x.shape[0] // size_x
    shape = (2 * count, cols + EXTRA)
    return pl.pallas_call(
        ends_x_kernel,
        out_shape=pltpu.HBM((size_x, *shape), f32),
        in_specs=[hbm_spec()] * 3,
        out_specs=hbm_spec(),
        scratch_shapes=[
            pltpu.VMEM((rows, cols), f32),
            pltpu.VMEM((count, 8, K), f32),
            pltpu.VMEM((count, 8, K), f32),
            pltpu.VMEM((8, cols), f32),
            pltpu.VMEM(shape, f32),
            pltpu.SemaphoreType.DMA((3,)),
            pltpu.SemaphoreType.DMA((count,)),
            pltpu.SemaphoreType.DMA((size_x,)),
        ],
        compiler_params=pltpu.CompilerParams(vmem_limit_bytes=16 << 20),
        cost_estimate=cost(2 * rows * cols * 16, 2 << 20),
        name="ends_x",
    )(*in_hbm(adj, depth, block_x))


def ends_y_kernel(adj, depth, block_y, py, vy, first, last, dcol, sems, row_sems):
    rows, cols = vy.shape
    count = first.shape[0]
    small = block_ends(block_y, lax.axis_index("gy"), first, last, sems)
    side = pltpu.make_async_copy(depth.at[:, pl.ds(cols - K, K)], dcol, sems.at[2])
    big = []
    for r in range(rows // K):
        here = pl.ds(r * K, K)
        big.append(pltpu.make_async_copy(adj.at[2, here, :], vy.at[here, :], row_sems.at[r]))
    for copy in small + big + [side]:
        copy.start()
    for copy in small:
        copy.wait()
    weights = [stacked(first, last, c) for c in range(count)]
    for r in range(rows // K):
        big[r].wait()
        for c in range(count):
            field = vy[r * K : (r + 1) * K, c * K : (c + 1) * K]
            py[2 * c : 2 * c + 2, r * K : (r + 1) * K] = two_rows(weights[c], field, NT)
    side.wait()
    at_last = (iota((8, K), 1) == K - 1).astype(f32).astype(bf16)
    high, low = halves(dcol[...])
    line = mm(at_last, high, NT) + mm(at_last, low, NT)
    for part in range(rows // K):
        py[part : part + 1, rows:] = line[0:1, part * K : (part + 1) * K]
    py[rows // K :, rows:] = jnp.zeros((8 - rows // K, EXTRA), f32)


def ends_y(adj, depth, block_y, size_y):
    rows, cols = depth.shape
    count = block_y.shape[0] // size_y
    return pl.pallas_call(
        ends_y_kernel,
        out_shape=jax.ShapeDtypeStruct((2 * count, rows + EXTRA), f32),
        in_specs=[hbm_spec()] * 3,
        out_specs=vmem_spec(),
        scratch_shapes=[
            pltpu.VMEM((rows, cols), f32),
            pltpu.VMEM((count, 8, K), f32),
            pltpu.VMEM((count, 8, K), f32),
            pltpu.VMEM((rows, K), f32),
            pltpu.SemaphoreType.DMA((3,)),
            pltpu.SemaphoreType.DMA((rows // K,)),
        ],
        compiler_params=pltpu.CompilerParams(vmem_limit_bytes=16 << 20),
        cost_estimate=cost(2 * rows * cols * 16, 2 << 20),
        name="ends_y",
    )(*in_hbm(adj, depth, block_y))


def carry_kernel(
    block_x, block_y, reduced_x_hbm, reduced_y_hbm,
    gx_hbm, gy_hbm, gside_hbm,
    gx, gy, gside, wx, wy, wpx, wpy, reduced_x, reduced_y, sems, out_sems,
):
    u = lax.axis_index("gx")
    v = lax.axis_index("gy")
    nbx = wx.shape[0]
    nby = wy.shape[0]
    before_x = jnp.maximum(u * nbx - 1, 0)
    before_y = jnp.maximum(v * nby - 1, 0)
    copies = [
        pltpu.make_async_copy(reduced_x_hbm, reduced_x, sems.at[4]),
        pltpu.make_async_copy(reduced_y_hbm, reduced_y, sems.at[5]),
        pltpu.make_async_copy(block_y.at[pl.ds(v * nby, nby)], wy, sems.at[1]),
        pltpu.make_async_copy(block_x.at[before_x, pl.ds(K - 8, 8), :], wpx, sems.at[2]),
        pltpu.make_async_copy(block_y.at[before_y, pl.ds(K - 8, 8), :], wpy, sems.at[3]),
        pltpu.make_async_copy(block_x.at[pl.ds(u * nbx, nbx)], wx, sems.at[0]),
    ]
    for copy in copies:
        copy.start()
    for copy in copies[:3]:
        copy.wait()
    own_x = reduced_x[pl.ds(pl.multiple_of(u * 8, 8), 8), :]
    own_y = reduced_y[pl.ds(pl.multiple_of(v * 8, 8), 8), :]
    prev_x = reduced_x[pl.ds(pl.multiple_of(jnp.maximum(u - 1, 0) * 8, 8), 8), :]
    prev_y = reduced_y[pl.ds(pl.multiple_of(jnp.maximum(v - 1, 0) * 8, 8), 8), :]
    row = iota((8, K), 0)
    lane = iota((8, K), 1)
    own = halves(own_y)
    for c in range(nby):
        pick = ((row == 2 * c) & (lane == 0)) | ((row == 2 * c + 1) & (lane == K - 1))
        pick = pick.astype(f32).astype(bf16)
        high, low = halves(wy[c])
        across = mm(pick, high, NT) + mm(pick, low, NT)
        gy[:, c * K : (c + 1) * K] = mm3(own, halves(across), TN)
    for copy in copies[3:]:
        copy.wait()
    for c in range(nbx):
        w = wx[c]
        gx[c * K : (c + 1) * K, :] = (
            w[:, 0:1] * own_x[2 * c : 2 * c + 1, :] + w[:, K - 1 : K] * own_x[2 * c + 1 : 2 * c + 2, :]
        )

    def side(w, prev, index):
        width = prev.shape[1]
        g = w[7:8, 0:1] * prev[6:7, :] + w[7:8, K - 1 : K] * prev[7:8, :]
        g = g + (iota((1, width), 1) == index * 8 - 1).astype(f32)
        return jnp.where(index > 0, g, 0.0)

    gside[...] = jnp.zeros(gside.shape, f32)
    gside[0:1, :] = side(wpx[...], prev_x, u)
    gside[1:2, : reduced_y.shape[1]] = side(wpy[...], prev_y, v)
    outs = [
        pltpu.make_async_copy(gx, gx_hbm, out_sems.at[0]),
        pltpu.make_async_copy(gy, gy_hbm, out_sems.at[1]),
        pltpu.make_async_copy(gside, gside_hbm, out_sems.at[2]),
    ]
    for copy in outs:
        copy.start()
    for copy in outs:
        copy.wait()


def carry(block_x, block_y, reduced_x, reduced_y, size_x, size_y):
    nbx = block_x.shape[0] // size_x
    nby = block_y.shape[0] // size_y
    results = [
        ((nbx * K, reduced_x.shape[0]), f32),
        ((reduced_y.shape[0], nby * K), f32),
        ((8, reduced_x.shape[0]), f32),
    ]
    return pl.pallas_call(
        carry_kernel,
        out_shape=tuple(pltpu.HBM(*result) for result in results),
        in_specs=[hbm_spec()] * 4,
        out_specs=(hbm_spec(),) * 3,
        scratch_shapes=[pltpu.VMEM(*result) for result in results]
        + [
            pltpu.VMEM((nbx, K, K), f32),
            pltpu.VMEM((nby, K, K), f32),
            pltpu.VMEM((8, K), f32),
            pltpu.VMEM((8, K), f32),
            pltpu.VMEM(reduced_x.shape, f32),
            pltpu.VMEM(reduced_y.shape, f32),
            pltpu.SemaphoreType.DMA((6,)),
            pltpu.SemaphoreType.DMA((3,)),
        ],
        compiler_params=pltpu.CompilerParams(vmem_limit_bytes=16 << 20),
        cost_estimate=cost(1 << 24, 2 << 20),
        name="carry",
    )(*in_hbm(block_x, block_y, reduced_x, reduced_y))


def elev_kernel(
    tx, ta_in, tb_in, gside_in, gx_in, gy_in, block_x, block_y, adj, depth, basis_in,
    wet_in, coef_in, footprint_in, owner_in,
    elev_out, fx_out, fy_out, parts_out,
    ty, gside, gx, gy, wx, wy, vx, vy, a0, dep, basis, wet, coef, footprint, owner,
    elev, fx, fy, tyn, mom, parts, sems, row_sems, out_sems,
):
    u = lax.axis_index("gx")
    v = lax.axis_index("gy")
    rows, cols = dep.shape
    steps = rows // K
    half = ta_in.shape[0]
    nbx = wx.shape[0]
    nby = wy.shape[0]
    first = [
        pltpu.make_async_copy(ta_in, ty.at[pl.ds(0, half)], sems.at[0]),
        pltpu.make_async_copy(tb_in, ty.at[pl.ds(half, half)], sems.at[1]),
        pltpu.make_async_copy(gside_in, gside, sems.at[2]),
        pltpu.make_async_copy(gy_in, gy, sems.at[3]),
        pltpu.make_async_copy(block_y.at[pl.ds(v * nby, nby)], wy, sems.at[4]),
        pltpu.make_async_copy(gx_in, gx, sems.at[5]),
        pltpu.make_async_copy(block_x.at[pl.ds(u * nbx, nbx)], wx, sems.at[6]),
        pltpu.make_async_copy(basis_in, basis, sems.at[7]),
    ]
    last = [
        pltpu.make_async_copy(wet_in, wet, sems.at[8]),
        pltpu.make_async_copy(coef_in, coef, sems.at[9]),
        pltpu.make_async_copy(footprint_in, footprint, sems.at[10]),
        pltpu.make_async_copy(owner_in, owner, sems.at[11]),
    ]
    fields = []
    for r in range(steps):
        here = pl.ds(r * K, K)
        fields.append(
            [
                pltpu.make_async_copy(adj.at[1, here, :], vx.at[here, :], row_sems.at[r, 0]),
                pltpu.make_async_copy(adj.at[2, here, :], vy.at[here, :], row_sems.at[r, 1]),
                pltpu.make_async_copy(depth.at[here, :], dep.at[here, :], row_sems.at[r, 2]),
                pltpu.make_async_copy(adj.at[0, here, :], a0.at[here, :], row_sems.at[r, 3]),
            ]
        )
    for group in [first, *fields, last]:
        for copy in group:
            copy.start()
    for copy in first:
        copy.wait()
    tx_all = jnp.concatenate([tx[d][:, :cols] for d in range(tx.shape[0])], axis=0)
    for j in range(2 * half):
        tyn[j * 8 : (j + 1) * 8, :] = ty[j ^ v]
    ty_all = tyn[:, :rows]
    txs = halves(tx_all)
    tys = halves(ty_all)
    tyt = halves(ty_all.T)
    up = jnp.maximum(u - 1, 0)
    left = jnp.maximum(v - 1, 0)
    gs = gside[...]
    edge_x = mm3(halves(gs), txs, NN)[0:1, :]
    edge_y = mm3(halves(gs[:, : ty_all.shape[0]]), tys, NN)[1:2, :]
    drow = tx[up][:, cols:]
    drow = jnp.concatenate([drow[p : p + 1, :] for p in range(cols // K)], axis=1)
    dcol = tyn[pl.ds(pl.multiple_of(left * 8, 8), 8), rows:]
    dcol = jnp.concatenate([dcol[p : p + 1, :] for p in range(rows // K)], axis=1)
    carry = edge_x * drow
    side = halves(jnp.broadcast_to(edge_y * dcol, (8, rows)))
    row = iota((K, cols), 0)
    lane = iota((K, K), 1)
    corner = ((iota((8, K), 1) == 0) & (iota((8, K), 0) == 0)).astype(f32).astype(bf16)
    modes, tile_h, tile_w = basis.shape
    per = K // tile_h
    outs = []
    firsts = []
    to_y = []
    for c in range(nby):
        wh, wl = halves(wy[c].T)
        gh, gl = halves(gy[:, c * K : (c + 1) * K])
        to_y.append((jnp.concatenate([wh, gh], axis=0), jnp.concatenate([wl, gl], axis=0)))
    for r in range(steps):
        here = slice(r * K, (r + 1) * K)
        for copy in fields[r]:
            copy.wait()
        d = dep[here, :]
        wh, wl = halves(wx[r])
        gh, gl = halves(gx[here, :])
        vh, vl = halves(vx[here, :])
        flux_x = mm3(
            (jnp.concatenate([wh, gh], axis=1), jnp.concatenate([wl, gl], axis=1)),
            (jnp.concatenate([vh, txs[0]], axis=0), jnp.concatenate([vl, txs[1]], axis=0)),
            NN,
        )
        pieces = []
        for c in range(nby):
            vh, vl = halves(vy[here, c * K : (c + 1) * K])
            lhs = (
                jnp.concatenate([vh, tyt[0][here, :]], axis=1),
                jnp.concatenate([vl, tyt[1][here, :]], axis=1),
            )
            pieces.append(mm3(lhs, to_y[c], NN))
        flux_y = jnp.concatenate(pieces, axis=1)
        fx[here, :] = flux_x
        fy[here, :] = flux_y
        weighted_x = d * flux_x
        weighted_y = d * flux_y
        before_x = jnp.where(row == 0, carry, pltpu.roll(weighted_x, 1, 0))
        carry = weighted_x[K - 1 : K, :]
        edge = mm(side[0][:, here], corner, TN) + mm(side[1][:, here], corner, TN)
        turned = [edge] + [
            pltpu.roll(weighted_y[:, c * K : (c + 1) * K], 1, 1) for c in range(cols // K)
        ]
        before_y = jnp.concatenate(
            [jnp.where(lane == 0, turned[c], turned[c + 1]) for c in range(cols // K)], axis=1
        )
        e = a0[here, :] + courant * ((weighted_x - before_x) + (weighted_y - before_y))
        elev[here, :] = e
        where = pl.ds(r * K, K)
        for i, (source, target) in enumerate(((elev, elev_out), (fx, fx_out), (fy, fy_out))):
            copy = pltpu.make_async_copy(source.at[where, :], target.at[where, :], out_sems.at[r, i])
            copy.start()
            outs.append(copy)
        if r == 0:
            top = e[0:1, :]
        eh, el = halves(e[:, :K])
        firsts.append((mm(corner, eh, NT) + mm(corner, el, NT))[0:1, :])
        for a in range(per):
            for w in range(cols // tile_w):
                tile = e[a * tile_h : (a + 1) * tile_h, w * tile_w : (w + 1) * tile_w]
                for b in range(modes):
                    at = b * (rows // tile_h) + r * per + a
                    mom[at : at + 1, w * tile_w : (w + 1) * tile_w] = jnp.sum(
                        tile * basis[b], axis=0, keepdims=True
                    )
    for copy in last:
        copy.wait()
    tiles_y, tiles_x = wet.shape
    count = footprint.shape[1]
    places = footprint.shape[0]
    ones = jnp.ones((8, tile_w), bf16)
    pieces = []
    for w in range(tiles_y):
        high, low = halves(mom[:, w * tile_w : (w + 1) * tile_w])
        line = (mm(ones, high, NT) + mm(ones, low, NT))[0:1, :]
        keep = wet[w : w + 1, :].astype(f32)
        for b in range(modes):
            pieces.append(line[:, b * tiles_x : (b + 1) * tiles_x] * keep)
    high, low = halves(jnp.concatenate(pieces, axis=0))
    table = jnp.concatenate([high, low], axis=0)
    number = footprint[...]
    total_cols = tiles_y * lax.axis_size("gy")
    local_row = lax.shift_right_logical(number, total_cols.bit_length() - 1) - u * tiles_x
    local_col = (number & (total_cols - 1)) - v * tiles_y
    lines = tiles_y * modes
    tile_row = iota((tiles_x, count), 0)
    tile_col = lax.shift_right_logical(iota((lines, count), 0), modes.bit_length() - 1)
    acc = jnp.zeros((lines, count), f32)
    for f in range(places):
        at_row = (tile_row == local_row[f : f + 1, :]).astype(f32).astype(bf16)
        both = mm(table, at_row, NN)
        four = coef[f]
        scale = jnp.concatenate([four] * tiles_y, axis=0)
        hit = tile_col == local_col[f : f + 1, :]
        acc = acc + jnp.where(hit, (both[:lines] + both[lines:]) * scale, 0.0)
    total = jnp.sum(acc, axis=0, keepdims=True)
    devices = parts.shape[0] // 5
    slots = count // devices
    own = owner[...]
    slot_of = (iota((slots, count), 0) == (own & (slots - 1))).astype(f32)
    device_of = iota((devices, count), 0) == lax.shift_right_logical(own, slots.bit_length() - 1)
    device_of = device_of.astype(f32).astype(bf16)
    high, low = halves(slot_of * total)
    sums = mm(device_of, high, NT) + mm(device_of, low, NT)
    parts[...] = jnp.zeros(parts.shape, f32)
    parts[pl.ds(0, devices, stride=5), :] = jnp.concatenate(
        [sums, jnp.zeros((devices, K - slots), f32)], axis=1
    )
    size_y = lax.axis_size("gy")

    def put(device, line):
        for p in range(4):
            parts[pl.ds(device * 5 + 1 + p, 1), :] = line[:, p * K : (p + 1) * K]

    @pl.when(u > 0)
    def _():
        put((u - 1) * size_y + v, top)

    @pl.when(v > 0)
    def _():
        put(u * size_y + v - 1, jnp.concatenate(firsts, axis=1))

    outs.append(pltpu.make_async_copy(parts, parts_out, sems.at[12]))
    outs[-1].start()
    for copy in outs:
        copy.wait()


def elevation(tx, ta, tb, gx, gy, gside, block_x, block_y, adj, depth, basis, wet, coef, footprint, owner):
    rows, cols = depth.shape
    modes, tile_h, tile_w = basis.shape
    devices = lax.axis_size("gx") * lax.axis_size("gy")
    steps = rows // K
    wet = wet.T
    coef = coef.transpose(1, 2, 0)
    footprint = footprint.T
    owner = owner.reshape(1, -1)
    field = ((rows, cols), f32)
    far = (2 * ta.shape[0], 8, rows + EXTRA)
    parts = ((devices * 5, K), f32)
    like = lambda *arrays: [pltpu.VMEM(a.shape, a.dtype) for a in arrays]
    return pl.pallas_call(
        elev_kernel,
        out_shape=(pltpu.HBM(*field),) * 3 + (pltpu.HBM(*parts),),
        in_specs=[vmem_spec()] + [pl.BlockSpec(memory_space=pl.ANY)] * 2 + [hbm_spec()] * 12,
        out_specs=(hbm_spec(),) * 4,
        scratch_shapes=[pltpu.VMEM(far, f32)]
        + like(gside, gx, gy)
        + [pltpu.VMEM((rows // K, K, K), f32), pltpu.VMEM((cols // K, K, K), f32)]
        + [pltpu.VMEM(*field)] * 4
        + like(basis, wet, coef, footprint, owner)
        + [pltpu.VMEM(*field)] * 3
        + [
            pltpu.VMEM((far[0] * 8, far[2]), f32),
            pltpu.VMEM((rows // tile_h * modes, cols), f32),
            pltpu.VMEM(*parts),
            pltpu.SemaphoreType.DMA((13,)),
            pltpu.SemaphoreType.DMA((steps, 4)),
            pltpu.SemaphoreType.DMA((steps, 3)),
        ],
        compiler_params=pltpu.CompilerParams(vmem_limit_bytes=32 << 20),
        cost_estimate=cost(12 * rows * cols * K, 10 << 20),
        name="elevation",
    )(
        tx,
        ta,
        tb,
        *in_hbm(gside, gx, gy, block_x, block_y, adj, depth, basis, wet, coef, footprint, owner),
    )


def fluxes_kernel(elev_in, fx_in, fy_in, out, e, x, y, sems, out_sems):
    rows, cols = e.shape
    steps = rows // K
    reads = []
    for r in range(steps):
        here = pl.ds(r * K, K)
        pairs = ((elev_in, e), (fx_in, x), (fy_in, y))
        reads.append(
            [
                pltpu.make_async_copy(source.at[here, :], target.at[here, :], sems.at[r, i])
                for i, (source, target) in enumerate(pairs)
            ]
        )
    for group in reads:
        for copy in group:
            copy.start()
    row = iota((K, cols), 0)
    lane = iota((K, cols), 1)
    writes = []
    for copy in reads[0]:
        copy.wait()
    for r in range(steps):
        here = slice(r * K, (r + 1) * K)
        after = 0.0
        if r + 1 < steps:
            for copy in reads[r + 1]:
                copy.wait()
            after = e[(r + 1) * K : (r + 1) * K + 1, :]
        now = e[here, :]
        below = jnp.where(row == K - 1, after, pltpu.roll(now, K - 1, 0))
        right = jnp.where(lane == cols - 1, 0.0, pltpu.roll(now, cols - 1, 1))
        x[here, :] = x[here, :] + courant * (below - now)
        y[here, :] = y[here, :] + courant * (right - now)
        where = pl.ds(r * K, K)
        for i, source in enumerate((e, x, y)):
            copy = pltpu.make_async_copy(source.at[where, :], out.at[i, where, :], out_sems.at[r, i])
            copy.start()
            writes.append(copy)
    for copy in writes:
        copy.wait()


def fluxes(elev, fx, fy):
    rows, cols = elev.shape
    return pl.pallas_call(
        fluxes_kernel,
        out_shape=pltpu.HBM((3, rows, cols), f32),
        in_specs=[hbm_spec()] * 3,
        out_specs=hbm_spec(),
        scratch_shapes=[
            pltpu.VMEM((rows, cols), f32),
            pltpu.VMEM((rows, cols), f32),
            pltpu.VMEM((rows, cols), f32),
            pltpu.SemaphoreType.DMA((rows // K, 3)),
            pltpu.SemaphoreType.DMA((rows // K, 3)),
        ],
        compiler_params=pltpu.CompilerParams(vmem_limit_bytes=16 << 20),
        cost_estimate=cost(10 * rows * cols, 6 << 20),
        name="fluxes",
    )(*in_hbm(elev, fx, fy))


def finish_kernel(fields_in, sums, fields, grad, bottom, edge, sems, out_sems):
    u = lax.axis_index("gx")
    v = lax.axis_index("gy")
    size_x = lax.axis_size("gx")
    size_y = lax.axis_size("gy")
    rows, cols = fields.shape[1:]
    reads = [
        pltpu.make_async_copy(fields.at[1, pl.ds(rows - 8, 8), :], bottom, sems.at[0]),
        pltpu.make_async_copy(fields.at[2, :, pl.ds(cols - K, K)], edge, sems.at[1]),
    ]
    for copy in reads:
        copy.start()

    def line(device):
        return jnp.concatenate([sums[pl.ds(device * 5 + 1 + p, 1), :] for p in range(4)], axis=1)

    below = line(jnp.minimum(u + 1, size_x - 1) * size_y + v) * jnp.where(u + 1 < size_x, courant, 0.0)
    right = line(u * size_y + jnp.minimum(v + 1, size_y - 1)) * jnp.where(v + 1 < size_y, courant, 0.0)
    devices = sums.shape[0] // 5
    total = jnp.sum(sums[pl.ds(0, devices, stride=5), :], axis=0, keepdims=True)
    grad[...] = total[:, : grad.shape[1]]
    corner = ((iota((8, K), 1) == K - 1) & (iota((8, K), 0) == 0)).astype(f32).astype(bf16)
    high, low = halves(jnp.broadcast_to(right, (8, rows)))
    for copy in reads:
        copy.wait()
    bottom[7:8, :] = bottom[7:8, :] + below
    edge[...] = edge[...] + (mm(high, corner, TN) + mm(low, corner, TN))
    writes = [
        pltpu.make_async_copy(bottom, fields.at[1, pl.ds(rows - 8, 8), :], out_sems.at[0]),
        pltpu.make_async_copy(edge, fields.at[2, :, pl.ds(cols - K, K)], out_sems.at[1]),
    ]
    for copy in writes:
        copy.start()
    for copy in writes:
        copy.wait()


def finish(fields, sums, slots):
    _, rows, cols = fields.shape
    return pl.pallas_call(
        finish_kernel,
        out_shape=(pltpu.HBM(fields.shape, f32), jax.ShapeDtypeStruct((1, slots), f32)),
        in_specs=[hbm_spec(), vmem_spec()],
        out_specs=(hbm_spec(), vmem_spec()),
        input_output_aliases={0: 0},
        scratch_shapes=[
            pltpu.VMEM((8, cols), f32),
            pltpu.VMEM((rows, K), f32),
            pltpu.SemaphoreType.DMA((2,)),
            pltpu.SemaphoreType.DMA((2,)),
        ],
        compiler_params=pltpu.CompilerParams(vmem_limit_bytes=16 << 20),
        cost_estimate=cost(1 << 20, 1 << 20),
        name="finish",
    )(*in_hbm(fields), sums)


def partner(axis, bit):
    return [(i, i ^ bit) for i in range(lax.axis_size(axis))]


def body(
    adj_fields, depth, block_x, reduced_x, block_y, reduced_y, basis, coef, footprint, owner, wet
):
    size_x = lax.axis_size("gx")
    size_y = lax.axis_size("gy")
    ty = ends_y(adj_fields, depth, block_y, size_y)[None]
    px = ends_x(adj_fields, depth, block_x, size_x)
    tx = lax.all_to_all(px, "gx", split_axis=0, concat_axis=0, tiled=True)
    bit = 1
    while 2 * bit < size_y:
        ty = jnp.concatenate([ty, lax.ppermute(ty, "gy", partner("gy", bit))], axis=0)
        bit *= 2
    ty_far = lax.ppermute(ty, "gy", partner("gy", bit))
    carried = carry(block_x, block_y, reduced_x, reduced_y, size_x, size_y)
    elev, fx, fy, parts = elevation(
        tx, ty, ty_far, *carried, block_x, block_y, adj_fields, depth, basis, wet, coef, footprint, owner
    )
    devices = size_x * size_y
    sums = lax.all_to_all(
        parts[:, None, :], ("gx", "gy"), split_axis=0, concat_axis=0, tiled=True
    )
    slots = owner.shape[0] // devices
    adj_before, grad = finish(fluxes(elev, fx, fy), sums[:, 0, :], slots)
    return adj_before, grad.reshape(slots)


def solution(mesh):
    in_specs = (
        P(None, "gx", "gy"),
        P("gx", "gy"),
        P(),
        P(),
        P(),
        P(),
        P(),
        P(),
        P(),
        P(),
        P("gx", "gy"),
    )
    out_specs = (P(None, "gx", "gy"), P(("gx", "gy")))
    return jax.shard_map(body, mesh=mesh, in_specs=in_specs, out_specs=out_specs, check_vma=False)
```

time: 60.8 us -> 56.8 us (0.934)
  Pallas kernels: 24.9 us -> 21.4 us
  starting transfers between devices: 22.4 us -> 24.2 us
  waiting for transfers between devices: 11.9 us -> 10.1 us
    pallas_call x3, Pallas kernels: 12.5 us -> 7.61 us  [the longest x1 2.87 us: carry(): pl.pallas_call(carry_kernel, out_shape=tuple((pltpu.HBM(*result) for resu...]
    all_to_all x1, waiting for transfers between devices: 10.3 us -> 8.35 us  [body(): lax.all_to_all(parts[:, None, :], ('gx', 'gy'), split_axis=0, concat_axis...]
    all_to_all x1, starting transfers between devices: 8.93 us -> 10.7 us  [body(): lax.all_to_all(parts[:, None, :], ('gx', 'gy'), split_axis=0, concat_axis...]
    pallas_call x1, Pallas kernels: 7.2 us -> 8.1 us  [elevation(): pl.pallas_call(elev_kernel, out_shape=(pltpu.HBM(*field),) * 3 + (pltpu.H...]
  transfers between devices with their start and end apart: 5 -> 5, of which waited for: 2 -> 3; matrix products, arithmetic and copies ran while one was open for 0% -> 0% of each run, Pallas kernels for 21% -> 15%
where the time goes in v3:
time: 56.8 us; the launch traced here: 56.4 us
  starting transfers between devices  24.2 us (43%)
  Pallas kernels  21.4 us (38%)
  waiting for transfers between devices  10.1 us (18%)
  between operations  0.71 us (1%)
    all_to_all x1, starting transfers between devices, body(): lax.all_to_all(parts[:, None, :], ('gx', 'gy'), split_axis=0, concat_axis...  10.7 us
    all_to_all x1, waiting for transfers between devices, body(): lax.all_to_all(parts[:, None, :], ('gx', 'gy'), split_axis=0, concat_axis...  8.35 us
    pallas_call x1, Pallas kernels, elevation(): pl.pallas_call(elev_kernel, out_shape=(pltpu.HBM(*field),) * 3 + (pltpu.H...  8.1 us
    all_to_all x1, starting transfers between devices, body(): tx = lax.all_to_all(px, 'gx', split_axis=0, concat_axis=0, tiled=True)  7.69 us
    pallas_call x1, Pallas kernels, fluxes(): pl.pallas_call(fluxes_kernel, out_shape=pltpu.HBM((3, rows, cols), f32),...  3.2 us
    ppermute x1, starting transfers between devices, body(): ty_far = lax.ppermute(ty, 'gy', partner('gy', bit))  2.91 us
    ppermute x2, starting transfers between devices, body(): lax.ppermute(ty, 'gy', partner('gy', bit))  2.88 us
    pallas_call x1, Pallas kernels, carry(): pl.pallas_call(carry_kernel, out_shape=tuple((pltpu.HBM(*result) for resu...  2.87 us
  transfers between devices with their start and end apart: 5, of which 3 were waited for; matrix products, arithmetic and copies ran while one was open for 0% of the time, Pallas kernels for 15%

profile of v3, /device:TPU:1, one launch (start us, length us, event | category | flops | bytes accessed | tf_op | source)
XLA Modules:
  0.0 56.4 jit_solution(4111457704542532769)
XLA Ops:
  0.6 2.2 %ends_y.1 = f32[8,640]{1,0:T(8,128)S(1)} custom-call(f32[3,512,512]{2,1,0:T(8,128)} %adj.5, f32[512,512]{1,0:T(8,128)} %depth.5, f32[32,128,128]{2,1,0:T(8,128)} %block_y.5), custom_call_target="tpu_custom_call" | custom-call | flops 8388608 | bytes 2097152 | tf_op jit(solution)/shard_map/ends_y/pallas_call | solution.py:164
  2.9 1.5 %collective-permute-start = (f32[1,8,640]{2,1,0:T(8,128)S(1)}, f32[1,8,640]{2,1,0:T(8,128)S(1)}, u32[]{:S(2)}, u32[]{:S(2)}) collective-permute-start(f32[1,8,640]{2,1,0:T(8,128)S(1)} %bitcast.11), channel_id=1, source_target_pairs={{0,1},{1,0},{2,3},{3,2},{4,5},{5,4},{6,7},{7,6},{8,9},{9,8},{10,11... | collective-permute-start | bytes 61448 | tf_op jit(solution)/shard_map/ppermute | solution.py:646
  4.4 2.5 %ends_x.1 = f32[16,8,640]{2,1,0:T(8,128)} custom-call(f32[3,512,512]{2,1,0:T(8,128)} %adj.5, f32[512,512]{1,0:T(8,128)} %depth.5, f32[64,128,128]{2,1,0:T(8,128)} %block_x.5), custom_call_target="tpu_custom_call" | custom-call | flops 8388608 | bytes 2097152 | tf_op jit(solution)/shard_map/ends_x/pallas_call | solution.py:112
  6.9 7.7 %all-to-all-start = ((f32[16,8,640]{2,1,0:T(8,128)}), f32[16,8,640]{2,1,0:T(8,128)S(1)}, u32[]{:S(2)}, u32[]{:S(2)}) async-start(f32[16,8,640]{2,1,0:T(8,128)} %ends_x.1), calls=%async_computation | async-start | bytes 655360 | tf_op jit(solution)/shard_map/all_to_all | solution.py:643
  14.6 0.0 collective-permute-done
  14.6 1.4 %collective-permute-start.1 = (f32[2,8,640]{2,1,0:T(8,128)S(1)}, f32[2,8,640]{2,1,0:T(8,128)S(1)}, u32[]{:S(2)}, u32[]{:S(2)}) collective-permute-start(f32[2,8,640]{2,1,0:T(8,128)S(1)} %pad_maximum_fusion.1), channel_id=1, source_target_pairs={{0,2},{1,3},{2,0},{3,1},{4,6},{5,7},{6,4},{7,5},{8,10},{9,11},{10,... | collective-permute-start | bytes 122888 | tf_op jit(solution)/shard_map/ppermute | solution.py:646
  16.0 1.6 %collective-permute-done.1 = f32[2,8,640]{2,1,0:T(8,128)S(1)} collective-permute-done((f32[2,8,640]{2,1,0:T(8,128)S(1)}, f32[2,8,640]{2,1,0:T(8,128)S(1)}, u32[]{:S(2)}, u32[]{:S(2)}) %collective-permute-start.1) | collective-permute-done | bytes 40992 | tf_op jit(solution)/shard_map/ppermute | solution.py:646
  17.6 2.9 %collective-permute-start.2 = (f32[4,8,640]{2,1,0:T(8,128)S(1)}, f32[4,8,640]{2,1,0:T(8,128)S(1)}, u32[]{:S(2)}, u32[]{:S(2)}) collective-permute-start(f32[4,8,640]{2,1,0:T(8,128)S(1)} %pad_maximum_fusion.ta_in), channel_id=1, source_target_pairs={{0,4},{1,5},{2,6},{3,7},{4,0},{5,1},{6,2},{7,3},{8,12},{9,13},{10,... | collective-permute-start | bytes 245768 | tf_op jit(solution)/shard_map/ppermute | solution.py:648
  20.5 2.9 %carry.1 = (f32[512,128]{1,0:T(8,128)}, f32[64,512]{1,0:T(8,128)}, f32[8,128]{1,0:T(8,128)}) custom-call(f32[64,128,128]{2,1,0:T(8,128)} %block_x.5, f32[32,128,128]{2,1,0:T(8,128)} %block_y.5, f32[128,128]{1,0:T(8,128)} %reduced_x_hbm.1, f32[64,64]{1,0:T(8,128)} %reduced_y_hbm.1), custom_call_target="tpu_custom_call" | custom-call | flops 16777216 | bytes 2097152 | tf_op jit(solution)/shard_map/carry/pallas_call | solution.py:255
  23.3 0.0 collective-permute-done.2.tb_in
  23.4 0.2 all-to-all-done.tx
  23.6 8.1 %elevation.1 = (f32[512,512]{1,0:T(8,128)}, f32[512,512]{1,0:T(8,128)}, f32[512,512]{1,0:T(8,128)}, f32[640,128]{1,0:T(8,128)}) custom-call(f32[16,8,640]{2,1,0:T(8,128)S(1)} %all-to-all-done.tx, f32[4,8,640]{2,1,0:T(8,128)S(1)} %pad_maximum_fusion.ta_in, f32[4,8,640]{2,1,0:T(8,128)S(1)} %collective-permute-done.2.tb_in, ...), custom_call_target="tpu_custom_call" | custom-call | flops 402653184 | bytes 10485760 | tf_op jit(solution)/shard_map/elevation/pallas_call | solution.py:483
  31.7 10.7 %all-to-all-start.1 = ((f32[640,1,128]{2,1,0:T(1,128)}), f32[640,1,128]{2,1,0:T(1,128)S(1)}, u32[]{:S(2)}, u32[]{:S(2)}) async-start(f32[640,1,128]{2,1,0:T(1,128)} %bitcast.14), calls=%async_computation.1 | async-start | bytes 655360 | tf_op jit(solution)/shard_map/all_to_all | solution.py:654
  42.4 3.2 %fluxes.1.fields_in = f32[3,512,512]{2,1,0:T(8,128)} custom-call(f32[512,512]{1,0:T(8,128)} %get-tuple-element.14.elev_in, f32[512,512]{1,0:T(8,128)} %get-tuple-element.15.fx_in, f32[512,512]{1,0:T(8,128)} %get-tuple-element.16.fy_in), custom_call_target="tpu_custom_call" | custom-call | flops 2621440 | bytes 6291456 | tf_op jit(solution)/shard_map/fluxes/pallas_call | solution.py:557
  45.6 8.4 %all-to-all-done.1 = f32[640,1,128]{2,1,0:T(1,128)S(1)} async-done(((f32[640,1,128]{2,1,0:T(1,128)}), f32[640,1,128]{2,1,0:T(1,128)S(1)}, u32[]{:S(2)}, u32[]{:S(2)}) %all-to-all-start.1) | async-done | bytes 327712 | tf_op jit(solution)/shard_map/all_to_all | solution.py:654
  54.0 2.5 %finish.1 = (f32[3,512,512]{2,1,0:T(8,128)}, f32[1,16]{1,0:T(1,128)}) custom-call(f32[3,512,512]{2,1,0:T(8,128)} %fluxes.1.fields_in, f32[640,128]{1,0:T(8,128)S(1)} %bitcast.10), custom_call_target="tpu_custom_call", output_to_operand_aliasing={{0}: (0, {})} | custom-call | flops 1048576 | bytes 1048576 | tf_op jit(solution)/shard_map/finish/pallas_call | solution.py:614
  (2 shorter events, 0.0 us)
Async XLA Ops:
  2.9 11.7 %collective-permute-start = (f32[1,8,640]{2,1,0:T(8,128)S(1)}, f32[1,8,640]{2,1,0:T(8,128)S(1)}, u32[]{:S(2)}, u32[]{:S(2)}) collective-permute-start(f32[1,8,640]{2,1,0:T(8,128)S(1)} %bitcast.11), channel_id=1, source_target_pairs={{0,1},{1,0},{2,3},{3,2},{4,5},{5,4},{6,7},{7,6},{8,9},{9,8},{10,11... | collective-permute-start | bytes 61448 | tf_op jit(solution)/shard_map/ppermute | solution.py:646
  6.9 16.7 %all-to-all-start = ((f32[16,8,640]{2,1,0:T(8,128)}), f32[16,8,640]{2,1,0:T(8,128)S(1)}, u32[]{:S(2)}, u32[]{:S(2)}) async-start(f32[16,8,640]{2,1,0:T(8,128)} %ends_x.1), calls=%async_computation | async-start | bytes 655360 | tf_op jit(solution)/shard_map/all_to_all | solution.py:643
  14.6 2.9 %collective-permute-start.1 = (f32[2,8,640]{2,1,0:T(8,128)S(1)}, f32[2,8,640]{2,1,0:T(8,128)S(1)}, u32[]{:S(2)}, u32[]{:S(2)}) collective-permute-start(f32[2,8,640]{2,1,0:T(8,128)S(1)} %pad_maximum_fusion.1), channel_id=1, source_target_pairs={{0,2},{1,3},{2,0},{3,1},{4,6},{5,7},{6,4},{7,5},{8,10},{9,11},{10,... | collective-permute-start | bytes 122888 | tf_op jit(solution)/shard_map/ppermute | solution.py:646
  17.6 5.8 %collective-permute-start.2 = (f32[4,8,640]{2,1,0:T(8,128)S(1)}, f32[4,8,640]{2,1,0:T(8,128)S(1)}, u32[]{:S(2)}, u32[]{:S(2)}) collective-permute-start(f32[4,8,640]{2,1,0:T(8,128)S(1)} %pad_maximum_fusion.ta_in), channel_id=1, source_target_pairs={{0,4},{1,5},{2,6},{3,7},{4,0},{5,1},{6,2},{7,3},{8,12},{9,13},{10,... | collective-permute-start | bytes 245768 | tf_op jit(solution)/shard_map/ppermute | solution.py:648
  31.7 22.3 %all-to-all-start.1 = ((f32[640,1,128]{2,1,0:T(1,128)}), f32[640,1,128]{2,1,0:T(1,128)S(1)}, u32[]{:S(2)}, u32[]{:S(2)}) async-start(f32[640,1,128]{2,1,0:T(1,128)} %bitcast.14), calls=%async_computation.1 | async-start | bytes 655360 | tf_op jit(solution)/shard_map/all_to_all | solution.py:654

commit v4 on v3

--- a/solution.py
+++ b/solution.py
@@ -269,7 +269,7 @@
             pltpu.SemaphoreType.DMA((3,)),
         ],
         compiler_params=pltpu.CompilerParams(vmem_limit_bytes=16 << 20),
-        cost_estimate=cost(1 << 24, 2 << 20),
+        cost_estimate=cost(1 << 36, 2 << 20),
         name="carry",
     )(*in_hbm(block_x, block_y, reduced_x, reduced_y))
 
@@ -278,7 +278,7 @@
     tx, ta_in, tb_in, gside_in, gx_in, gy_in, block_x, block_y, adj, depth, basis_in,
     wet_in, coef_in, footprint_in, owner_in,
     elev_out, fx_out, fy_out, parts_out,
-    ty, gside, gx, gy, wx, wy, vx, vy, a0, dep, basis, wet, coef, footprint, owner,
+    ty, gside, gx, gy, wx, wy, planes, dep, basis, wet, coef, footprint, owner,
     elev, fx, fy, tyn, mom, parts, sems, row_sems, out_sems,
 ):
     u = lax.axis_index("gx")
@@ -309,10 +309,8 @@
         here = pl.ds(r * K, K)
         fields.append(
             [
-                pltpu.make_async_copy(adj.at[1, here, :], vx.at[here, :], row_sems.at[r, 0]),
-                pltpu.make_async_copy(adj.at[2, here, :], vy.at[here, :], row_sems.at[r, 1]),
-                pltpu.make_async_copy(depth.at[here, :], dep.at[here, :], row_sems.at[r, 2]),
-                pltpu.make_async_copy(adj.at[0, here, :], a0.at[here, :], row_sems.at[r, 3]),
+                pltpu.make_async_copy(adj.at[:, here, :], planes.at[:, here, :], row_sems.at[r, 0]),
+                pltpu.make_async_copy(depth.at[here, :], dep.at[here, :], row_sems.at[r, 1]),
             ]
         )
     for group in [first, *fields, last]:
@@ -352,12 +350,13 @@
         to_y.append((jnp.concatenate([wh, gh], axis=0), jnp.concatenate([wl, gl], axis=0)))
     for r in range(steps):
         here = slice(r * K, (r + 1) * K)
-        for copy in fields[r]:
-            copy.wait()
+        if r % 2 == 0:
+            for copy in fields[r] + fields[r + 1]:
+                copy.wait()
         d = dep[here, :]
         wh, wl = halves(wx[r])
         gh, gl = halves(gx[here, :])
-        vh, vl = halves(vx[here, :])
+        vh, vl = halves(planes[1, here, :])
         flux_x = mm3(
             (jnp.concatenate([wh, gh], axis=1), jnp.concatenate([wl, gl], axis=1)),
             (jnp.concatenate([vh, txs[0]], axis=0), jnp.concatenate([vl, txs[1]], axis=0)),
@@ -365,7 +364,7 @@
         )
         pieces = []
         for c in range(nby):
-            vh, vl = halves(vy[here, c * K : (c + 1) * K])
+            vh, vl = halves(planes[2, here, c * K : (c + 1) * K])
             lhs = (
                 jnp.concatenate([vh, tyt[0][here, :]], axis=1),
                 jnp.concatenate([vl, tyt[1][here, :]], axis=1),
@@ -385,7 +384,7 @@
         before_y = jnp.concatenate(
             [jnp.where(lane == 0, turned[c], turned[c + 1]) for c in range(cols // K)], axis=1
         )
-        e = a0[here, :] + courant * ((weighted_x - before_x) + (weighted_y - before_y))
+        e = planes[0, here, :] + courant * ((weighted_x - before_x) + (weighted_y - before_y))
         elev[here, :] = e
         where = pl.ds(r * K, K)
         for i, (source, target) in enumerate(((elev, elev_out), (fx, fx_out), (fy, fy_out))):
@@ -488,7 +487,7 @@
         scratch_shapes=[pltpu.VMEM(far, f32)]
         + like(gside, gx, gy)
         + [pltpu.VMEM((rows // K, K, K), f32), pltpu.VMEM((cols // K, K, K), f32)]
-        + [pltpu.VMEM(*field)] * 4
+        + [pltpu.VMEM((3, rows, cols), f32), pltpu.VMEM(*field)]
         + like(basis, wet, coef, footprint, owner)
         + [pltpu.VMEM(*field)] * 3
         + [
@@ -496,7 +495,7 @@
             pltpu.VMEM((rows // tile_h * modes, cols), f32),
             pltpu.VMEM(*parts),
             pltpu.SemaphoreType.DMA((13,)),
-            pltpu.SemaphoreType.DMA((steps, 4)),
+            pltpu.SemaphoreType.DMA((steps, 2)),
             pltpu.SemaphoreType.DMA((steps, 3)),
         ],
         compiler_params=pltpu.CompilerParams(vmem_limit_bytes=32 << 20),
@@ -640,12 +639,14 @@
     size_y = lax.axis_size("gy")
     ty = ends_y(adj_fields, depth, block_y, size_y)[None]
     px = ends_x(adj_fields, depth, block_x, size_x)
-    tx = lax.all_to_all(px, "gx", split_axis=0, concat_axis=0, tiled=True)
-    bit = 1
+    ty = jnp.concatenate([ty, lax.ppermute(ty, "gy", partner("gy", 1))], axis=0)
+    px, ty = lax.optimization_barrier((px, ty))
+    bit = 2
     while 2 * bit < size_y:
         ty = jnp.concatenate([ty, lax.ppermute(ty, "gy", partner("gy", bit))], axis=0)
         bit *= 2
     ty_far = lax.ppermute(ty, "gy", partner("gy", bit))
+    tx = lax.all_to_all(px, "gx", split_axis=0, concat_axis=0, tiled=True)
     carried = carry(block_x, block_y, reduced_x, reduced_y, size_x, size_y)
     elev, fx, fy, parts = elevation(
         tx, ty, ty_far, *carried, block_x, block_y, adj_fields, depth, basis, wet, coef, footprint, owner

time: 56.8 us -> 53.3 us (0.938)
  starting transfers between devices: 24.2 us -> 20.1 us
  waiting for transfers between devices: 10.1 us -> 11.6 us
  Pallas kernels: 21.4 us -> 20.5 us
    all_to_all x1, starting transfers between devices: 10.7 us -> 6.8 us  [body(): lax.all_to_all(parts[:, None, :], ('gx', 'gy'), split_axis=0, concat_axis...]
    all_to_all x1, waiting for transfers between devices: 0.21 us -> 3.28 us  [body(): tx = lax.all_to_all(px, 'gx', split_axis=0, concat_axis=0, tiled=True)]
    ppermute x2 -> x1, waiting for transfers between devices: 1.56 us -> 0.01 us  [body(): lax.ppermute(ty, 'gy', partner('gy', bit))]
    ppermute x0 -> x1, starting transfers between devices: none -> 1.5 us  [body(): ty = jnp.concatenate([ty, lax.ppermute(ty, 'gy', partner('gy', 1))], axis=0)]
    ppermute x2 -> x1, starting transfers between devices: 2.88 us -> 1.46 us  [body(): lax.ppermute(ty, 'gy', partner('gy', bit))]
    pallas_call x1, Pallas kernels: 8.1 us -> 7.27 us  [elevation(): pl.pallas_call(elev_kernel, out_shape=(pltpu.HBM(*field),) * 3 + (pltpu.H...]
  transfers between devices with their start and end apart: 5 -> 5, of which waited for: 3 -> 2; matrix products, arithmetic and copies ran while one was open for 0% -> 0% of each run, Pallas kernels for 15% -> 16%
where the time goes in v4:
time: 53.3 us; the launch traced here: 53 us
  Pallas kernels  20.5 us (38%)
  starting transfers between devices  20.1 us (38%)
  waiting for transfers between devices  11.6 us (22%)
  between operations  0.73 us (1%)
    all_to_all x1, waiting for transfers between devices, body(): lax.all_to_all(parts[:, None, :], ('gx', 'gy'), split_axis=0, concat_axis...  8.35 us
    all_to_all x1, starting transfers between devices, body(): tx = lax.all_to_all(px, 'gx', split_axis=0, concat_axis=0, tiled=True)  7.6 us
    pallas_call x1, Pallas kernels, elevation(): pl.pallas_call(elev_kernel, out_shape=(pltpu.HBM(*field),) * 3 + (pltpu.H...  7.27 us
    all_to_all x1, starting transfers between devices, body(): lax.all_to_all(parts[:, None, :], ('gx', 'gy'), split_axis=0, concat_axis...  6.8 us
    all_to_all x1, waiting for transfers between devices, body(): tx = lax.all_to_all(px, 'gx', split_axis=0, concat_axis=0, tiled=True)  3.28 us
    pallas_call x1, Pallas kernels, fluxes(): pl.pallas_call(fluxes_kernel, out_shape=pltpu.HBM((3, rows, cols), f32),...  3.2 us
    pallas_call x1, Pallas kernels, carry(): pl.pallas_call(carry_kernel, out_shape=tuple((pltpu.HBM(*result) for resu...  2.87 us
    ppermute x1, starting transfers between devices, body(): ty_far = lax.ppermute(ty, 'gy', partner('gy', bit))  2.7 us
  transfers between devices with their start and end apart: 5, of which 2 were waited for; matrix products, arithmetic and copies ran while one was open for 0% of the time, Pallas kernels for 16%

profile of v4, /device:TPU:1, one launch (start us, length us, event | category | flops | bytes accessed | tf_op | source)
XLA Modules:
  0.0 53.0 jit_solution(5634268577907271823)
XLA Ops:
  0.6 2.2 %ends_y.1 = f32[8,640]{1,0:T(8,128)S(1)} custom-call(f32[3,512,512]{2,1,0:T(8,128)} %adj.5, f32[512,512]{1,0:T(8,128)} %depth.5, f32[32,128,128]{2,1,0:T(8,128)} %block_y.5), custom_call_target="tpu_custom_call" | custom-call | flops 8388608 | bytes 2097152 | tf_op jit(solution)/shard_map/ends_y/pallas_call | solution.py:164
  2.9 1.5 %collective-permute-start = (f32[1,8,640]{2,1,0:T(8,128)S(1)}, f32[1,8,640]{2,1,0:T(8,128)S(1)}, u32[]{:S(2)}, u32[]{:S(2)}) collective-permute-start(f32[1,8,640]{2,1,0:T(8,128)S(1)} %bitcast.11), channel_id=1, source_target_pairs={{0,1},{1,0},{2,3},{3,2},{4,5},{5,4},{6,7},{7,6},{8,9},{9,8},{10,11... | collective-permute-start | bytes 61448 | tf_op jit(solution)/shard_map/ppermute | solution.py:642
  4.4 2.5 %ends_x.1 = f32[16,8,640]{2,1,0:T(8,128)} custom-call(f32[3,512,512]{2,1,0:T(8,128)} %adj.5, f32[512,512]{1,0:T(8,128)} %depth.5, f32[64,128,128]{2,1,0:T(8,128)} %block_x.5), custom_call_target="tpu_custom_call" | custom-call | flops 8388608 | bytes 2097152 | tf_op jit(solution)/shard_map/ends_x/pallas_call | solution.py:112
  6.9 0.0 collective-permute-done
  6.9 1.5 %collective-permute-start.1 = (f32[2,8,640]{2,1,0:T(8,128)S(1)}, f32[2,8,640]{2,1,0:T(8,128)S(1)}, u32[]{:S(2)}, u32[]{:S(2)}) collective-permute-start(f32[2,8,640]{2,1,0:T(8,128)S(1)} %pad_maximum_fusion), channel_id=1, source_target_pairs={{0,2},{1,3},{2,0},{3,1},{4,6},{5,7},{6,4},{7,5},{8,10},{9,11},{10,... | collective-permute-start | bytes 122888 | tf_op jit(solution)/shard_map/ppermute | solution.py:646
  8.4 7.6 %all-to-all-start = ((f32[16,8,640]{2,1,0:T(8,128)}), f32[16,8,640]{2,1,0:T(8,128)S(1)}, u32[]{:S(2)}, u32[]{:S(2)}) async-start(f32[16,8,640]{2,1,0:T(8,128)} %ends_x.1), calls=%async_computation | async-start | bytes 655360 | tf_op jit(solution)/shard_map/all_to_all | solution.py:649
  16.0 0.0 collective-permute-done.1
  16.0 2.7 %collective-permute-start.2 = (f32[4,8,640]{2,1,0:T(8,128)S(1)}, f32[4,8,640]{2,1,0:T(8,128)S(1)}, u32[]{:S(2)}, u32[]{:S(2)}) collective-permute-start(f32[4,8,640]{2,1,0:T(8,128)S(1)} %constant_dynamic-update-slice_fusion.ta_in), channel_id=1, source_target_pairs={{0,4},{1,5},{2,6},{3,7},{4,0},{5,1},{6,2},{7,3},{8,12},{9,13},{10,... | collective-permute-start | bytes 245768 | tf_op jit(solution)/shard_map/ppermute | solution.py:648
  18.7 2.9 %carry.1 = (f32[512,128]{1,0:T(8,128)}, f32[64,512]{1,0:T(8,128)}, f32[8,128]{1,0:T(8,128)}) custom-call(f32[64,128,128]{2,1,0:T(8,128)} %block_x.5, f32[32,128,128]{2,1,0:T(8,128)} %block_y.5, f32[128,128]{1,0:T(8,128)} %reduced_x_hbm.1, f32[64,64]{1,0:T(8,128)} %reduced_y_hbm.1), custom_call_target="tpu_custom_call" | custom-call | flops 68719476736 | bytes 2097152 | tf_op jit(solution)/shard_map/carry/pallas_call | solution.py:255
  21.6 0.0 collective-permute-done.2.tb_in
  21.6 3.3 %all-to-all-done.tx = f32[16,8,640]{2,1,0:T(8,128)S(1)} async-done(((f32[16,8,640]{2,1,0:T(8,128)}), f32[16,8,640]{2,1,0:T(8,128)S(1)}, u32[]{:S(2)}, u32[]{:S(2)}) %all-to-all-start) | async-done | bytes 327712 | tf_op jit(solution)/shard_map/all_to_all | solution.py:649
  24.9 7.3 %elevation.1 = (f32[512,512]{1,0:T(8,128)}, f32[512,512]{1,0:T(8,128)}, f32[512,512]{1,0:T(8,128)}, f32[640,128]{1,0:T(8,128)}) custom-call(f32[16,8,640]{2,1,0:T(8,128)S(1)} %all-to-all-done.tx, f32[4,8,640]{2,1,0:T(8,128)S(1)} %constant_dynamic-update-slice_fusion.ta_in, f32[4,8,640]{2,1,0:T(8,128)S(1)} %collective-permute-done.2.tb_in, ...), custom_call_target="tpu_custom_call" | custom-call | flops 402653184 | bytes 10485760 | tf_op jit(solution)/shard_map/elevation/pallas_call | solution.py:482
  32.2 6.8 %all-to-all-start.1 = ((f32[640,1,128]{2,1,0:T(1,128)}), f32[640,1,128]{2,1,0:T(1,128)S(1)}, u32[]{:S(2)}, u32[]{:S(2)}) async-start(f32[640,1,128]{2,1,0:T(1,128)} %bitcast.13), calls=%async_computation.1 | async-start | bytes 655360 | tf_op jit(solution)/shard_map/all_to_all | solution.py:655
  39.0 3.2 %fluxes.1.fields_in = f32[3,512,512]{2,1,0:T(8,128)} custom-call(f32[512,512]{1,0:T(8,128)} %get-tuple-element.18.elev_in, f32[512,512]{1,0:T(8,128)} %get-tuple-element.19.fx_in, f32[512,512]{1,0:T(8,128)} %get-tuple-element.20.fy_in), custom_call_target="tpu_custom_call" | custom-call | flops 2621440 | bytes 6291456 | tf_op jit(solution)/shard_map/fluxes/pallas_call | solution.py:556
  42.2 8.4 %all-to-all-done.1 = f32[640,1,128]{2,1,0:T(1,128)S(1)} async-done(((f32[640,1,128]{2,1,0:T(1,128)}), f32[640,1,128]{2,1,0:T(1,128)S(1)}, u32[]{:S(2)}, u32[]{:S(2)}) %all-to-all-start.1) | async-done | bytes 327712 | tf_op jit(solution)/shard_map/all_to_all | solution.py:655
  50.5 2.5 %finish.1 = (f32[3,512,512]{2,1,0:T(8,128)}, f32[1,16]{1,0:T(1,128)}) custom-call(f32[3,512,512]{2,1,0:T(8,128)} %fluxes.1.fields_in, f32[640,128]{1,0:T(8,128)S(1)} %bitcast.10), custom_call_target="tpu_custom_call", output_to_operand_aliasing={{0}: (0, {})} | custom-call | flops 1048576 | bytes 1048576 | tf_op jit(solution)/shard_map/finish/pallas_call | solution.py:613
  (3 shorter events, 0.0 us)
Async XLA Ops:
  2.9 4.0 %collective-permute-start = (f32[1,8,640]{2,1,0:T(8,128)S(1)}, f32[1,8,640]{2,1,0:T(8,128)S(1)}, u32[]{:S(2)}, u32[]{:S(2)}) collective-permute-start(f32[1,8,640]{2,1,0:T(8,128)S(1)} %bitcast.11), channel_id=1, source_target_pairs={{0,1},{1,0},{2,3},{3,2},{4,5},{5,4},{6,7},{7,6},{8,9},{9,8},{10,11... | collective-permute-start | bytes 61448 | tf_op jit(solution)/shard_map/ppermute | solution.py:642
  6.9 9.1 %collective-permute-start.1 = (f32[2,8,640]{2,1,0:T(8,128)S(1)}, f32[2,8,640]{2,1,0:T(8,128)S(1)}, u32[]{:S(2)}, u32[]{:S(2)}) collective-permute-start(f32[2,8,640]{2,1,0:T(8,128)S(1)} %pad_maximum_fusion), channel_id=1, source_target_pairs={{0,2},{1,3},{2,0},{3,1},{4,6},{5,7},{6,4},{7,5},{8,10},{9,11},{10,... | collective-permute-start | bytes 122888 | tf_op jit(solution)/shard_map/ppermute | solution.py:646
  8.4 16.5 %all-to-all-start = ((f32[16,8,640]{2,1,0:T(8,128)}), f32[16,8,640]{2,1,0:T(8,128)S(1)}, u32[]{:S(2)}, u32[]{:S(2)}) async-start(f32[16,8,640]{2,1,0:T(8,128)} %ends_x.1), calls=%async_computation | async-start | bytes 655360 | tf_op jit(solution)/shard_map/all_to_all | solution.py:649
  16.0 5.6 %collective-permute-start.2 = (f32[4,8,640]{2,1,0:T(8,128)S(1)}, f32[4,8,640]{2,1,0:T(8,128)S(1)}, u32[]{:S(2)}, u32[]{:S(2)}) collective-permute-start(f32[4,8,640]{2,1,0:T(8,128)S(1)} %constant_dynamic-update-slice_fusion.ta_in), channel_id=1, source_target_pairs={{0,4},{1,5},{2,6},{3,7},{4,0},{5,1},{6,2},{7,3},{8,12},{9,13},{10,... | collective-permute-start | bytes 245768 | tf_op jit(solution)/shard_map/ppermute | solution.py:648
  32.2 18.4 %all-to-all-start.1 = ((f32[640,1,128]{2,1,0:T(1,128)}), f32[640,1,128]{2,1,0:T(1,128)S(1)}, u32[]{:S(2)}, u32[]{:S(2)}) async-start(f32[640,1,128]{2,1,0:T(1,128)} %bitcast.13), calls=%async_computation.1 | async-start | bytes 655360 | tf_op jit(solution)/shard_map/all_to_all | solution.py:655

commit v5 on v4

v5 whole, which is shorter than its diff:
```python
import jax
import jax.numpy as jnp
from jax import lax
from jax.experimental import pallas as pl
from jax.experimental.pallas import tpu as pltpu
from jax.sharding import PartitionSpec as P

courant = 0.5
f32 = jnp.float32
bf16 = jnp.bfloat16
K = 128
EXTRA = 128

NN = (((1,), (0,)), ((), ()))
NT = (((1,), (1,)), ((), ()))
TN = (((0,), (0,)), ((), ()))


def halves(x):
    high = x.astype(bf16)
    return high, (x - high.astype(f32)).astype(bf16)


def mm(a, b, dims):
    return lax.dot_general(a, b, dims, preferred_element_type=f32)


def mm3(a, b, dims):
    ah, al = a
    bh, bl = b
    return mm(ah, bh, dims) + (mm(ah, bl, dims) + mm(al, bh, dims))


def exact(a, b, dims):
    return lax.dot_general(a, b, dims, precision=lax.Precision.HIGHEST, preferred_element_type=f32)


def iota(shape, dim):
    return lax.broadcasted_iota(jnp.int32, shape, dim)


def hbm_spec():
    return pl.BlockSpec(memory_space=pltpu.HBM)


def vmem_spec():
    return pl.BlockSpec(memory_space=pltpu.VMEM)


def in_hbm(*arrays):
    return tuple(pltpu.with_memory_space_constraint(a, pltpu.HBM) for a in arrays)


def in_vmem(*arrays):
    return tuple(pltpu.with_memory_space_constraint(a, pltpu.VMEM) for a in arrays)


def cost(flops, nbytes):
    return pl.CostEstimate(flops=flops, bytes_accessed=nbytes, transcendentals=0)


def stacked(first, last, c):
    high, low = halves(jnp.concatenate([first[c, 0:1, :], last[c, 7:8, :]], axis=0))
    return jnp.concatenate([high, low], axis=0)


def two_rows(weights, field, dims):
    high, low = halves(field)
    both = mm(weights, high, dims)
    return both[0:2] + both[2:4] + mm(weights[0:2], low, dims)


def block_ends(blocks, index, first, last, sems):
    here = pl.ds(index * first.shape[0], first.shape[0])
    return [
        pltpu.make_async_copy(blocks.at[here, pl.ds(0, 8), :], first, sems.at[0]),
        pltpu.make_async_copy(blocks.at[here, pl.ds(K - 8, 8), :], last, sems.at[1]),
    ]


def ends_kernel(
    adj, depth, block_x, block_y, px_hbm, py,
    vx, vy, first_x, last_x, first_y, last_y, drow, dcol, px, sems, out_sems,
):
    rows, cols = vx.shape
    nbx = first_x.shape[0]
    nby = first_y.shape[0]
    small = block_ends(block_x, lax.axis_index("gx"), first_x, last_x, sems)
    small += block_ends(block_y, lax.axis_index("gy"), first_y, last_y, sems.at[pl.ds(2, 2)])
    small.append(pltpu.make_async_copy(depth.at[pl.ds(rows - 8, 8), :], drow, sems.at[4]))
    side = pltpu.make_async_copy(depth.at[:, pl.ds(cols - K, K)], dcol, sems.at[5])
    field_x = pltpu.make_async_copy(adj.at[1], vx, sems.at[6])
    field_y = pltpu.make_async_copy(adj.at[2], vy, sems.at[7])
    for copy in small + [field_x, side, field_y]:
        copy.start()
    for copy in small:
        copy.wait()
    for part in range(cols // K):
        px[part : part + 1, cols:] = drow[7:8, part * K : (part + 1) * K]
    px[cols // K :, cols:] = jnp.zeros((8 - cols // K, EXTRA), f32)
    weights_x = [stacked(first_x, last_x, c) for c in range(nbx)]
    weights_y = [stacked(first_y, last_y, c) for c in range(nby)]
    field_x.wait()
    for c in range(nbx):
        px[2 * c : 2 * c + 2, :cols] = two_rows(weights_x[c], vx[c * K : (c + 1) * K, :], NN)
    outs = [pltpu.make_async_copy(px, px_hbm.at[d], out_sems.at[d]) for d in range(px_hbm.shape[0])]
    for copy in outs:
        copy.start()
    side.wait()
    field_y.wait()
    at_last = (iota((8, K), 1) == K - 1).astype(f32).astype(bf16)
    high, low = halves(dcol[...])
    line = mm(at_last, high, NT) + mm(at_last, low, NT)
    for part in range(rows // K):
        py[part : part + 1, rows:] = line[0:1, part * K : (part + 1) * K]
    py[rows // K :, rows:] = jnp.zeros((8 - rows // K, EXTRA), f32)
    for r in range(rows // K):
        for c in range(nby):
            field = vy[r * K : (r + 1) * K, c * K : (c + 1) * K]
            py[2 * c : 2 * c + 2, r * K : (r + 1) * K] = two_rows(weights_y[c], field, NT)
    for copy in outs:
        copy.wait()


def ends(adj, depth, block_x, block_y, size_x, size_y):
    rows, cols = depth.shape
    nbx = block_x.shape[0] // size_x
    nby = block_y.shape[0] // size_y
    shape = (2 * nbx, cols + EXTRA)
    return pl.pallas_call(
        ends_kernel,
        out_shape=(
            pltpu.HBM((size_x, *shape), f32),
            jax.ShapeDtypeStruct((2 * nby, rows + EXTRA), f32),
        ),
        in_specs=[hbm_spec()] * 4,
        out_specs=(hbm_spec(), vmem_spec()),
        scratch_shapes=[
            pltpu.VMEM((rows, cols), f32),
            pltpu.VMEM((rows, cols), f32),
            pltpu.VMEM((nbx, 8, K), f32),
            pltpu.VMEM((nbx, 8, K), f32),
            pltpu.VMEM((nby, 8, K), f32),
            pltpu.VMEM((nby, 8, K), f32),
            pltpu.VMEM((8, cols), f32),
            pltpu.VMEM((rows, K), f32),
            pltpu.VMEM(shape, f32),
            pltpu.SemaphoreType.DMA((8,)),
            pltpu.SemaphoreType.DMA((size_x,)),
        ],
        compiler_params=pltpu.CompilerParams(vmem_limit_bytes=16 << 20),
        cost_estimate=cost(2 * rows * cols * 32, 3 << 20),
        name="ends",
    )(*in_hbm(adj, depth, block_x, block_y))


def carry_kernel(
    block_x, block_y, reduced_x_hbm, reduced_y_hbm, mx_hbm, my_hbm,
    mx, my, wx, wy, reduced_x, reduced_y, sems, out_sems,
):
    u = lax.axis_index("gx")
    v = lax.axis_index("gy")
    nbx = wx.shape[0]
    nby = wy.shape[0]
    copies = [
        pltpu.make_async_copy(reduced_x_hbm, reduced_x, sems.at[0]),
        pltpu.make_async_copy(block_x.at[pl.ds(u * nbx, nbx)], wx, sems.at[1]),
        pltpu.make_async_copy(reduced_y_hbm, reduced_y, sems.at[2]),
        pltpu.make_async_copy(block_y.at[pl.ds(v * nby, nby)], wy, sems.at[3]),
    ]
    for copy in copies:
        copy.start()
    outs = [
        pltpu.make_async_copy(mx, mx_hbm, out_sems.at[0]),
        pltpu.make_async_copy(my, my_hbm, out_sems.at[1]),
    ]
    for copy in copies[:2]:
        copy.wait()
    own_x = reduced_x[pl.ds(pl.multiple_of(u * 8, 8), 8), :]
    for c in range(nbx):
        w = wx[c]
        g = w[:, 0:1] * own_x[2 * c : 2 * c + 1, :] + w[:, K - 1 : K] * own_x[2 * c + 1 : 2 * c + 2, :]
        for i, part in enumerate(zip(halves(w), halves(g))):
            mx[i, c * K : (c + 1) * K, :] = jnp.concatenate(part, axis=1)
    outs[0].start()
    for copy in copies[2:]:
        copy.wait()
    own_y = halves(reduced_y[pl.ds(pl.multiple_of(v * 8, 8), 8), :])
    sub = iota((8, K), 0)
    for c in range(nby):
        turned = wy[c].T
        across = jnp.where(sub == 2 * c, turned[0:1, :], 0.0)
        across = jnp.where(sub == 2 * c + 1, turned[K - 1 : K, :], across)
        g = mm3(own_y, halves(across), TN)
        for i, part in enumerate(zip(halves(turned), halves(g))):
            my[i, :, c * K : (c + 1) * K] = jnp.concatenate(part, axis=0)
    outs[1].start()
    for copy in outs:
        copy.wait()


def carry(block_x, block_y, reduced_x, reduced_y):
    nbx = block_x.shape[0] // lax.axis_size("gx")
    nby = block_y.shape[0] // lax.axis_size("gy")
    results = [
        ((2, nbx * K, K + reduced_x.shape[0]), bf16),
        ((2, K + reduced_y.shape[0], nby * K), bf16),
    ]
    return pl.pallas_call(
        carry_kernel,
        out_shape=tuple(pltpu.HBM(*result) for result in results),
        in_specs=[hbm_spec()] * 4,
        out_specs=(hbm_spec(),) * 2,
        scratch_shapes=[pltpu.VMEM(*result) for result in results]
        + [
            pltpu.VMEM((nbx, K, K), f32),
            pltpu.VMEM((nby, K, K), f32),
            pltpu.VMEM(reduced_x.shape, f32),
            pltpu.VMEM(reduced_y.shape, f32),
            pltpu.SemaphoreType.DMA((4,)),
            pltpu.SemaphoreType.DMA((2,)),
        ],
        compiler_params=pltpu.CompilerParams(vmem_limit_bytes=16 << 20),
        cost_estimate=cost(1 << 24, 2 << 20),
        name="carry",
    )(*in_hbm(block_x, block_y, reduced_x, reduced_y))


def shares_kernel(
    block_x, block_y, reduced_x_hbm, reduced_y_hbm, coef_hbm, footprint_hbm,
    gside_hbm, share_hbm, at_row_hbm,
    gside, share, at_row, wpx, wpy, reduced_x, reduced_y, coef, footprint, sems, out_sems,
):
    u = lax.axis_index("gx")
    v = lax.axis_index("gy")
    nbx = block_x.shape[0] // lax.axis_size("gx")
    nby = block_y.shape[0] // lax.axis_size("gy")
    before_x = jnp.maximum(u * nbx - 1, 0)
    before_y = jnp.maximum(v * nby - 1, 0)
    copies = [
        pltpu.make_async_copy(footprint_hbm, footprint, sems.at[0]),
        pltpu.make_async_copy(coef_hbm, coef, sems.at[1]),
        pltpu.make_async_copy(reduced_x_hbm, reduced_x, sems.at[2]),
        pltpu.make_async_copy(reduced_y_hbm, reduced_y, sems.at[3]),
        pltpu.make_async_copy(block_x.at[before_x, pl.ds(K - 8, 8), :], wpx, sems.at[4]),
        pltpu.make_async_copy(block_y.at[before_y, pl.ds(K - 8, 8), :], wpy, sems.at[5]),
    ]
    for copy in copies:
        copy.start()
    outs = [
        pltpu.make_async_copy(share, share_hbm, out_sems.at[0]),
        pltpu.make_async_copy(at_row, at_row_hbm, out_sems.at[1]),
        pltpu.make_async_copy(gside, gside_hbm, out_sems.at[2]),
    ]
    for copy in copies[:2]:
        copy.wait()
    places, modes, count = coef.shape
    tiles_y = share.shape[1] // modes
    tiles_x = at_row.shape[1]
    total_cols = tiles_y * lax.axis_size("gy")
    number = footprint[...]
    row = lax.shift_right_logical(number, total_cols.bit_length() - 1)
    col = (number & (total_cols - 1)) - v * tiles_y
    top = jnp.min(row, axis=0, keepdims=True)
    tile_row = iota((tiles_x, count), 0)
    tile_col = lax.shift_right_logical(iota((tiles_y * modes, count), 0), modes.bit_length() - 1)
    for step in range(2):
        at_row[step] = (tile_row == top + step - u * tiles_x).astype(f32).astype(bf16)
        index = jnp.where(row == top + step, col, -1)
        acc = jnp.zeros((tiles_y * modes, count), f32)
        for f in range(places):
            scale = jnp.concatenate([coef[f]] * tiles_y, axis=0)
            acc = acc + jnp.where(tile_col == index[f : f + 1, :], scale, 0.0)
        share[step] = acc
    for copy in outs[:2]:
        copy.start()
    for copy in copies[2:]:
        copy.wait()

    def side(w, reduced, index):
        prev = reduced[pl.ds(pl.multiple_of(jnp.maximum(index - 1, 0) * 8, 8), 8), :]
        width = prev.shape[1]
        g = w[7:8, 0:1] * prev[6:7, :] + w[7:8, K - 1 : K] * prev[7:8, :]
        g = g + (iota((1, width), 1) == index * 8 - 1).astype(f32)
        return jnp.where(index > 0, g, 0.0)

    gside[...] = jnp.zeros(gside.shape, f32)
    gside[0:1, :] = side(wpx[...], reduced_x, u)
    gside[1:2, : reduced_y.shape[1]] = side(wpy[...], reduced_y, v)
    outs[2].start()
    for copy in outs:
        copy.wait()


def shares(block_x, block_y, reduced_x, reduced_y, coef, footprint, wet):
    coef = coef.transpose(1, 2, 0)
    footprint = footprint.T
    _, modes, count = coef.shape
    tiles_x, tiles_y = wet.shape
    results = [
        ((8, reduced_x.shape[0]), f32),
        ((2, tiles_y * modes, count), f32),
        ((2, tiles_x, count), bf16),
    ]
    return pl.pallas_call(
        shares_kernel,
        out_shape=tuple(pltpu.HBM(*result) for result in results),
        in_specs=[hbm_spec()] * 6,
        out_specs=(hbm_spec(),) * 3,
        scratch_shapes=[pltpu.VMEM(*result) for result in results]
        + [
            pltpu.VMEM((8, K), f32),
            pltpu.VMEM((8, K), f32),
            pltpu.VMEM(reduced_x.shape, f32),
            pltpu.VMEM(reduced_y.shape, f32),
            pltpu.VMEM(coef.shape, f32),
            pltpu.VMEM(footprint.shape, jnp.int32),
            pltpu.SemaphoreType.DMA((6,)),
            pltpu.SemaphoreType.DMA((3,)),
        ],
        compiler_params=pltpu.CompilerParams(vmem_limit_bytes=16 << 20),
        cost_estimate=cost(1 << 24, 2 << 20),
        name="shares",
    )(*in_hbm(block_x, block_y, reduced_x, reduced_y, coef, footprint))


def elev_kernel(
    tx, ta_in, tb_in, mx_in, my_in, gside_in, share_in, at_row_in, adj, depth, basis_in, wet_in, owner_in,
    fields_out, parts_out,
    ty, mx, my, gside, share, at_row, planes, dep, basis, wet, owner,
    elev, fx, fy, tyn, mom, parts, sems, row_sems, out_sems,
):
    u = lax.axis_index("gx")
    v = lax.axis_index("gy")
    rows, cols = dep.shape
    steps = rows // K
    half = ta_in.shape[0]
    first = [
        pltpu.make_async_copy(ta_in, ty.at[pl.ds(0, half)], sems.at[0]),
        pltpu.make_async_copy(tb_in, ty.at[pl.ds(half, half)], sems.at[1]),
        pltpu.make_async_copy(gside_in, gside, sems.at[2]),
        pltpu.make_async_copy(owner_in, owner, sems.at[3]),
    ]
    second = [
        pltpu.make_async_copy(mx_in, mx, sems.at[4]),
        pltpu.make_async_copy(my_in, my, sems.at[5]),
    ]
    last = [
        pltpu.make_async_copy(basis_in, basis, sems.at[6]),
        pltpu.make_async_copy(wet_in, wet, sems.at[7]),
        pltpu.make_async_copy(share_in, share, sems.at[8]),
        pltpu.make_async_copy(at_row_in, at_row, sems.at[9]),
    ]
    fields = []
    for r in range(steps):
        here = pl.ds(r * K, K)
        fields.append(
            [
                pltpu.make_async_copy(adj.at[:, here, :], planes.at[:, here, :], row_sems.at[r, 0]),
                pltpu.make_async_copy(depth.at[here, :], dep.at[here, :], row_sems.at[r, 1]),
            ]
        )
    for group in [fields[0], first, second, fields[1], last[:1], fields[2], fields[3], last[1:]]:
        for copy in group:
            copy.start()
    txs = halves(jnp.concatenate([tx[d][:, :cols] for d in range(tx.shape[0])], axis=0))
    parts[...] = jnp.zeros(parts.shape, f32)
    for copy in first:
        copy.wait()
    devices = parts.shape[0] // 5
    count = owner.shape[1]
    slots = count // devices
    own = owner[...]
    device_of = iota((devices, count), 0) == lax.shift_right_logical(own, slots.bit_length() - 1)
    device_of = device_of.astype(f32).astype(bf16)
    slot_of = iota((slots, count), 0) == (own & (slots - 1))
    for j in range(2 * half):
        far = j ^ v
        place = 0
        for i, bit in enumerate(rounds(2 * half)):
            place = place | (((far // bit) & 1) << i)
        tyn[j * 8 : (j + 1) * 8, :] = ty[place]
    ty_all = tyn[:, :rows]
    tys = halves(ty_all)
    tyt = halves(ty_all.T)
    up = jnp.maximum(u - 1, 0)
    left = jnp.maximum(v - 1, 0)
    gs = gside[...]
    edge_x = mm3(halves(gs), txs, NN)[0:1, :]
    edge_y = mm3(halves(gs[:, : ty_all.shape[0]]), tys, NN)[1:2, :]
    drow = tx[up][:, cols:]
    drow = jnp.concatenate([drow[p : p + 1, :] for p in range(cols // K)], axis=1)
    dcol = tyn[pl.ds(pl.multiple_of(left * 8, 8), 8), rows:]
    dcol = jnp.concatenate([dcol[p : p + 1, :] for p in range(rows // K)], axis=1)
    carry = edge_x * drow
    side = jnp.broadcast_to(edge_y * dcol, (8, rows)).T
    row = iota((K, cols), 0)
    lane = iota((K, K), 1)
    modes, tile_h, tile_w = basis.shape
    per = K // tile_h
    outs = []
    firsts = []

    def send(plane, source, r):
        here = pl.ds(r * K, K)
        copy = pltpu.make_async_copy(
            source.at[here, :], fields_out.at[plane, here, :], out_sems.at[r, plane]
        )
        copy.start()
        outs.append(copy)

    for copy in second:
        copy.wait()
    for r in range(steps):
        here = slice(r * K, (r + 1) * K)
        if r == 0:
            for copy in fields[0] + fields[1] + last[:1]:
                copy.wait()
        if r == 2:
            for copy in fields[2] + fields[3]:
                copy.wait()
        d = dep[here, :]
        high, low = halves(planes[1, here, :])
        flux_x = mm3(
            (mx[0, here, :], mx[1, here, :]),
            (jnp.concatenate([high, txs[0]], axis=0), jnp.concatenate([low, txs[1]], axis=0)),
            NN,
        )
        if r % 2 == 0:
            pair = slice(r * K, (r + 2) * K)
            pieces = []
            for c in range(cols // K):
                block = slice(c * K, (c + 1) * K)
                high, low = halves(planes[2, pair, block])
                lhs = (
                    jnp.concatenate([high, tyt[0][pair, :]], axis=1),
                    jnp.concatenate([low, tyt[1][pair, :]], axis=1),
                )
                pieces.append(mm3(lhs, (my[0, :, block], my[1, :, block]), NN))
        flux_y = jnp.concatenate([piece[(r % 2) * K : (r % 2 + 1) * K] for piece in pieces], axis=1)
        weighted_x = d * flux_x
        weighted_y = d * flux_y
        before_x = jnp.where(row == 0, carry, pltpu.roll(weighted_x, 1, 0))
        carry = weighted_x[K - 1 : K, :]
        turned = [side[here, 0:1]] + [
            pltpu.roll(weighted_y[:, c * K : (c + 1) * K], 1, 1) for c in range(cols // K)
        ]
        before_y = jnp.concatenate(
            [jnp.where(lane == 0, turned[c], turned[c + 1]) for c in range(cols // K)], axis=1
        )
        e = planes[0, here, :] + courant * ((weighted_x - before_x) + (weighted_y - before_y))
        elev[here, :] = e
        send(0, elev, r)
        right = [pltpu.roll(e[:, c * K : (c + 1) * K], K - 1, 1) for c in range(cols // K)] + [0.0]
        right = jnp.concatenate(
            [jnp.where(lane == K - 1, right[c + 1], right[c]) for c in range(cols // K)], axis=1
        )
        fy[here, :] = flux_y + courant * (right - e)
        send(2, fy, r)
        fx[here, :] = flux_x + courant * (jnp.where(row == K - 1, 0.0, pltpu.roll(e, K - 1, 0)) - e)
        if r > 0:
            end = slice(r * K - 8, r * K)
            fx[end, :] = fx[end, :] + jnp.where(row[:8] == 7, courant * e[0:1, :], 0.0)
            send(1, fx, r - 1)
        if r == 0:
            top = e[0:1, :]
        firsts.append(e[:, :K].T[0:1, :])
        for a in range(per):
            for w in range(cols // tile_w):
                tile = e[a * tile_h : (a + 1) * tile_h, w * tile_w : (w + 1) * tile_w]
                for b in range(modes):
                    at = b * (rows // tile_h) + r * per + a
                    mom[at : at + 1, w * tile_w : (w + 1) * tile_w] = jnp.sum(
                        tile * basis[b], axis=0, keepdims=True
                    )
    send(1, fx, steps - 1)
    for copy in last[1:]:
        copy.wait()
    tiles_y, tiles_x = wet.shape
    ones = jnp.ones((8, tile_w), bf16)
    pieces = []
    for w in range(tiles_y):
        high, low = halves(mom[:, w * tile_w : (w + 1) * tile_w])
        line = (mm(ones, high, NT) + mm(ones, low, NT))[0:1, :]
        keep = wet[w : w + 1, :].astype(f32)
        for b in range(modes):
            pieces.append(line[:, b * tiles_x : (b + 1) * tiles_x] * keep)
    high, low = halves(jnp.concatenate(pieces, axis=0))
    table = jnp.concatenate([high, low], axis=0)
    lines = tiles_y * modes
    acc = jnp.zeros((lines, count), f32)
    for step in range(2):
        both = mm(table, at_row[step], NN)
        acc = acc + (both[:lines] + both[lines:]) * share[step]
    total = jnp.sum(acc, axis=0, keepdims=True)
    placed = jnp.concatenate(halves(jnp.where(slot_of, total, 0.0)), axis=0)
    both = mm(device_of, placed, NT)
    sums = both[:, :slots] + both[:, slots:]
    parts[pl.ds(0, devices, stride=5), :] = jnp.concatenate(
        [sums, jnp.zeros((devices, K - slots), f32)], axis=1
    )
    size_y = lax.axis_size("gy")

    def put(device, line):
        for p in range(4):
            parts[pl.ds(device * 5 + 1 + p, 1), :] = line[:, p * K : (p + 1) * K]

    @pl.when(u > 0)
    def _():
        put((u - 1) * size_y + v, top)

    @pl.when(v > 0)
    def _():
        put(u * size_y + v - 1, jnp.concatenate(firsts, axis=1))

    outs.append(pltpu.make_async_copy(parts, parts_out, sems.at[10]))
    outs[-1].start()
    for copy in outs:
        copy.wait()


def elevation(tx, ta, tb, carried, adj, depth, basis, wet, owner):
    rows, cols = depth.shape
    modes, tile_h, tile_w = basis.shape
    devices = lax.axis_size("gx") * lax.axis_size("gy")
    steps = rows // K
    wet = wet.T
    owner = owner.reshape(1, -1)
    field = ((rows, cols), f32)
    far = (2 * ta.shape[0], 8, rows + EXTRA)
    parts = ((devices * 5, K), f32)
    like = lambda *arrays: [pltpu.VMEM(a.shape, a.dtype) for a in arrays]
    return pl.pallas_call(
        elev_kernel,
        out_shape=(pltpu.HBM((3, rows, cols), f32), pltpu.HBM(*parts)),
        in_specs=[vmem_spec()] + [pl.BlockSpec(memory_space=pl.ANY)] * 2 + [hbm_spec()] * 10,
        out_specs=(hbm_spec(),) * 2,
        scratch_shapes=[pltpu.VMEM(far, f32)]
        + like(*carried)
        + [pltpu.VMEM((3, rows, cols), f32), pltpu.VMEM(*field)]
        + like(basis, wet, owner)
        + [pltpu.VMEM(*field)] * 3
        + [
            pltpu.VMEM((far[0] * 8, far[2]), f32),
            pltpu.VMEM((rows // tile_h * modes, cols), f32),
            pltpu.VMEM(*parts),
            pltpu.SemaphoreType.DMA((11,)),
            pltpu.SemaphoreType.DMA((steps, 2)),
            pltpu.SemaphoreType.DMA((steps, 3)),
        ],
        compiler_params=pltpu.CompilerParams(vmem_limit_bytes=32 << 20),
        cost_estimate=cost(12 * rows * cols * K, 10 << 20),
        name="elevation",
    )(tx, ta, tb, *in_hbm(*carried, adj, depth, basis, wet, owner))


def finish_kernel(fields_in, sums, bottom_in, edge_in, fields, grad, bottom, edge, out_sems):
    u = lax.axis_index("gx")
    v = lax.axis_index("gy")
    size_x = lax.axis_size("gx")
    size_y = lax.axis_size("gy")
    rows, cols = fields.shape[1:]

    def line(device):
        return jnp.concatenate([sums[pl.ds(device * 5 + 1 + p, 1), :] for p in range(4)], axis=1)

    below = line(jnp.minimum(u + 1, size_x - 1) * size_y + v) * jnp.where(u + 1 < size_x, courant, 0.0)
    right = line(u * size_y + jnp.minimum(v + 1, size_y - 1)) * jnp.where(v + 1 < size_y, courant, 0.0)
    right = jnp.broadcast_to(right, (8, rows)).T[:, 0:1]
    edge[...] = edge_in[...] + jnp.where(iota((rows, K), 1) == K - 1, right, 0.0)
    bottom[...] = bottom_in[...] + jnp.where(iota((8, cols), 0) == 7, below, 0.0)
    writes = [
        pltpu.make_async_copy(edge, fields.at[2, :, pl.ds(cols - K, K)], out_sems.at[0]),
        pltpu.make_async_copy(bottom, fields.at[1, pl.ds(rows - 8, 8), :], out_sems.at[1]),
    ]
    for copy in writes:
        copy.start()
    devices = sums.shape[0] // 5
    total = jnp.sum(sums[pl.ds(0, devices, stride=5), :], axis=0, keepdims=True)
    grad[...] = total[:, : grad.shape[1]]
    for copy in writes:
        copy.wait()


def finish(fields, sums, slots):
    _, rows, cols = fields.shape
    bottom = fields[1, rows - 8 :, :]
    edge = fields[2, :, cols - K :]
    return pl.pallas_call(
        finish_kernel,
        out_shape=(pltpu.HBM(fields.shape, f32), jax.ShapeDtypeStruct((1, slots), f32)),
        in_specs=[hbm_spec(), vmem_spec(), vmem_spec(), vmem_spec()],
        out_specs=(hbm_spec(), vmem_spec()),
        input_output_aliases={0: 0},
        scratch_shapes=[
            pltpu.VMEM((8, cols), f32),
            pltpu.VMEM((rows, K), f32),
            pltpu.SemaphoreType.DMA((2,)),
        ],
        compiler_params=pltpu.CompilerParams(vmem_limit_bytes=16 << 20),
        cost_estimate=cost(1 << 20, 1 << 20),
        name="finish",
    )(*in_hbm(fields), sums, bottom, edge)


def rounds(size):
    return [size >> i for i in range(1, size.bit_length())]


def partner(axis, bit):
    return [(i, i ^ bit) for i in range(lax.axis_size(axis))]


def body(
    adj_fields, depth, block_x, reduced_x, block_y, reduced_y, basis, coef, footprint, owner, wet
):
    size_x = lax.axis_size("gx")
    size_y = lax.axis_size("gy")
    px, py = ends(adj_fields, depth, block_x, block_y, size_x, size_y)
    tx = lax.all_to_all(px, "gx", split_axis=0, concat_axis=0, tiled=True)
    matrices = carry(block_x, block_y, reduced_x, reduced_y)
    sides = shares(block_x, block_y, reduced_x, reduced_y, coef, footprint, wet)
    ty = py[None]
    bits = rounds(size_y)
    for bit in bits[:-1]:
        ty = jnp.concatenate([ty, lax.ppermute(ty, "gy", partner("gy", bit))], axis=0)
    ty, matrices = lax.optimization_barrier((ty, matrices))
    ty_far = lax.ppermute(ty, "gy", partner("gy", bits[-1]))
    carried = (*matrices, *sides)
    fields, parts = elevation(tx, ty, ty_far, carried, adj_fields, depth, basis, wet, owner)
    devices = size_x * size_y
    sums = lax.all_to_all(
        parts[:, None, :], ("gx", "gy"), split_axis=0, concat_axis=0, tiled=True
    )
    slots = owner.shape[0] // devices
    adj_before, grad = finish(fields, sums[:, 0, :], slots)
    return adj_before, grad.reshape(slots)


def solution(mesh):
    in_specs = (
        P(None, "gx", "gy"),
        P("gx", "gy"),
        P(),
        P(),
        P(),
        P(),
        P(),
        P(),
        P(),
        P(),
        P("gx", "gy"),
    )
    out_specs = (P(None, "gx", "gy"), P(("gx", "gy")))
    return jax.shard_map(body, mesh=mesh, in_specs=in_specs, out_specs=out_specs, check_vma=False)
```

time: 53.3 us -> 49.6 us (0.931)
  Pallas kernels: 20.5 us -> 15.1 us
  local copies, waits for them, and re-layouts: 0.01 us -> 1.69 us
  waiting for transfers between devices: 11.6 us -> 10.5 us
  starting transfers between devices: 20.1 us -> 21.1 us
    pallas_call x4 -> x3, Pallas kernels: 15.2 us -> 11.3 us  [the longest x1 6.4 us: elevation(): pl.pallas_call(elev_kernel, out_shape=(pltpu.HBM((3, rows, cols), f32), p...]
    ppermute x1 -> x2, starting transfers between devices: 1.46 us -> 4.3 us  [body(): lax.ppermute(ty, 'gy', partner('gy', bit))]
    all_to_all x1, waiting for transfers between devices: 3.28 us -> 0.53 us  [body(): tx = lax.all_to_all(px, 'gx', split_axis=0, concat_axis=0, tiled=True)]
    ppermute x2 -> x1, starting transfers between devices: 4.2 us -> 2.38 us  [body(): ty_far = lax.ppermute(ty, 'gy', partner('gy', bits[-1]))]
    squeeze x0 -> x2, local copies, waits for them, and re-layouts: none -> 1.69 us  [the longest x1 0.97 us: finish(): edge = fields[2, :, cols - K:]]
    all_to_all x1, waiting for transfers between devices: 8.35 us -> 9.87 us  [body(): lax.all_to_all(parts[:, None, :], ('gx', 'gy'), split_axis=0, concat_axis...]
    pallas_call x1, Pallas kernels: 2.46 us -> 1.49 us  [finish(): pl.pallas_call(finish_kernel, out_shape=(pltpu.HBM(fields.shape, f32), ja...]
    pallas_call x1, Pallas kernels: 2.87 us -> 2.33 us  [carry(): pl.pallas_call(carry_kernel, out_shape=tuple((pltpu.HBM(*result) for resu...]
  transfers between devices with their start and end apart: 5 -> 5, of which waited for: 2 -> 3; matrix products, arithmetic and copies ran while one was open for 0% -> 3% of each run, Pallas kernels for 16% -> 9%
where the time goes in v5:
time: 49.6 us; the launch traced here: 49.2 us
  starting transfers between devices  21.1 us (43%)
  Pallas kernels  15.1 us (30%)
  waiting for transfers between devices  10.5 us (21%)
  local copies, waits for them, and re-layouts  1.69 us (3%)
  between operations  0.71 us (1%)
    all_to_all x1, waiting for transfers between devices, body(): lax.all_to_all(parts[:, None, :], ('gx', 'gy'), split_axis=0, concat_axis...  9.87 us
    all_to_all x1, starting transfers between devices, body(): tx = lax.all_to_all(px, 'gx', split_axis=0, concat_axis=0, tiled=True)  7.6 us
    all_to_all x1, starting transfers between devices, body(): lax.all_to_all(parts[:, None, :], ('gx', 'gy'), split_axis=0, concat_axis...  6.81 us
    pallas_call x1, Pallas kernels, elevation(): pl.pallas_call(elev_kernel, out_shape=(pltpu.HBM((3, rows, cols), f32), p...  6.4 us
    ppermute x2, starting transfers between devices, body(): lax.ppermute(ty, 'gy', partner('gy', bit))  4.3 us
    pallas_call x1, Pallas kernels, ends(): pl.pallas_call(ends_kernel, out_shape=(pltpu.HBM((size_x, *shape), f32),...  2.7 us
    ppermute x1, starting transfers between devices, body(): ty_far = lax.ppermute(ty, 'gy', partner('gy', bits[-1]))  2.38 us
    pallas_call x1, Pallas kernels, carry(): pl.pallas_call(carry_kernel, out_shape=tuple((pltpu.HBM(*result) for resu...  2.33 us
  transfers between devices with their start and end apart: 5, of which 3 were waited for; matrix products, arithmetic and copies ran while one was open for 3% of the time, Pallas kernels for 9%

profile of v5, /device:TPU:1, one launch (start us, length us, event | category | flops | bytes accessed | tf_op | source)
XLA Modules:
  0.0 49.2 jit_solution(6661542901239359689)
XLA Ops:
  0.6 2.7 %ends.1 = (f32[16,8,640]{2,1,0:T(8,128)}, f32[8,640]{1,0:T(8,128)S(1)}) custom-call(f32[3,512,512]{2,1,0:T(8,128)} %adj.3, f32[512,512]{1,0:T(8,128)} %depth.3, f32[64,128,128]{2,1,0:T(8,128)} %block_x.5, f32[32,128,128]{2,1,0:T(8,128)} %block_y.5), custom_call_target="tpu_custom_call" | custom-call | flops 16777216 | bytes 3145728 | tf_op jit(solution)/shard_map/ends/pallas_call | solution.py:130
  3.3 3.8 %collective-permute-start = (f32[1,8,640]{2,1,0:T(8,128)S(1)}, f32[1,8,640]{2,1,0:T(8,128)S(1)}, u32[]{:S(2)}, u32[]{:S(2)}) collective-permute-start(f32[1,8,640]{2,1,0:T(8,128)S(1)} %bitcast.15), channel_id=1, source_target_pairs={{0,4},{1,5},{2,6},{3,7},{4,0},{5,1},{6,2},{7,3},{8,12},{9,13},{10,... | collective-permute-start | bytes 61448 | tf_op jit(solution)/shard_map/ppermute | solution.py:626
  7.2 7.6 %all-to-all-start = ((f32[16,8,640]{2,1,0:T(8,128)}), f32[16,8,640]{2,1,0:T(8,128)S(1)}, u32[]{:S(2)}, u32[]{:S(2)}) async-start(f32[16,8,640]{2,1,0:T(8,128)} %get-tuple-element.16), calls=%async_computation | async-start | bytes 655360 | tf_op jit(solution)/shard_map/all_to_all | solution.py:620
  14.8 0.0 collective-permute-done
  14.8 0.5 collective-permute-start.1
  15.3 2.3 %carry.1 = (bf16[2,512,256]{2,1,0:T(8,128)(2,1)}, bf16[2,192,512]{2,1,0:T(8,128)(2,1)}) custom-call(f32[64,128,128]{2,1,0:T(8,128)} %block_x.5, f32[32,128,128]{2,1,0:T(8,128)} %block_y.5, f32[128,128]{1,0:T(8,128)} %reduced_x_hbm.3, f32[64,64]{1,0:T(8,128)} %reduced_y_hbm.3), custom_call_target="tpu_custom_call" | custom-call | flops 16777216 | bytes 2097152 | tf_op jit(solution)/shard_map/carry/pallas_call | solution.py:209
  17.6 0.1 collective-permute-done.1
  17.7 2.4 %collective-permute-start.2 = (f32[4,8,640]{2,1,0:T(8,128)S(1)}, f32[4,8,640]{2,1,0:T(8,128)S(1)}, u32[]{:S(2)}, u32[]{:S(2)}) collective-permute-start(f32[4,8,640]{2,1,0:T(8,128)S(1)} %pad_maximum_fusion.ta_in), channel_id=1, source_target_pairs={{0,1},{1,0},{2,3},{3,2},{4,5},{5,4},{6,7},{7,6},{8,9},{9,8},{10,11... | collective-permute-start | bytes 245768 | tf_op jit(solution)/shard_map/ppermute | solution.py:628
  20.1 2.2 %shares.1 = (f32[8,128]{1,0:T(8,128)}, f32[2,16,2048]{2,1,0:T(8,128)}, bf16[2,16,2048]{2,1,0:T(8,128)(2,1)}) custom-call(f32[64,128,128]{2,1,0:T(8,128)} %block_x.5, f32[32,128,128]{2,1,0:T(8,128)} %block_y.5, f32[128,128]{1,0:T(8,128)} %reduced_x_hbm.3, f32[64,64]{1,0:T(8,128)} %reduced_y_hbm.3, f32[8,4,2048]{2,1,0:T(4,128)} %bitcast.19, s32[8,2048]{1,0:T(8,128)} %bitcast.20), custom_call_target="tpu_custom_call" | custom-call | flops 16777216 | bytes 2097152 | tf_op jit(solution)/shard_map/shares/pallas_call | solution.py:305
  22.3 0.0 collective-permute-done.2.tb_in
  22.3 0.5 %all-to-all-done.tx = f32[16,8,640]{2,1,0:T(8,128)S(1)} async-done(((f32[16,8,640]{2,1,0:T(8,128)}), f32[16,8,640]{2,1,0:T(8,128)S(1)}, u32[]{:S(2)}, u32[]{:S(2)}) %all-to-all-start) | async-done | bytes 327712 | tf_op jit(solution)/shard_map/all_to_all | solution.py:620
  22.9 6.4 %elevation.1 = (f32[3,512,512]{2,1,0:T(8,128)}, f32[640,128]{1,0:T(8,128)}) custom-call(f32[16,8,640]{2,1,0:T(8,128)S(1)} %all-to-all-done.tx, f32[4,8,640]{2,1,0:T(8,128)S(1)} %pad_maximum_fusion.ta_in, f32[4,8,640]{2,1,0:T(8,128)S(1)} %collective-permute-done.2.tb_in, bf16[2,512,256]{2,1,0:T(8,128)(2,1)} %get-tuple-element.21.mx_in, ...), custom_call_target="tpu_custom_call" | custom-call | flops 402653184 | bytes 10485760 | tf_op jit(solution)/shard_map/elevation/pallas_call | solution.py:533
  29.3 6.8 %all-to-all-start.1 = ((f32[640,1,128]{2,1,0:T(1,128)}), f32[640,1,128]{2,1,0:T(1,128)S(1)}, u32[]{:S(2)}, u32[]{:S(2)}) async-start(f32[640,1,128]{2,1,0:T(1,128)} %bitcast.18), calls=%async_computation.1 | async-start | bytes 655360 | tf_op jit(solution)/shard_map/all_to_all | solution.py:632
  36.1 0.7 %slice_bitcast_fusion.1.bottom_in = f32[8,512]{1,0:T(8,128)S(1)} fusion(f32[3,512,512]{2,1,0:T(8,128)} %get-tuple-element.26.fields_in), kind=kLoop, calls=%fused_computation.3 | loop fusion | bytes 32768 | tf_op jit(solution)/shard_map/squeeze | solution.py:587
  36.8 1.0 %slice_bitcast_fusion.edge_in = f32[512,128]{1,0:T(8,128)S(1)} fusion(f32[3,512,512]{2,1,0:T(8,128)} %get-tuple-element.26.fields_in), kind=kLoop, calls=%fused_computation | loop fusion | bytes 524288 | tf_op jit(solution)/shard_map/squeeze | solution.py:588
  37.8 9.9 %all-to-all-done.1 = f32[640,1,128]{2,1,0:T(1,128)S(1)} async-done(((f32[640,1,128]{2,1,0:T(1,128)}), f32[640,1,128]{2,1,0:T(1,128)S(1)}, u32[]{:S(2)}, u32[]{:S(2)}) %all-to-all-start.1) | async-done | bytes 327712 | tf_op jit(solution)/shard_map/all_to_all | solution.py:632
  47.7 1.5 %finish.1 = (f32[3,512,512]{2,1,0:T(8,128)}, f32[1,16]{1,0:T(1,128)}) custom-call(f32[3,512,512]{2,1,0:T(8,128)} %get-tuple-element.26.fields_in, f32[640,128]{1,0:T(8,128)S(1)} %bitcast.14, f32[8,512]{1,0:T(8,128)S(1)} %slice_bitcast_fusion.1.bottom_in, f32[512,128]{1,0:T(8,128)S(1)} %slice_bitcast_fusion.edge_in), custom_call_target="tpu_custom_call", output_to_operand_aliasing={{0}: (0, {})} | custom-call | flops 1048576 | bytes 1048576 | tf_op jit(solution)/shard_map/finish/pallas_call | solution.py:589
  (2 shorter events, 0.0 us)
Async XLA Ops:
  3.3 11.4 %collective-permute-start = (f32[1,8,640]{2,1,0:T(8,128)S(1)}, f32[1,8,640]{2,1,0:T(8,128)S(1)}, u32[]{:S(2)}, u32[]{:S(2)}) collective-permute-start(f32[1,8,640]{2,1,0:T(8,128)S(1)} %bitcast.15), channel_id=1, source_target_pairs={{0,4},{1,5},{2,6},{3,7},{4,0},{5,1},{6,2},{7,3},{8,12},{9,13},{10,... | collective-permute-start | bytes 61448 | tf_op jit(solution)/shard_map/ppermute | solution.py:626
  7.2 15.7 %all-to-all-start = ((f32[16,8,640]{2,1,0:T(8,128)}), f32[16,8,640]{2,1,0:T(8,128)S(1)}, u32[]{:S(2)}, u32[]{:S(2)}) async-start(f32[16,8,640]{2,1,0:T(8,128)} %get-tuple-element.16), calls=%async_computation | async-start | bytes 655360 | tf_op jit(solution)/shard_map/all_to_all | solution.py:620
  14.8 2.9 %collective-permute-start.1 = (f32[2,8,640]{2,1,0:T(8,128)S(1)}, f32[2,8,640]{2,1,0:T(8,128)S(1)}, u32[]{:S(2)}, u32[]{:S(2)}) collective-permute-start(f32[2,8,640]{2,1,0:T(8,128)S(1)} %pad_maximum_fusion.1), channel_id=1, source_target_pairs={{0,2},{1,3},{2,0},{3,1},{4,6},{5,7},{6,4},{7,5},{8,10},{9,11},{10,... | collective-permute-start | bytes 122888 | tf_op jit(solution)/shard_map/ppermute | solution.py:626
  17.7 4.6 %collective-permute-start.2 = (f32[4,8,640]{2,1,0:T(8,128)S(1)}, f32[4,8,640]{2,1,0:T(8,128)S(1)}, u32[]{:S(2)}, u32[]{:S(2)}) collective-permute-start(f32[4,8,640]{2,1,0:T(8,128)S(1)} %pad_maximum_fusion.ta_in), channel_id=1, source_target_pairs={{0,1},{1,0},{2,3},{3,2},{4,5},{5,4},{6,7},{7,6},{8,9},{9,8},{10,11... | collective-permute-start | bytes 245768 | tf_op jit(solution)/shard_map/ppermute | solution.py:628
  29.3 18.4 %all-to-all-start.1 = ((f32[640,1,128]{2,1,0:T(1,128)}), f32[640,1,128]{2,1,0:T(1,128)S(1)}, u32[]{:S(2)}, u32[]{:S(2)}) async-start(f32[640,1,128]{2,1,0:T(1,128)} %bitcast.18), calls=%async_computation.1 | async-start | bytes 655360 | tf_op jit(solution)/shard_map/all_to_all | solution.py:632

commit v6 on v5

--- a/solution.py
+++ b/solution.py
@@ -155,102 +155,34 @@
 
 
 def carry_kernel(
-    block_x, block_y, reduced_x_hbm, reduced_y_hbm, mx_hbm, my_hbm,
-    mx, my, wx, wy, reduced_x, reduced_y, sems, out_sems,
+    block_x, block_y, reduced_x_hbm, reduced_y_hbm, coef_hbm, footprint_hbm,
+    mx_hbm, my_hbm, gside_hbm, share_hbm, at_row_hbm,
+    mx, my, gside, share, at_row, wx, wy, wpx, wpy, reduced_x, reduced_y, coef, footprint, sems, out_sems,
 ):
     u = lax.axis_index("gx")
     v = lax.axis_index("gy")
     nbx = wx.shape[0]
     nby = wy.shape[0]
-    copies = [
-        pltpu.make_async_copy(reduced_x_hbm, reduced_x, sems.at[0]),
-        pltpu.make_async_copy(block_x.at[pl.ds(u * nbx, nbx)], wx, sems.at[1]),
-        pltpu.make_async_copy(reduced_y_hbm, reduced_y, sems.at[2]),
-        pltpu.make_async_copy(block_y.at[pl.ds(v * nby, nby)], wy, sems.at[3]),
-    ]
-    for copy in copies:
-        copy.start()
-    outs = [
-        pltpu.make_async_copy(mx, mx_hbm, out_sems.at[0]),
-        pltpu.make_async_copy(my, my_hbm, out_sems.at[1]),
-    ]
-    for copy in copies[:2]:
-        copy.wait()
-    own_x = reduced_x[pl.ds(pl.multiple_of(u * 8, 8), 8), :]
-    for c in range(nbx):
-        w = wx[c]
-        g = w[:, 0:1] * own_x[2 * c : 2 * c + 1, :] + w[:, K - 1 : K] * own_x[2 * c + 1 : 2 * c + 2, :]
-        for i, part in enumerate(zip(halves(w), halves(g))):
-            mx[i, c * K : (c + 1) * K, :] = jnp.concatenate(part, axis=1)
-    outs[0].start()
-    for copy in copies[2:]:
-        copy.wait()
-    own_y = halves(reduced_y[pl.ds(pl.multiple_of(v * 8, 8), 8), :])
-    sub = iota((8, K), 0)
-    for c in range(nby):
-        turned = wy[c].T
-        across = jnp.where(sub == 2 * c, turned[0:1, :], 0.0)
-        across = jnp.where(sub == 2 * c + 1, turned[K - 1 : K, :], across)
-        g = mm3(own_y, halves(across), TN)
-        for i, part in enumerate(zip(halves(turned), halves(g))):
-            my[i, :, c * K : (c + 1) * K] = jnp.concatenate(part, axis=0)
-    outs[1].start()
-    for copy in outs:
-        copy.wait()
-
-
-def carry(block_x, block_y, reduced_x, reduced_y):
-    nbx = block_x.shape[0] // lax.axis_size("gx")
-    nby = block_y.shape[0] // lax.axis_size("gy")
-    results = [
-        ((2, nbx * K, K + reduced_x.shape[0]), bf16),
-        ((2, K + reduced_y.shape[0], nby * K), bf16),
-    ]
-    return pl.pallas_call(
-        carry_kernel,
-        out_shape=tuple(pltpu.HBM(*result) for result in results),
-        in_specs=[hbm_spec()] * 4,
-        out_specs=(hbm_spec(),) * 2,
-        scratch_shapes=[pltpu.VMEM(*result) for result in results]
-        + [
-            pltpu.VMEM((nbx, K, K), f32),
-            pltpu.VMEM((nby, K, K), f32),
-            pltpu.VMEM(reduced_x.shape, f32),
-            pltpu.VMEM(reduced_y.shape, f32),
-            pltpu.SemaphoreType.DMA((4,)),
-            pltpu.SemaphoreType.DMA((2,)),
-        ],
-        compiler_params=pltpu.CompilerParams(vmem_limit_bytes=16 << 20),
-        cost_estimate=cost(1 << 24, 2 << 20),
-        name="carry",
-    )(*in_hbm(block_x, block_y, reduced_x, reduced_y))
-
-
-def shares_kernel(
-    block_x, block_y, reduced_x_hbm, reduced_y_hbm, coef_hbm, footprint_hbm,
-    gside_hbm, share_hbm, at_row_hbm,
-    gside, share, at_row, wpx, wpy, reduced_x, reduced_y, coef, footprint, sems, out_sems,
-):
-    u = lax.axis_index("gx")
-    v = lax.axis_index("gy")
-    nbx = block_x.shape[0] // lax.axis_size("gx")
-    nby = block_y.shape[0] // lax.axis_size("gy")
     before_x = jnp.maximum(u * nbx - 1, 0)
     before_y = jnp.maximum(v * nby - 1, 0)
     copies = [
         pltpu.make_async_copy(footprint_hbm, footprint, sems.at[0]),
         pltpu.make_async_copy(coef_hbm, coef, sems.at[1]),
         pltpu.make_async_copy(reduced_x_hbm, reduced_x, sems.at[2]),
-        pltpu.make_async_copy(reduced_y_hbm, reduced_y, sems.at[3]),
-        pltpu.make_async_copy(block_x.at[before_x, pl.ds(K - 8, 8), :], wpx, sems.at[4]),
-        pltpu.make_async_copy(block_y.at[before_y, pl.ds(K - 8, 8), :], wpy, sems.at[5]),
+        pltpu.make_async_copy(block_x.at[pl.ds(u * nbx, nbx)], wx, sems.at[3]),
+        pltpu.make_async_copy(reduced_y_hbm, reduced_y, sems.at[4]),
+        pltpu.make_async_copy(block_y.at[pl.ds(v * nby, nby)], wy, sems.at[5]),
+        pltpu.make_async_copy(block_x.at[before_x, pl.ds(K - 8, 8), :], wpx, sems.at[6]),
+        pltpu.make_async_copy(block_y.at[before_y, pl.ds(K - 8, 8), :], wpy, sems.at[7]),
     ]
     for copy in copies:
         copy.start()
     outs = [
         pltpu.make_async_copy(share, share_hbm, out_sems.at[0]),
         pltpu.make_async_copy(at_row, at_row_hbm, out_sems.at[1]),
-        pltpu.make_async_copy(gside, gside_hbm, out_sems.at[2]),
+        pltpu.make_async_copy(mx, mx_hbm, out_sems.at[2]),
+        pltpu.make_async_copy(my, my_hbm, out_sems.at[3]),
+        pltpu.make_async_copy(gside, gside_hbm, out_sems.at[4]),
     ]
     for copy in copies[:2]:
         copy.wait()
@@ -274,61 +206,87 @@
         share[step] = acc
     for copy in outs[:2]:
         copy.start()
-    for copy in copies[2:]:
-        copy.wait()
-
-    def side(w, reduced, index):
-        prev = reduced[pl.ds(pl.multiple_of(jnp.maximum(index - 1, 0) * 8, 8), 8), :]
+    for copy in copies[2:4]:
+        copy.wait()
+    own_x = reduced_x[pl.ds(pl.multiple_of(u * 8, 8), 8), :]
+    prev_x = reduced_x[pl.ds(pl.multiple_of(jnp.maximum(u - 1, 0) * 8, 8), 8), :]
+    for c in range(nbx):
+        w = wx[c]
+        g = w[:, 0:1] * own_x[2 * c : 2 * c + 1, :] + w[:, K - 1 : K] * own_x[2 * c + 1 : 2 * c + 2, :]
+        for i, part in enumerate(zip(halves(w), halves(g))):
+            mx[i, c * K : (c + 1) * K, :] = jnp.concatenate(part, axis=1)
+    outs[2].start()
+    for copy in copies[4:]:
+        copy.wait()
+    own_y = halves(reduced_y[pl.ds(pl.multiple_of(v * 8, 8), 8), :])
+    prev_y = reduced_y[pl.ds(pl.multiple_of(jnp.maximum(v - 1, 0) * 8, 8), 8), :]
+    sub = iota((8, K), 0)
+    for c in range(nby):
+        turned = wy[c].T
+        across = jnp.where(sub == 2 * c, turned[0:1, :], 0.0)
+        across = jnp.where(sub == 2 * c + 1, turned[K - 1 : K, :], across)
+        g = mm3(own_y, halves(across), TN)
+        for i, part in enumerate(zip(halves(turned), halves(g))):
+            my[i, :, c * K : (c + 1) * K] = jnp.concatenate(part, axis=0)
+    outs[3].start()
+
+    def side(w, prev, index):
         width = prev.shape[1]
         g = w[7:8, 0:1] * prev[6:7, :] + w[7:8, K - 1 : K] * prev[7:8, :]
         g = g + (iota((1, width), 1) == index * 8 - 1).astype(f32)
         return jnp.where(index > 0, g, 0.0)
 
     gside[...] = jnp.zeros(gside.shape, f32)
-    gside[0:1, :] = side(wpx[...], reduced_x, u)
-    gside[1:2, : reduced_y.shape[1]] = side(wpy[...], reduced_y, v)
-    outs[2].start()
+    gside[0:1, :] = side(wpx[...], prev_x, u)
+    gside[1:2, : reduced_y.shape[1]] = side(wpy[...], prev_y, v)
+    outs[4].start()
     for copy in outs:
         copy.wait()
 
 
-def shares(block_x, block_y, reduced_x, reduced_y, coef, footprint, wet):
+def carry(block_x, block_y, reduced_x, reduced_y, coef, footprint, wet):
+    nbx = block_x.shape[0] // lax.axis_size("gx")
+    nby = block_y.shape[0] // lax.axis_size("gy")
     coef = coef.transpose(1, 2, 0)
     footprint = footprint.T
     _, modes, count = coef.shape
     tiles_x, tiles_y = wet.shape
     results = [
+        ((2, nbx * K, K + reduced_x.shape[0]), bf16),
+        ((2, K + reduced_y.shape[0], nby * K), bf16),
         ((8, reduced_x.shape[0]), f32),
         ((2, tiles_y * modes, count), f32),
         ((2, tiles_x, count), bf16),
     ]
     return pl.pallas_call(
-        shares_kernel,
+        carry_kernel,
         out_shape=tuple(pltpu.HBM(*result) for result in results),
         in_specs=[hbm_spec()] * 6,
-        out_specs=(hbm_spec(),) * 3,
+        out_specs=(hbm_spec(),) * 5,
         scratch_shapes=[pltpu.VMEM(*result) for result in results]
         + [
+            pltpu.VMEM((nbx, K, K), f32),
+            pltpu.VMEM((nby, K, K), f32),
             pltpu.VMEM((8, K), f32),
             pltpu.VMEM((8, K), f32),
             pltpu.VMEM(reduced_x.shape, f32),
             pltpu.VMEM(reduced_y.shape, f32),
             pltpu.VMEM(coef.shape, f32),
             pltpu.VMEM(footprint.shape, jnp.int32),
-            pltpu.SemaphoreType.DMA((6,)),
-            pltpu.SemaphoreType.DMA((3,)),
+            pltpu.SemaphoreType.DMA((8,)),
+            pltpu.SemaphoreType.DMA((5,)),
         ],
         compiler_params=pltpu.CompilerParams(vmem_limit_bytes=16 << 20),
         cost_estimate=cost(1 << 24, 2 << 20),
-        name="shares",
+        name="carry",
     )(*in_hbm(block_x, block_y, reduced_x, reduced_y, coef, footprint))
 
 
 def elev_kernel(
     tx, ta_in, tb_in, mx_in, my_in, gside_in, share_in, at_row_in, adj, depth, basis_in, wet_in, owner_in,
-    fields_out, parts_out,
+    fields_out, parts_out, erow_out, ecol_out,
     ty, mx, my, gside, share, at_row, planes, dep, basis, wet, owner,
-    elev, fx, fy, tyn, mom, parts, sems, row_sems, out_sems,
+    elev, fx, fy, tyn, mom, parts, erow, ecol, sems, row_sems, out_sems,
 ):
     u = lax.axis_index("gx")
     v = lax.axis_index("gy")
@@ -364,10 +322,9 @@
         for copy in group:
             copy.start()
     txs = halves(jnp.concatenate([tx[d][:, :cols] for d in range(tx.shape[0])], axis=0))
-    parts[...] = jnp.zeros(parts.shape, f32)
     for copy in first:
         copy.wait()
-    devices = parts.shape[0] // 5
+    devices = parts.shape[0]
     count = owner.shape[1]
     slots = count // devices
     own = owner[...]
@@ -399,7 +356,6 @@
     modes, tile_h, tile_w = basis.shape
     per = K // tile_h
     outs = []
-    firsts = []
 
     def send(plane, source, r):
         here = pl.ds(r * K, K)
@@ -463,8 +419,10 @@
             fx[end, :] = fx[end, :] + jnp.where(row[:8] == 7, courant * e[0:1, :], 0.0)
             send(1, fx, r - 1)
         if r == 0:
-            top = e[0:1, :]
-        firsts.append(e[:, :K].T[0:1, :])
+            erow[...] = e[0:1, :]
+            outs.append(pltpu.make_async_copy(erow, erow_out, sems.at[11]))
+            outs[-1].start()
+        ecol[:, here] = e[:, :K].T[0:1, :]
         for a in range(per):
             for w in range(cols // tile_w):
                 tile = e[a * tile_h : (a + 1) * tile_h, w * tile_w : (w + 1) * tile_w]
@@ -474,6 +432,8 @@
                         tile * basis[b], axis=0, keepdims=True
                     )
     send(1, fx, steps - 1)
+    outs.append(pltpu.make_async_copy(ecol, ecol_out, sems.at[12]))
+    outs[-1].start()
     for copy in last[1:]:
         copy.wait()
     tiles_y, tiles_x = wet.shape
@@ -496,23 +456,7 @@
     placed = jnp.concatenate(halves(jnp.where(slot_of, total, 0.0)), axis=0)
     both = mm(device_of, placed, NT)
     sums = both[:, :slots] + both[:, slots:]
-    parts[pl.ds(0, devices, stride=5), :] = jnp.concatenate(
-        [sums, jnp.zeros((devices, K - slots), f32)], axis=1
-    )
-    size_y = lax.axis_size("gy")
-
-    def put(device, line):
-        for p in range(4):
-            parts[pl.ds(device * 5 + 1 + p, 1), :] = line[:, p * K : (p + 1) * K]
-
-    @pl.when(u > 0)
-    def _():
-        put((u - 1) * size_y + v, top)
-
-    @pl.when(v > 0)
-    def _():
-        put(u * size_y + v - 1, jnp.concatenate(firsts, axis=1))
-
+    parts[...] = jnp.concatenate([sums, jnp.zeros((devices, K - slots), f32)], axis=1)
     outs.append(pltpu.make_async_copy(parts, parts_out, sems.at[10]))
     outs[-1].start()
     for copy in outs:
@@ -528,13 +472,14 @@
     owner = owner.reshape(1, -1)
     field = ((rows, cols), f32)
     far = (2 * ta.shape[0], 8, rows + EXTRA)
-    parts = ((devices * 5, K), f32)
+    parts = ((devices, K), f32)
+    halos = [((1, cols), f32), ((1, rows), f32)]
     like = lambda *arrays: [pltpu.VMEM(a.shape, a.dtype) for a in arrays]
     return pl.pallas_call(
         elev_kernel,
-        out_shape=(pltpu.HBM((3, rows, cols), f32), pltpu.HBM(*parts)),
+        out_shape=(pltpu.HBM((3, rows, cols), f32), pltpu.HBM(*parts), *(pltpu.HBM(*h) for h in halos)),
         in_specs=[vmem_spec()] + [pl.BlockSpec(memory_space=pl.ANY)] * 2 + [hbm_spec()] * 10,
-        out_specs=(hbm_spec(),) * 2,
+        out_specs=(hbm_spec(),) * 4,
         scratch_shapes=[pltpu.VMEM(far, f32)]
         + like(*carried)
         + [pltpu.VMEM((3, rows, cols), f32), pltpu.VMEM(*field)]
@@ -544,7 +489,8 @@
             pltpu.VMEM((far[0] * 8, far[2]), f32),
             pltpu.VMEM((rows // tile_h * modes, cols), f32),
             pltpu.VMEM(*parts),
-            pltpu.SemaphoreType.DMA((11,)),
+            *(pltpu.VMEM(*h) for h in halos),
+            pltpu.SemaphoreType.DMA((13,)),
             pltpu.SemaphoreType.DMA((steps, 2)),
             pltpu.SemaphoreType.DMA((steps, 3)),
         ],
@@ -554,18 +500,15 @@
     )(tx, ta, tb, *in_hbm(*carried, adj, depth, basis, wet, owner))
 
 
-def finish_kernel(fields_in, sums, bottom_in, edge_in, fields, grad, bottom, edge, out_sems):
+def finish_kernel(fields_in, sums, hrow, hcol, bottom_in, edge_in, fields, grad, bottom, edge, out_sems):
     u = lax.axis_index("gx")
     v = lax.axis_index("gy")
     size_x = lax.axis_size("gx")
     size_y = lax.axis_size("gy")
     rows, cols = fields.shape[1:]
 
-    def line(device):
-        return jnp.concatenate([sums[pl.ds(device * 5 + 1 + p, 1), :] for p in range(4)], axis=1)
-
-    below = line(jnp.minimum(u + 1, size_x - 1) * size_y + v) * jnp.where(u + 1 < size_x, courant, 0.0)
-    right = line(u * size_y + jnp.minimum(v + 1, size_y - 1)) * jnp.where(v + 1 < size_y, courant, 0.0)
+    below = hrow[...] * jnp.where(u + 1 < size_x, courant, 0.0)
+    right = hcol[...] * jnp.where(v + 1 < size_y, courant, 0.0)
     right = jnp.broadcast_to(right, (8, rows)).T[:, 0:1]
     edge[...] = edge_in[...] + jnp.where(iota((rows, K), 1) == K - 1, right, 0.0)
     bottom[...] = bottom_in[...] + jnp.where(iota((8, cols), 0) == 7, below, 0.0)
@@ -575,21 +518,20 @@
     ]
     for copy in writes:
         copy.start()
-    devices = sums.shape[0] // 5
-    total = jnp.sum(sums[pl.ds(0, devices, stride=5), :], axis=0, keepdims=True)
+    total = jnp.sum(sums[...], axis=0, keepdims=True)
     grad[...] = total[:, : grad.shape[1]]
     for copy in writes:
         copy.wait()
 
 
-def finish(fields, sums, slots):
+def finish(fields, sums, hrow, hcol, slots):
     _, rows, cols = fields.shape
     bottom = fields[1, rows - 8 :, :]
     edge = fields[2, :, cols - K :]
     return pl.pallas_call(
         finish_kernel,
         out_shape=(pltpu.HBM(fields.shape, f32), jax.ShapeDtypeStruct((1, slots), f32)),
-        in_specs=[hbm_spec(), vmem_spec(), vmem_spec(), vmem_spec()],
+        in_specs=[hbm_spec()] + [vmem_spec()] * 5,
         out_specs=(hbm_spec(), vmem_spec()),
         input_output_aliases={0: 0},
         scratch_shapes=[
@@ -600,7 +542,7 @@
         compiler_params=pltpu.CompilerParams(vmem_limit_bytes=16 << 20),
         cost_estimate=cost(1 << 20, 1 << 20),
         name="finish",
-    )(*in_hbm(fields), sums, bottom, edge)
+    )(*in_hbm(fields), sums, hrow, hcol, bottom, edge)
 
 
 def rounds(size):
@@ -609,6 +551,11 @@
 
 def partner(axis, bit):
     return [(i, i ^ bit) for i in range(lax.axis_size(axis))]
+
+
+def previous(axis):
+    size = lax.axis_size(axis)
+    return [(i, (i - 1) % size) for i in range(size)]
 
 
 def body(
@@ -618,22 +565,22 @@
     size_y = lax.axis_size("gy")
     px, py = ends(adj_fields, depth, block_x, block_y, size_x, size_y)
     tx = lax.all_to_all(px, "gx", split_axis=0, concat_axis=0, tiled=True)
-    matrices = carry(block_x, block_y, reduced_x, reduced_y)
-    sides = shares(block_x, block_y, reduced_x, reduced_y, coef, footprint, wet)
+    carried = carry(block_x, block_y, reduced_x, reduced_y, coef, footprint, wet)
     ty = py[None]
     bits = rounds(size_y)
     for bit in bits[:-1]:
         ty = jnp.concatenate([ty, lax.ppermute(ty, "gy", partner("gy", bit))], axis=0)
-    ty, matrices = lax.optimization_barrier((ty, matrices))
+    ty, carried = lax.optimization_barrier((ty, carried))
     ty_far = lax.ppermute(ty, "gy", partner("gy", bits[-1]))
-    carried = (*matrices, *sides)
-    fields, parts = elevation(tx, ty, ty_far, carried, adj_fields, depth, basis, wet, owner)
+    fields, parts, erow, ecol = elevation(tx, ty, ty_far, carried, adj_fields, depth, basis, wet, owner)
     devices = size_x * size_y
+    hrow = lax.ppermute(erow, "gx", previous("gx"))
+    hcol = lax.ppermute(ecol, "gy", previous("gy"))
     sums = lax.all_to_all(
         parts[:, None, :], ("gx", "gy"), split_axis=0, concat_axis=0, tiled=True
     )
     slots = owner.shape[0] // devices
-    adj_before, grad = finish(fields, sums[:, 0, :], slots)
+    adj_before, grad = finish(fields, sums[:, 0, :], hrow, hcol, slots)
     return adj_before, grad.reshape(slots)
 
 

time: 49.6 us -> 46.8 us (0.944)
  waiting for transfers between devices: 10.5 us -> 4.55 us
  starting transfers between devices: 21.1 us -> 26.1 us
  Pallas kernels: 15.1 us -> 13.3 us
    all_to_all x1, waiting for transfers between devices: 9.87 us -> 0.57 us  [body(): lax.all_to_all(parts[:, None, :], ('gx', 'gy'), split_axis=0, concat_axis...]
    ppermute x0 -> x2, starting transfers between devices: none -> 6.13 us  [the longest x1 5.48 us: body(): hrow = lax.ppermute(erow, 'gx', previous('gx'))]
    pallas_call x1 -> x0, Pallas kernels: 2.22 us -> none  [shares(): pl.pallas_call(shares_kernel, out_shape=tuple((pltpu.HBM(*result) for res...]
    all_to_all x1, waiting for transfers between devices: 0.53 us -> 1.84 us  [body(): tx = lax.all_to_all(px, 'gx', split_axis=0, concat_axis=0, tiled=True)]
    ppermute x0 -> x2, waiting for transfers between devices: none -> 1.21 us  [the longest x1 1.21 us: body(): hcol = lax.ppermute(ecol, 'gy', previous('gy'))]
    ppermute x1, waiting for transfers between devices: 0.01 us -> 0.92 us  [body(): ty_far = lax.ppermute(ty, 'gy', partner('gy', bits[-1]))]
    all_to_all x1, starting transfers between devices: 6.81 us -> 6.11 us  [body(): lax.all_to_all(parts[:, None, :], ('gx', 'gy'), split_axis=0, concat_axis...]
    pallas_call x1, Pallas kernels: 2.33 us -> 2.83 us  [carry(): pl.pallas_call(carry_kernel, out_shape=tuple((pltpu.HBM(*result) for resu...]
  transfers between devices with their start and end apart: 5 -> 7, of which waited for: 3 -> 4; matrix products, arithmetic and copies ran while one was open for 3% -> 4% of each run, Pallas kernels for 9% -> 6%
where the time goes in v6:
time: 46.8 us; the launch traced here: 46.4 us
  starting transfers between devices  26.1 us (56%)
  Pallas kernels  13.3 us (28%)
  waiting for transfers between devices  4.55 us (10%)
  local copies, waits for them, and re-layouts  1.69 us (4%)
  between operations  0.71 us (2%)
    all_to_all x1, starting transfers between devices, body(): tx = lax.all_to_all(px, 'gx', split_axis=0, concat_axis=0, tiled=True)  7.6 us
    pallas_call x1, Pallas kernels, elevation(): pl.pallas_call(elev_kernel, out_shape=(pltpu.HBM((3, rows, cols), f32), p...  6.31 us
    all_to_all x1, starting transfers between devices, body(): lax.all_to_all(parts[:, None, :], ('gx', 'gy'), split_axis=0, concat_axis...  6.11 us
    ppermute x1, starting transfers between devices, body(): hrow = lax.ppermute(erow, 'gx', previous('gx'))  5.48 us
    ppermute x2, starting transfers between devices, body(): lax.ppermute(ty, 'gy', partner('gy', bit))  4.3 us
    pallas_call x1, Pallas kernels, carry(): pl.pallas_call(carry_kernel, out_shape=tuple((pltpu.HBM(*result) for resu...  2.83 us
    pallas_call x1, Pallas kernels, ends(): pl.pallas_call(ends_kernel, out_shape=(pltpu.HBM((size_x, *shape), f32),...  2.7 us
    ppermute x1, starting transfers between devices, body(): ty_far = lax.ppermute(ty, 'gy', partner('gy', bits[-1]))  1.98 us
  transfers between devices with their start and end apart: 7, of which 4 were waited for; matrix products, arithmetic and copies ran while one was open for 4% of the time, Pallas kernels for 6%

profile of v6, /device:TPU:1, one launch (start us, length us, event | category | flops | bytes accessed | tf_op | source)
XLA Modules:
  0.0 46.4 jit_solution(9948041416555612913)
XLA Ops:
  0.6 2.7 %ends.1 = (f32[16,8,640]{2,1,0:T(8,128)}, f32[8,640]{1,0:T(8,128)S(1)}) custom-call(f32[3,512,512]{2,1,0:T(8,128)} %adj.3, f32[512,512]{1,0:T(8,128)} %depth.3, f32[64,128,128]{2,1,0:T(8,128)} %block_x.3, f32[32,128,128]{2,1,0:T(8,128)} %block_y.3), custom_call_target="tpu_custom_call" | custom-call | flops 16777216 | bytes 3145728 | tf_op jit(solution)/shard_map/ends/pallas_call | solution.py:130
  3.3 3.8 %collective-permute-start = (f32[1,8,640]{2,1,0:T(8,128)S(1)}, f32[1,8,640]{2,1,0:T(8,128)S(1)}, u32[]{:S(2)}, u32[]{:S(2)}) collective-permute-start(f32[1,8,640]{2,1,0:T(8,128)S(1)} %bitcast.15), channel_id=1, source_target_pairs={{0,4},{1,5},{2,6},{3,7},{4,0},{5,1},{6,2},{7,3},{8,12},{9,13},{10,... | collective-permute-start | bytes 61448 | tf_op jit(solution)/shard_map/ppermute | solution.py:572
  7.2 7.6 %all-to-all-start = ((f32[16,8,640]{2,1,0:T(8,128)}), f32[16,8,640]{2,1,0:T(8,128)S(1)}, u32[]{:S(2)}, u32[]{:S(2)}) async-start(f32[16,8,640]{2,1,0:T(8,128)} %get-tuple-element.21), calls=%async_computation | async-start | bytes 655360 | tf_op jit(solution)/shard_map/all_to_all | solution.py:567
  14.8 0.0 collective-permute-done
  14.8 0.5 %collective-permute-start.1 = (f32[2,8,640]{2,1,0:T(8,128)S(1)}, f32[2,8,640]{2,1,0:T(8,128)S(1)}, u32[]{:S(2)}, u32[]{:S(2)}) collective-permute-start(f32[2,8,640]{2,1,0:T(8,128)S(1)} %pad_maximum_fusion.1), channel_id=1, source_target_pairs={{0,2},{1,3},{2,0},{3,1},{4,6},{5,7},{6,4},{7,5},{8,10},{9,11},{10,... | collective-permute-start | bytes 122888 | tf_op jit(solution)/shard_map/ppermute | solution.py:572
  15.3 2.8 %carry.1 = (bf16[2,512,256]{2,1,0:T(8,128)(2,1)}, bf16[2,192,512]{2,1,0:T(8,128)(2,1)}, f32[8,128]{1,0:T(8,128)}, f32[2,16,2048]{2,1,0:T(8,128)}, bf16[2,16,2048]{2,1,0:T(8,128)(2,1)}) custom-call(f32[64,128,128]{2,1,0:T(8,128)} %block_x.3, f32[32,128,128]{2,1,0:T(8,128)} %block_y.3, f32[128,128]{1,0:T(8,128)} %reduced_x_hbm.1, f32[64,64]{1,0:T(8,128)} %reduced_y_hbm.1, ...), custom_call_target="tpu_custom_call" | custom-call | flops 16777216 | bytes 2097152 | tf_op jit(solution)/shard_map/carry/pallas_call | solution.py:261
  18.1 0.0 collective-permute-done.1
  18.1 2.0 %collective-permute-start.2 = (f32[4,8,640]{2,1,0:T(8,128)S(1)}, f32[4,8,640]{2,1,0:T(8,128)S(1)}, u32[]{:S(2)}, u32[]{:S(2)}) collective-permute-start(f32[4,8,640]{2,1,0:T(8,128)S(1)} %pad_maximum_fusion.ta_in), channel_id=1, source_target_pairs={{0,1},{1,0},{2,3},{3,2},{4,5},{5,4},{6,7},{7,6},{8,9},{9,8},{10,11... | collective-permute-start | bytes 245768 | tf_op jit(solution)/shard_map/ppermute | solution.py:574
  20.1 0.9 %collective-permute-done.2.tb_in = f32[4,8,640]{2,1,0:T(8,128)S(1)} collective-permute-done((f32[4,8,640]{2,1,0:T(8,128)S(1)}, f32[4,8,640]{2,1,0:T(8,128)S(1)}, u32[]{:S(2)}, u32[]{:S(2)}) %collective-permute-start.2) | collective-permute-done | bytes 81952 | tf_op jit(solution)/shard_map/ppermute | solution.py:574
  21.0 1.8 %all-to-all-done.tx = f32[16,8,640]{2,1,0:T(8,128)S(1)} async-done(((f32[16,8,640]{2,1,0:T(8,128)}), f32[16,8,640]{2,1,0:T(8,128)S(1)}, u32[]{:S(2)}, u32[]{:S(2)}) %all-to-all-start) | async-done | bytes 327712 | tf_op jit(solution)/shard_map/all_to_all | solution.py:567
  22.9 6.3 %elevation.1 = (f32[3,512,512]{2,1,0:T(8,128)}, f32[128,128]{1,0:T(8,128)}, f32[1,512]{1,0:T(1,128)}, f32[1,512]{1,0:T(1,128)}) custom-call(f32[16,8,640]{2,1,0:T(8,128)S(1)} %all-to-all-done.tx, f32[4,8,640]{2,1,0:T(8,128)S(1)} %pad_maximum_fusion.ta_in, f32[4,8,640]{2,1,0:T(8,128)S(1)} %collective-permute-done.2.tb_in, ...), custom_call_target="tpu_custom_call" | custom-call | flops 402653184 | bytes 10485760 | tf_op jit(solution)/shard_map/elevation/pallas_call | solution.py:478
  29.2 6.1 %all-to-all-start.1 = ((f32[128,1,128]{2,1,0:T(1,128)}), f32[128,1,128]{2,1,0:T(1,128)S(1)}, u32[]{:S(2)}, u32[]{:S(2)}) async-start(f32[128,1,128]{2,1,0:T(1,128)} %bitcast.20), calls=%async_computation.1 | async-start | bytes 131072 | tf_op jit(solution)/shard_map/all_to_all | solution.py:579
  35.3 5.5 %collective-permute-start.3 = (f32[1,512]{1,0:T(1,128)}, f32[1,512]{1,0:T(1,128)S(1)}, u32[]{:S(2)}, u32[]{:S(2)}) collective-permute-start(f32[1,512]{1,0:T(1,128)} %get-tuple-element.36), channel_id=1, source_target_pairs={{0,120},{8,0},{16,8},{24,16},{32,24},{40,32},{48,40},{56,48},{64,5... | collective-permute-start | bytes 6152 | tf_op jit(solution)/shard_map/ppermute | solution.py:577
  40.8 0.6 %collective-permute-start.4 = (f32[1,512]{1,0:T(1,128)}, f32[1,512]{1,0:T(1,128)S(1)}, u32[]{:S(2)}, u32[]{:S(2)}) collective-permute-start(f32[1,512]{1,0:T(1,128)} %get-tuple-element.37), channel_id=1, source_target_pairs={{0,7},{1,0},{2,1},{3,2},{4,3},{5,4},{6,5},{7,6},{8,15},{9,8},{10,9... | collective-permute-start | bytes 6152 | tf_op jit(solution)/shard_map/ppermute | solution.py:578
  41.4 1.0 %slice_bitcast_fusion.edge_in = f32[512,128]{1,0:T(8,128)S(1)} fusion(f32[3,512,512]{2,1,0:T(8,128)} %get-tuple-element.34.fields_in), kind=kLoop, calls=%fused_computation | loop fusion | bytes 524288 | tf_op jit(solution)/shard_map/squeeze | solution.py:530
  42.4 0.7 %slice_bitcast_fusion.1.bottom_in = f32[8,512]{1,0:T(8,128)S(1)} fusion(f32[3,512,512]{2,1,0:T(8,128)} %get-tuple-element.34.fields_in), kind=kLoop, calls=%fused_computation.3 | loop fusion | bytes 32768 | tf_op jit(solution)/shard_map/squeeze | solution.py:529
  43.1 0.0 collective-permute-done.3.hrow
  43.1 1.2 %collective-permute-done.4.hcol = f32[1,512]{1,0:T(1,128)S(1)} collective-permute-done((f32[1,512]{1,0:T(1,128)}, f32[1,512]{1,0:T(1,128)S(1)}, u32[]{:S(2)}, u32[]{:S(2)}) %collective-permute-start.4) | collective-permute-done | bytes 2080 | tf_op jit(solution)/shard_map/ppermute | solution.py:578
  44.4 0.6 %all-to-all-done.1 = f32[128,1,128]{2,1,0:T(1,128)S(1)} async-done(((f32[128,1,128]{2,1,0:T(1,128)}), f32[128,1,128]{2,1,0:T(1,128)S(1)}, u32[]{:S(2)}, u32[]{:S(2)}) %all-to-all-start.1) | async-done | bytes 65568 | tf_op jit(solution)/shard_map/all_to_all | solution.py:579
  44.9 1.5 %finish.1 = (f32[3,512,512]{2,1,0:T(8,128)}, f32[1,16]{1,0:T(1,128)}) custom-call(f32[3,512,512]{2,1,0:T(8,128)} %get-tuple-element.34.fields_in, f32[128,128]{1,0:T(8,128)S(1)} %bitcast.14, f32[1,512]{1,0:T(1,128)S(1)} %collective-permute-done.3.hrow, f32[1,512]{1,0:T(1,128)S(1)} %collective-permute-done.4.hcol, ...), custom_call_target="tpu_custom_call", output_to_operand_aliasing={{0}: (0, {})} | custom-call | flops 1048576 | bytes 1048576 | tf_op jit(solution)/shard_map/finish/pallas_call | solution.py:531
  (2 shorter events, 0.0 us)
Async XLA Ops:
  3.3 11.4 %collective-permute-start = (f32[1,8,640]{2,1,0:T(8,128)S(1)}, f32[1,8,640]{2,1,0:T(8,128)S(1)}, u32[]{:S(2)}, u32[]{:S(2)}) collective-permute-start(f32[1,8,640]{2,1,0:T(8,128)S(1)} %bitcast.15), channel_id=1, source_target_pairs={{0,4},{1,5},{2,6},{3,7},{4,0},{5,1},{6,2},{7,3},{8,12},{9,13},{10,... | collective-permute-start | bytes 61448 | tf_op jit(solution)/shard_map/ppermute | solution.py:572
  7.2 15.7 %all-to-all-start = ((f32[16,8,640]{2,1,0:T(8,128)}), f32[16,8,640]{2,1,0:T(8,128)S(1)}, u32[]{:S(2)}, u32[]{:S(2)}) async-start(f32[16,8,640]{2,1,0:T(8,128)} %get-tuple-element.21), calls=%async_computation | async-start | bytes 655360 | tf_op jit(solution)/shard_map/all_to_all | solution.py:567
  14.8 3.3 %collective-permute-start.1 = (f32[2,8,640]{2,1,0:T(8,128)S(1)}, f32[2,8,640]{2,1,0:T(8,128)S(1)}, u32[]{:S(2)}, u32[]{:S(2)}) collective-permute-start(f32[2,8,640]{2,1,0:T(8,128)S(1)} %pad_maximum_fusion.1), channel_id=1, source_target_pairs={{0,2},{1,3},{2,0},{3,1},{4,6},{5,7},{6,4},{7,5},{8,10},{9,11},{10,... | collective-permute-start | bytes 122888 | tf_op jit(solution)/shard_map/ppermute | solution.py:572
  18.1 2.9 %collective-permute-start.2 = (f32[4,8,640]{2,1,0:T(8,128)S(1)}, f32[4,8,640]{2,1,0:T(8,128)S(1)}, u32[]{:S(2)}, u32[]{:S(2)}) collective-permute-start(f32[4,8,640]{2,1,0:T(8,128)S(1)} %pad_maximum_fusion.ta_in), channel_id=1, source_target_pairs={{0,1},{1,0},{2,3},{3,2},{4,5},{5,4},{6,7},{7,6},{8,9},{9,8},{10,11... | collective-permute-start | bytes 245768 | tf_op jit(solution)/shard_map/ppermute | solution.py:574
  29.2 15.7 %all-to-all-start.1 = ((f32[128,1,128]{2,1,0:T(1,128)}), f32[128,1,128]{2,1,0:T(1,128)S(1)}, u32[]{:S(2)}, u32[]{:S(2)}) async-start(f32[128,1,128]{2,1,0:T(1,128)} %bitcast.20), calls=%async_computation.1 | async-start | bytes 131072 | tf_op jit(solution)/shard_map/all_to_all | solution.py:579
  35.3 7.8 %collective-permute-start.3 = (f32[1,512]{1,0:T(1,128)}, f32[1,512]{1,0:T(1,128)S(1)}, u32[]{:S(2)}, u32[]{:S(2)}) collective-permute-start(f32[1,512]{1,0:T(1,128)} %get-tuple-element.36), channel_id=1, source_target_pairs={{0,120},{8,0},{16,8},{24,16},{32,24},{40,32},{48,40},{56,48},{64,5... | collective-permute-start | bytes 6152 | tf_op jit(solution)/shard_map/ppermute | solution.py:577
  40.8 3.5 %collective-permute-start.4 = (f32[1,512]{1,0:T(1,128)}, f32[1,512]{1,0:T(1,128)S(1)}, u32[]{:S(2)}, u32[]{:S(2)}) collective-permute-start(f32[1,512]{1,0:T(1,128)} %get-tuple-element.37), channel_id=1, source_target_pairs={{0,7},{1,0},{2,1},{3,2},{4,3},{5,4},{6,5},{7,6},{8,15},{9,8},{10,9... | collective-permute-start | bytes 6152 | tf_op jit(solution)/shard_map/ppermute | solution.py:578

commit v7 on v6

--- a/solution.py
+++ b/solution.py
@@ -277,13 +277,13 @@
             pltpu.SemaphoreType.DMA((5,)),
         ],
         compiler_params=pltpu.CompilerParams(vmem_limit_bytes=16 << 20),
-        cost_estimate=cost(1 << 24, 2 << 20),
+        cost_estimate=cost(1 << 36, 2 << 20),
         name="carry",
     )(*in_hbm(block_x, block_y, reduced_x, reduced_y, coef, footprint))
 
 
 def elev_kernel(
-    tx, ta_in, tb_in, mx_in, my_in, gside_in, share_in, at_row_in, adj, depth, basis_in, wet_in, owner_in,
+    tx, t0, t1, t2, t3, mx_in, my_in, gside_in, share_in, at_row_in, adj, depth, basis_in, wet_in, owner_in,
     fields_out, parts_out, erow_out, ecol_out,
     ty, mx, my, gside, share, at_row, planes, dep, basis, wet, owner,
     elev, fx, fy, tyn, mom, parts, erow, ecol, sems, row_sems, out_sems,
@@ -292,10 +292,9 @@
     v = lax.axis_index("gy")
     rows, cols = dep.shape
     steps = rows // K
-    half = ta_in.shape[0]
+    near = (t0, t1, t2, t3)
     first = [
-        pltpu.make_async_copy(ta_in, ty.at[pl.ds(0, half)], sems.at[0]),
-        pltpu.make_async_copy(tb_in, ty.at[pl.ds(half, half)], sems.at[1]),
+        *(pltpu.make_async_copy(part, ty.at[i], sems.at[13 + i]) for i, part in enumerate(near)),
         pltpu.make_async_copy(gside_in, gside, sems.at[2]),
         pltpu.make_async_copy(owner_in, owner, sems.at[3]),
     ]
@@ -331,12 +330,9 @@
     device_of = iota((devices, count), 0) == lax.shift_right_logical(own, slots.bit_length() - 1)
     device_of = device_of.astype(f32).astype(bf16)
     slot_of = iota((slots, count), 0) == (own & (slots - 1))
-    for j in range(2 * half):
+    for j in range(ty.shape[0] * ty.shape[1]):
         far = j ^ v
-        place = 0
-        for i, bit in enumerate(rounds(2 * half)):
-            place = place | (((far // bit) & 1) << i)
-        tyn[j * 8 : (j + 1) * 8, :] = ty[place]
+        tyn[j * 8 : (j + 1) * 8, :] = ty[far & (ty.shape[0] - 1), far // ty.shape[0]]
     ty_all = tyn[:, :rows]
     tys = halves(ty_all)
     tyt = halves(ty_all.T)
@@ -463,7 +459,7 @@
         copy.wait()
 
 
-def elevation(tx, ta, tb, carried, adj, depth, basis, wet, owner):
+def elevation(tx, near, carried, adj, depth, basis, wet, owner):
     rows, cols = depth.shape
     modes, tile_h, tile_w = basis.shape
     devices = lax.axis_size("gx") * lax.axis_size("gy")
@@ -471,14 +467,14 @@
     wet = wet.T
     owner = owner.reshape(1, -1)
     field = ((rows, cols), f32)
-    far = (2 * ta.shape[0], 8, rows + EXTRA)
+    far = (len(near), *near[0].shape)
     parts = ((devices, K), f32)
     halos = [((1, cols), f32), ((1, rows), f32)]
     like = lambda *arrays: [pltpu.VMEM(a.shape, a.dtype) for a in arrays]
     return pl.pallas_call(
         elev_kernel,
         out_shape=(pltpu.HBM((3, rows, cols), f32), pltpu.HBM(*parts), *(pltpu.HBM(*h) for h in halos)),
-        in_specs=[vmem_spec()] + [pl.BlockSpec(memory_space=pl.ANY)] * 2 + [hbm_spec()] * 10,
+        in_specs=[vmem_spec()] + [pl.BlockSpec(memory_space=pl.ANY)] * 4 + [hbm_spec()] * 10,
         out_specs=(hbm_spec(),) * 4,
         scratch_shapes=[pltpu.VMEM(far, f32)]
         + like(*carried)
@@ -486,18 +482,18 @@
         + like(basis, wet, owner)
         + [pltpu.VMEM(*field)] * 3
         + [
-            pltpu.VMEM((far[0] * 8, far[2]), f32),
+            pltpu.VMEM((far[0] * far[1] * 8, far[3]), f32),
             pltpu.VMEM((rows // tile_h * modes, cols), f32),
             pltpu.VMEM(*parts),
             *(pltpu.VMEM(*h) for h in halos),
-            pltpu.SemaphoreType.DMA((13,)),
+            pltpu.SemaphoreType.DMA((17,)),
             pltpu.SemaphoreType.DMA((steps, 2)),
             pltpu.SemaphoreType.DMA((steps, 3)),
         ],
         compiler_params=pltpu.CompilerParams(vmem_limit_bytes=32 << 20),
         cost_estimate=cost(12 * rows * cols * K, 10 << 20),
         name="elevation",
-    )(tx, ta, tb, *in_hbm(*carried, adj, depth, basis, wet, owner))
+    )(tx, *near, *in_hbm(*carried, adj, depth, basis, wet, owner))
 
 
 def finish_kernel(fields_in, sums, hrow, hcol, bottom_in, edge_in, fields, grad, bottom, edge, out_sems):
@@ -545,10 +541,6 @@
     )(*in_hbm(fields), sums, hrow, hcol, bottom, edge)
 
 
-def rounds(size):
-    return [size >> i for i in range(1, size.bit_length())]
-
-
 def partner(axis, bit):
     return [(i, i ^ bit) for i in range(lax.axis_size(axis))]
 
@@ -567,12 +559,9 @@
     tx = lax.all_to_all(px, "gx", split_axis=0, concat_axis=0, tiled=True)
     carried = carry(block_x, block_y, reduced_x, reduced_y, coef, footprint, wet)
     ty = py[None]
-    bits = rounds(size_y)
-    for bit in bits[:-1]:
-        ty = jnp.concatenate([ty, lax.ppermute(ty, "gy", partner("gy", bit))], axis=0)
-    ty, carried = lax.optimization_barrier((ty, carried))
-    ty_far = lax.ppermute(ty, "gy", partner("gy", bits[-1]))
-    fields, parts, erow, ecol = elevation(tx, ty, ty_far, carried, adj_fields, depth, basis, wet, owner)
+    ty = jnp.concatenate([ty, lax.ppermute(ty, "gy", partner("gy", size_y // 2))], axis=0)
+    near = [ty] + [lax.ppermute(ty, "gy", partner("gy", bits)) for bits in range(1, size_y // 2)]
+    fields, parts, erow, ecol = elevation(tx, near, carried, adj_fields, depth, basis, wet, owner)
     devices = size_x * size_y
     hrow = lax.ppermute(erow, "gx", previous("gx"))
     hcol = lax.ppermute(ecol, "gy", previous("gy"))

time: 46.8 us -> 46.4 us (level)
    ppermute x3 -> x4, waiting for transfers between devices: 0.93 us -> 0.01 us  [the longest x3 0.01 us: body(): lax.ppermute(ty, 'gy', partner('gy', bits))]
    all_to_all x1, waiting for transfers between devices: 1.84 us -> 2.55 us  [body(): tx = lax.all_to_all(px, 'gx', split_axis=0, concat_axis=0, tiled=True)]
    all_to_all x1, starting transfers between devices: 6.11 us -> 5.58 us  [body(): lax.all_to_all(parts[:, None, :], ('gx', 'gy'), split_axis=0, concat_axis...]
    ppermute x3 -> x4, starting transfers between devices: 6.28 us -> 6.49 us  [the longest x1 3.82 us: body(): lax.ppermute(ty, 'gy', partner('gy', size_y // 2))]
  transfers between devices with their start and end apart: 7 -> 8, of which waited for: 4 -> 3; matrix products, arithmetic and copies ran while one was open for 4% -> 4% of each run, Pallas kernels for 6% -> 6%
where the time goes in v7:
time: 46.4 us; the launch traced here: 46 us
  starting transfers between devices  25.9 us (56%)
  Pallas kernels  13.4 us (29%)
  waiting for transfers between devices  4.35 us (9%)
  local copies, waits for them, and re-layouts  1.69 us (4%)
  between operations  0.72 us (2%)
    all_to_all x1, starting transfers between devices, body(): tx = lax.all_to_all(px, 'gx', split_axis=0, concat_axis=0, tiled=True)  7.6 us
    pallas_call x1, Pallas kernels, elevation(): pl.pallas_call(elev_kernel, out_shape=(pltpu.HBM((3, rows, cols), f32), p...  6.34 us
    ppermute x1, starting transfers between devices, body(): hrow = lax.ppermute(erow, 'gx', previous('gx'))  5.62 us
    all_to_all x1, starting transfers between devices, body(): lax.all_to_all(parts[:, None, :], ('gx', 'gy'), split_axis=0, concat_axis...  5.58 us
    ppermute x1, starting transfers between devices, body(): lax.ppermute(ty, 'gy', partner('gy', size_y // 2))  3.82 us
    pallas_call x1, Pallas kernels, carry(): pl.pallas_call(carry_kernel, out_shape=tuple((pltpu.HBM(*result) for resu...  2.83 us
    pallas_call x1, Pallas kernels, ends(): pl.pallas_call(ends_kernel, out_shape=(pltpu.HBM((size_x, *shape), f32),...  2.7 us
    ppermute x3, starting transfers between devices, body(): lax.ppermute(ty, 'gy', partner('gy', bits))  2.67 us
  transfers between devices with their start and end apart: 8, of which 3 were waited for; matrix products, arithmetic and copies ran while one was open for 4% of the time, Pallas kernels for 6%

profile of v7, /device:TPU:1, one launch (start us, length us, event | category | flops | bytes accessed | tf_op | source)
XLA Modules:
  0.0 46.0 jit_solution(5424014871743762361)
XLA Ops:
  0.6 2.7 %ends.1 = (f32[16,8,640]{2,1,0:T(8,128)}, f32[8,640]{1,0:T(8,128)S(1)}) custom-call(f32[3,512,512]{2,1,0:T(8,128)} %adj.3, f32[512,512]{1,0:T(8,128)} %depth.3, f32[64,128,128]{2,1,0:T(8,128)} %block_x.3, f32[32,128,128]{2,1,0:T(8,128)} %block_y.3), custom_call_target="tpu_custom_call" | custom-call | flops 16777216 | bytes 3145728 | tf_op jit(solution)/shard_map/ends/pallas_call | solution.py:130
  3.3 3.8 %collective-permute-start = (f32[1,8,640]{2,1,0:T(8,128)S(1)}, f32[1,8,640]{2,1,0:T(8,128)S(1)}, u32[]{:S(2)}, u32[]{:S(2)}) collective-permute-start(f32[1,8,640]{2,1,0:T(8,128)S(1)} %bitcast.15), channel_id=1, source_target_pairs={{0,4},{1,5},{2,6},{3,7},{4,0},{5,1},{6,2},{7,3},{8,12},{9,13},{10,... | collective-permute-start | bytes 61448 | tf_op jit(solution)/shard_map/ppermute | solution.py:562
  7.2 7.6 %all-to-all-start = ((f32[16,8,640]{2,1,0:T(8,128)}), f32[16,8,640]{2,1,0:T(8,128)S(1)}, u32[]{:S(2)}, u32[]{:S(2)}) async-start(f32[16,8,640]{2,1,0:T(8,128)} %get-tuple-element.15), calls=%async_computation | async-start | bytes 655360 | tf_op jit(solution)/shard_map/all_to_all | solution.py:559
  14.8 0.0 collective-permute-done
  14.8 1.6 %collective-permute-start.3 = (f32[2,8,640]{2,1,0:T(8,128)S(1)}, f32[2,8,640]{2,1,0:T(8,128)S(1)}, u32[]{:S(2)}, u32[]{:S(2)}) collective-permute-start(f32[2,8,640]{2,1,0:T(8,128)S(1)} %pad_maximum_fusion.t0), channel_id=1, source_target_pairs={{0,3},{1,2},{2,1},{3,0},{4,7},{5,6},{6,5},{7,4},{8,11},{9,10},{10,... | collective-permute-start | bytes 122888 | tf_op jit(solution)/shard_map/ppermute | solution.py:563
  16.4 1.1 %collective-permute-start.2 = (f32[2,8,640]{2,1,0:T(8,128)S(1)}, f32[2,8,640]{2,1,0:T(8,128)S(1)}, u32[]{:S(2)}, u32[]{:S(2)}) collective-permute-start(f32[2,8,640]{2,1,0:T(8,128)S(1)} %pad_maximum_fusion.t0), channel_id=1, source_target_pairs={{0,2},{1,3},{2,0},{3,1},{4,6},{5,7},{6,4},{7,5},{8,10},{9,11},{10,... | collective-permute-start | bytes 122888 | tf_op jit(solution)/shard_map/ppermute | solution.py:563
  17.5 0.0 collective-permute-start.1
  17.5 2.8 %carry.1 = (bf16[2,512,256]{2,1,0:T(8,128)(2,1)}, bf16[2,192,512]{2,1,0:T(8,128)(2,1)}, f32[8,128]{1,0:T(8,128)}, f32[2,16,2048]{2,1,0:T(8,128)}, bf16[2,16,2048]{2,1,0:T(8,128)(2,1)}) custom-call(f32[64,128,128]{2,1,0:T(8,128)} %block_x.3, f32[32,128,128]{2,1,0:T(8,128)} %block_y.3, f32[128,128]{1,0:T(8,128)} %reduced_x_hbm.1, f32[64,64]{1,0:T(8,128)} %reduced_y_hbm.1, ...), custom_call_target="tpu_custom_call" | custom-call | flops 68719476736 | bytes 2097152 | tf_op jit(solution)/shard_map/carry/pallas_call | solution.py:261
  20.3 0.0 collective-permute-done.3.t3
  20.3 0.0 collective-permute-done.2.t2
  20.3 0.0 collective-permute-done.1.t1
  20.3 2.5 %all-to-all-done.tx = f32[16,8,640]{2,1,0:T(8,128)S(1)} async-done(((f32[16,8,640]{2,1,0:T(8,128)}), f32[16,8,640]{2,1,0:T(8,128)S(1)}, u32[]{:S(2)}, u32[]{:S(2)}) %all-to-all-start) | async-done | bytes 327712 | tf_op jit(solution)/shard_map/all_to_all | solution.py:559
  22.9 6.3 %elevation.1 = (f32[3,512,512]{2,1,0:T(8,128)}, f32[128,128]{1,0:T(8,128)}, f32[1,512]{1,0:T(1,128)}, f32[1,512]{1,0:T(1,128)}) custom-call(f32[16,8,640]{2,1,0:T(8,128)S(1)} %all-to-all-done.tx, f32[2,8,640]{2,1,0:T(8,128)S(1)} %pad_maximum_fusion.t0, f32[2,8,640]{2,1,0:T(8,128)S(1)} %collective-permute-done.1.t1, ...), custom_call_target="tpu_custom_call" | custom-call | flops 402653184 | bytes 10485760 | tf_op jit(solution)/shard_map/elevation/pallas_call | solution.py:474
  29.2 5.6 %all-to-all-start.1 = ((f32[128,1,128]{2,1,0:T(1,128)}), f32[128,1,128]{2,1,0:T(1,128)S(1)}, u32[]{:S(2)}, u32[]{:S(2)}) async-start(f32[128,1,128]{2,1,0:T(1,128)} %bitcast.17), calls=%async_computation.1 | async-start | bytes 131072 | tf_op jit(solution)/shard_map/all_to_all | solution.py:568
  34.8 5.6 %collective-permute-start.4 = (f32[1,512]{1,0:T(1,128)}, f32[1,512]{1,0:T(1,128)S(1)}, u32[]{:S(2)}, u32[]{:S(2)}) collective-permute-start(f32[1,512]{1,0:T(1,128)} %get-tuple-element.24), channel_id=1, source_target_pairs={{0,120},{8,0},{16,8},{24,16},{32,24},{40,32},{48,40},{56,48},{64,5... | collective-permute-start | bytes 6152 | tf_op jit(solution)/shard_map/ppermute | solution.py:566
  40.4 0.6 %collective-permute-start.5 = (f32[1,512]{1,0:T(1,128)}, f32[1,512]{1,0:T(1,128)S(1)}, u32[]{:S(2)}, u32[]{:S(2)}) collective-permute-start(f32[1,512]{1,0:T(1,128)} %get-tuple-element.25), channel_id=1, source_target_pairs={{0,7},{1,0},{2,1},{3,2},{4,3},{5,4},{6,5},{7,6},{8,15},{9,8},{10,9... | collective-permute-start | bytes 6152 | tf_op jit(solution)/shard_map/ppermute | solution.py:567
  41.1 1.0 %slice_bitcast_fusion.edge_in = f32[512,128]{1,0:T(8,128)S(1)} fusion(f32[3,512,512]{2,1,0:T(8,128)} %get-tuple-element.22.fields_in), kind=kLoop, calls=%fused_computation | loop fusion | bytes 524288 | tf_op jit(solution)/shard_map/squeeze | solution.py:526
  42.0 0.7 %slice_bitcast_fusion.1.bottom_in = f32[8,512]{1,0:T(8,128)S(1)} fusion(f32[3,512,512]{2,1,0:T(8,128)} %get-tuple-element.22.fields_in), kind=kLoop, calls=%fused_computation.2 | loop fusion | bytes 32768 | tf_op jit(solution)/shard_map/squeeze | solution.py:525
  42.8 0.0 collective-permute-done.4.hrow
  42.8 1.2 %collective-permute-done.5.hcol = f32[1,512]{1,0:T(1,128)S(1)} collective-permute-done((f32[1,512]{1,0:T(1,128)}, f32[1,512]{1,0:T(1,128)S(1)}, u32[]{:S(2)}, u32[]{:S(2)}) %collective-permute-start.5) | collective-permute-done | bytes 2080 | tf_op jit(solution)/shard_map/ppermute | solution.py:567
  44.0 0.6 %all-to-all-done.1 = f32[128,1,128]{2,1,0:T(1,128)S(1)} async-done(((f32[128,1,128]{2,1,0:T(1,128)}), f32[128,1,128]{2,1,0:T(1,128)S(1)}, u32[]{:S(2)}, u32[]{:S(2)}) %all-to-all-start.1) | async-done | bytes 65568 | tf_op jit(solution)/shard_map/all_to_all | solution.py:568
  44.6 1.5 %finish.1 = (f32[3,512,512]{2,1,0:T(8,128)}, f32[1,16]{1,0:T(1,128)}) custom-call(f32[3,512,512]{2,1,0:T(8,128)} %get-tuple-element.22.fields_in, f32[128,128]{1,0:T(8,128)S(1)} %bitcast.14, f32[1,512]{1,0:T(1,128)S(1)} %collective-permute-done.4.hrow, f32[1,512]{1,0:T(1,128)S(1)} %collective-permute-done.5.hcol, ...), custom_call_target="tpu_custom_call", output_to_operand_aliasing={{0}: (0, {})} | custom-call | flops 1048576 | bytes 1048576 | tf_op jit(solution)/shard_map/finish/pallas_call | solution.py:527
  (1 shorter events, 0.0 us)
Async XLA Ops:
  3.3 11.4 %collective-permute-start = (f32[1,8,640]{2,1,0:T(8,128)S(1)}, f32[1,8,640]{2,1,0:T(8,128)S(1)}, u32[]{:S(2)}, u32[]{:S(2)}) collective-permute-start(f32[1,8,640]{2,1,0:T(8,128)S(1)} %bitcast.15), channel_id=1, source_target_pairs={{0,4},{1,5},{2,6},{3,7},{4,0},{5,1},{6,2},{7,3},{8,12},{9,13},{10,... | collective-permute-start | bytes 61448 | tf_op jit(solution)/shard_map/ppermute | solution.py:562
  7.2 15.7 %all-to-all-start = ((f32[16,8,640]{2,1,0:T(8,128)}), f32[16,8,640]{2,1,0:T(8,128)S(1)}, u32[]{:S(2)}, u32[]{:S(2)}) async-start(f32[16,8,640]{2,1,0:T(8,128)} %get-tuple-element.15), calls=%async_computation | async-start | bytes 655360 | tf_op jit(solution)/shard_map/all_to_all | solution.py:559
  14.8 5.5 %collective-permute-start.3 = (f32[2,8,640]{2,1,0:T(8,128)S(1)}, f32[2,8,640]{2,1,0:T(8,128)S(1)}, u32[]{:S(2)}, u32[]{:S(2)}) collective-permute-start(f32[2,8,640]{2,1,0:T(8,128)S(1)} %pad_maximum_fusion.t0), channel_id=1, source_target_pairs={{0,3},{1,2},{2,1},{3,0},{4,7},{5,6},{6,5},{7,4},{8,11},{9,10},{10,... | collective-permute-start | bytes 122888 | tf_op jit(solution)/shard_map/ppermute | solution.py:563
  16.4 3.9 %collective-permute-start.2 = (f32[2,8,640]{2,1,0:T(8,128)S(1)}, f32[2,8,640]{2,1,0:T(8,128)S(1)}, u32[]{:S(2)}, u32[]{:S(2)}) collective-permute-start(f32[2,8,640]{2,1,0:T(8,128)S(1)} %pad_maximum_fusion.t0), channel_id=1, source_target_pairs={{0,2},{1,3},{2,0},{3,1},{4,6},{5,7},{6,4},{7,5},{8,10},{9,11},{10,... | collective-permute-start | bytes 122888 | tf_op jit(solution)/shard_map/ppermute | solution.py:563
  17.5 2.9 %collective-permute-start.1 = (f32[2,8,640]{2,1,0:T(8,128)S(1)}, f32[2,8,640]{2,1,0:T(8,128)S(1)}, u32[]{:S(2)}, u32[]{:S(2)}) collective-permute-start(f32[2,8,640]{2,1,0:T(8,128)S(1)} %pad_maximum_fusion.t0), channel_id=1, source_target_pairs={{0,1},{1,0},{2,3},{3,2},{4,5},{5,4},{6,7},{7,6},{8,9},{9,8},{10,11... | collective-permute-start | bytes 122888 | tf_op jit(solution)/shard_map/ppermute | solution.py:563
  29.2 15.3 %all-to-all-start.1 = ((f32[128,1,128]{2,1,0:T(1,128)}), f32[128,1,128]{2,1,0:T(1,128)S(1)}, u32[]{:S(2)}, u32[]{:S(2)}) async-start(f32[128,1,128]{2,1,0:T(1,128)} %bitcast.17), calls=%async_computation.1 | async-start | bytes 131072 | tf_op jit(solution)/shard_map/all_to_all | solution.py:568
  34.8 8.0 %collective-permute-start.4 = (f32[1,512]{1,0:T(1,128)}, f32[1,512]{1,0:T(1,128)S(1)}, u32[]{:S(2)}, u32[]{:S(2)}) collective-permute-start(f32[1,512]{1,0:T(1,128)} %get-tuple-element.24), channel_id=1, source_target_pairs={{0,120},{8,0},{16,8},{24,16},{32,24},{40,32},{48,40},{56,48},{64,5... | collective-permute-start | bytes 6152 | tf_op jit(solution)/shard_map/ppermute | solution.py:566
  40.4 3.5 %collective-permute-start.5 = (f32[1,512]{1,0:T(1,128)}, f32[1,512]{1,0:T(1,128)S(1)}, u32[]{:S(2)}, u32[]{:S(2)}) collective-permute-start(f32[1,512]{1,0:T(1,128)} %get-tuple-element.25), channel_id=1, source_target_pairs={{0,7},{1,0},{2,1},{3,2},{4,3},{5,4},{6,5},{7,6},{8,15},{9,8},{10,9... | collective-permute-start | bytes 6152 | tf_op jit(solution)/shard_map/ppermute | solution.py:567

commit v8 on v7

--- a/solution.py
+++ b/solution.py
@@ -114,10 +114,8 @@
     for part in range(rows // K):
         py[part : part + 1, rows:] = line[0:1, part * K : (part + 1) * K]
     py[rows // K :, rows:] = jnp.zeros((8 - rows // K, EXTRA), f32)
-    for r in range(rows // K):
-        for c in range(nby):
-            field = vy[r * K : (r + 1) * K, c * K : (c + 1) * K]
-            py[2 * c : 2 * c + 2, r * K : (r + 1) * K] = two_rows(weights_y[c], field, NT)
+    for c in range(nby):
+        py[2 * c : 2 * c + 2, :rows] = two_rows(weights_y[c], vy[:, c * K : (c + 1) * K], NT)
     for copy in outs:
         copy.wait()
 
@@ -496,26 +494,29 @@
     )(tx, *near, *in_hbm(*carried, adj, depth, basis, wet, owner))
 
 
-def finish_kernel(fields_in, sums, hrow, hcol, bottom_in, edge_in, fields, grad, bottom, edge, out_sems):
+def finish_kernel(
+    fields_in, sums, hrow, hcol, bottom_in, edge_in, fields, grad_out, bottom, edge, grad, out_sems
+):
     u = lax.axis_index("gx")
     v = lax.axis_index("gy")
     size_x = lax.axis_size("gx")
     size_y = lax.axis_size("gy")
     rows, cols = fields.shape[1:]
 
-    below = hrow[...] * jnp.where(u + 1 < size_x, courant, 0.0)
     right = hcol[...] * jnp.where(v + 1 < size_y, courant, 0.0)
     right = jnp.broadcast_to(right, (8, rows)).T[:, 0:1]
     edge[...] = edge_in[...] + jnp.where(iota((rows, K), 1) == K - 1, right, 0.0)
+    below = hrow[...] * jnp.where(u + 1 < size_x, courant, 0.0)
     bottom[...] = bottom_in[...] + jnp.where(iota((8, cols), 0) == 7, below, 0.0)
+    total = jnp.sum(sums[...], axis=0, keepdims=True)
+    grad[...] = total[:, : grad.shape[1]]
     writes = [
         pltpu.make_async_copy(edge, fields.at[2, :, pl.ds(cols - K, K)], out_sems.at[0]),
         pltpu.make_async_copy(bottom, fields.at[1, pl.ds(rows - 8, 8), :], out_sems.at[1]),
+        pltpu.make_async_copy(grad, grad_out, out_sems.at[2]),
     ]
     for copy in writes:
         copy.start()
-    total = jnp.sum(sums[...], axis=0, keepdims=True)
-    grad[...] = total[:, : grad.shape[1]]
     for copy in writes:
         copy.wait()
 
@@ -526,14 +527,15 @@
     edge = fields[2, :, cols - K :]
     return pl.pallas_call(
         finish_kernel,
-        out_shape=(pltpu.HBM(fields.shape, f32), jax.ShapeDtypeStruct((1, slots), f32)),
+        out_shape=(pltpu.HBM(fields.shape, f32), pltpu.HBM((1, slots), f32)),
         in_specs=[hbm_spec()] + [vmem_spec()] * 5,
-        out_specs=(hbm_spec(), vmem_spec()),
+        out_specs=(hbm_spec(), hbm_spec()),
         input_output_aliases={0: 0},
         scratch_shapes=[
             pltpu.VMEM((8, cols), f32),
             pltpu.VMEM((rows, K), f32),
-            pltpu.SemaphoreType.DMA((2,)),
+            pltpu.VMEM((1, slots), f32),
+            pltpu.SemaphoreType.DMA((3,)),
         ],
         compiler_params=pltpu.CompilerParams(vmem_limit_bytes=16 << 20),
         cost_estimate=cost(1 << 20, 1 << 20),

time: 46.4 us -> 45.7 us (0.985)
  Pallas kernels: 13.4 us -> 12.7 us
    pallas_call x1, Pallas kernels: 1.49 us -> 0.99 us  [finish(): pl.pallas_call(finish_kernel, out_shape=(pltpu.HBM(fields.shape, f32), pl...]
where the time goes in v8:
time: 45.7 us; the launch traced here: 45.3 us
  starting transfers between devices  25.9 us (57%)
  Pallas kernels  12.7 us (28%)
  waiting for transfers between devices  4.35 us (10%)
  local copies, waits for them, and re-layouts  1.69 us (4%)
  between operations  0.72 us (2%)
    all_to_all x1, starting transfers between devices, body(): tx = lax.all_to_all(px, 'gx', split_axis=0, concat_axis=0, tiled=True)  7.6 us
    pallas_call x1, Pallas kernels, elevation(): pl.pallas_call(elev_kernel, out_shape=(pltpu.HBM((3, rows, cols), f32), p...  6.35 us
    ppermute x1, starting transfers between devices, body(): hrow = lax.ppermute(erow, 'gx', previous('gx'))  5.62 us
    all_to_all x1, starting transfers between devices, body(): lax.all_to_all(parts[:, None, :], ('gx', 'gy'), split_axis=0, concat_axis...  5.57 us
    ppermute x1, starting transfers between devices, body(): lax.ppermute(ty, 'gy', partner('gy', size_y // 2))  3.82 us
    pallas_call x1, Pallas kernels, carry(): pl.pallas_call(carry_kernel, out_shape=tuple((pltpu.HBM(*result) for resu...  2.83 us
    ppermute x3, starting transfers between devices, body(): lax.ppermute(ty, 'gy', partner('gy', bits))  2.67 us
    all_to_all x1, waiting for transfers between devices, body(): tx = lax.all_to_all(px, 'gx', split_axis=0, concat_axis=0, tiled=True)  2.55 us
  transfers between devices with their start and end apart: 8, of which 3 were waited for; matrix products, arithmetic and copies ran while one was open for 4% of the time, Pallas kernels for 6%

profile of v8, /device:TPU:1, one launch (start us, length us, event | category | flops | bytes accessed | tf_op | source)
XLA Modules:
  0.0 45.3 jit_solution(12648869857819122820)
XLA Ops:
  0.6 2.5 %ends.1 = (f32[16,8,640]{2,1,0:T(8,128)}, f32[8,640]{1,0:T(8,128)S(1)}) custom-call(f32[3,512,512]{2,1,0:T(8,128)} %adj.3, f32[512,512]{1,0:T(8,128)} %depth.3, f32[64,128,128]{2,1,0:T(8,128)} %block_x.3, f32[32,128,128]{2,1,0:T(8,128)} %block_y.3), custom_call_target="tpu_custom_call" | custom-call | flops 16777216 | bytes 3145728 | tf_op jit(solution)/shard_map/ends/pallas_call | solution.py:128
  3.1 3.8 %collective-permute-start = (f32[1,8,640]{2,1,0:T(8,128)S(1)}, f32[1,8,640]{2,1,0:T(8,128)S(1)}, u32[]{:S(2)}, u32[]{:S(2)}) collective-permute-start(f32[1,8,640]{2,1,0:T(8,128)S(1)} %bitcast.15), channel_id=1, source_target_pairs={{0,4},{1,5},{2,6},{3,7},{4,0},{5,1},{6,2},{7,3},{8,12},{9,13},{10,... | collective-permute-start | bytes 61448 | tf_op jit(solution)/shard_map/ppermute | solution.py:564
  7.0 7.6 %all-to-all-start = ((f32[16,8,640]{2,1,0:T(8,128)}), f32[16,8,640]{2,1,0:T(8,128)S(1)}, u32[]{:S(2)}, u32[]{:S(2)}) async-start(f32[16,8,640]{2,1,0:T(8,128)} %get-tuple-element.15), calls=%async_computation | async-start | bytes 655360 | tf_op jit(solution)/shard_map/all_to_all | solution.py:561
  14.6 0.0 collective-permute-done
  14.6 1.6 %collective-permute-start.3 = (f32[2,8,640]{2,1,0:T(8,128)S(1)}, f32[2,8,640]{2,1,0:T(8,128)S(1)}, u32[]{:S(2)}, u32[]{:S(2)}) collective-permute-start(f32[2,8,640]{2,1,0:T(8,128)S(1)} %pad_maximum_fusion.t0), channel_id=1, source_target_pairs={{0,3},{1,2},{2,1},{3,0},{4,7},{5,6},{6,5},{7,4},{8,11},{9,10},{10,... | collective-permute-start | bytes 122888 | tf_op jit(solution)/shard_map/ppermute | solution.py:565
  16.2 1.1 %collective-permute-start.2 = (f32[2,8,640]{2,1,0:T(8,128)S(1)}, f32[2,8,640]{2,1,0:T(8,128)S(1)}, u32[]{:S(2)}, u32[]{:S(2)}) collective-permute-start(f32[2,8,640]{2,1,0:T(8,128)S(1)} %pad_maximum_fusion.t0), channel_id=1, source_target_pairs={{0,2},{1,3},{2,0},{3,1},{4,6},{5,7},{6,4},{7,5},{8,10},{9,11},{10,... | collective-permute-start | bytes 122888 | tf_op jit(solution)/shard_map/ppermute | solution.py:565
  17.2 0.0 collective-permute-start.1
  17.2 2.8 %carry.1 = (bf16[2,512,256]{2,1,0:T(8,128)(2,1)}, bf16[2,192,512]{2,1,0:T(8,128)(2,1)}, f32[8,128]{1,0:T(8,128)}, f32[2,16,2048]{2,1,0:T(8,128)}, bf16[2,16,2048]{2,1,0:T(8,128)(2,1)}) custom-call(f32[64,128,128]{2,1,0:T(8,128)} %block_x.3, f32[32,128,128]{2,1,0:T(8,128)} %block_y.3, f32[128,128]{1,0:T(8,128)} %reduced_x_hbm.1, f32[64,64]{1,0:T(8,128)} %reduced_y_hbm.1, ...), custom_call_target="tpu_custom_call" | custom-call | flops 68719476736 | bytes 2097152 | tf_op jit(solution)/shard_map/carry/pallas_call | solution.py:259
  20.1 0.0 collective-permute-done.3.t3
  20.1 0.0 collective-permute-done.2.t2
  20.1 0.0 collective-permute-done.1.t1
  20.1 2.6 %all-to-all-done.tx = f32[16,8,640]{2,1,0:T(8,128)S(1)} async-done(((f32[16,8,640]{2,1,0:T(8,128)}), f32[16,8,640]{2,1,0:T(8,128)S(1)}, u32[]{:S(2)}, u32[]{:S(2)}) %all-to-all-start) | async-done | bytes 327712 | tf_op jit(solution)/shard_map/all_to_all | solution.py:561
  22.7 6.3 %elevation.1 = (f32[3,512,512]{2,1,0:T(8,128)}, f32[128,128]{1,0:T(8,128)}, f32[1,512]{1,0:T(1,128)}, f32[1,512]{1,0:T(1,128)}) custom-call(f32[16,8,640]{2,1,0:T(8,128)S(1)} %all-to-all-done.tx, f32[2,8,640]{2,1,0:T(8,128)S(1)} %pad_maximum_fusion.t0, f32[2,8,640]{2,1,0:T(8,128)S(1)} %collective-permute-done.1.t1, ...), custom_call_target="tpu_custom_call" | custom-call | flops 402653184 | bytes 10485760 | tf_op jit(solution)/shard_map/elevation/pallas_call | solution.py:472
  29.0 5.6 %all-to-all-start.1 = ((f32[128,1,128]{2,1,0:T(1,128)}), f32[128,1,128]{2,1,0:T(1,128)S(1)}, u32[]{:S(2)}, u32[]{:S(2)}) async-start(f32[128,1,128]{2,1,0:T(1,128)} %bitcast.17), calls=%async_computation.1 | async-start | bytes 131072 | tf_op jit(solution)/shard_map/all_to_all | solution.py:570
  34.6 5.6 %collective-permute-start.4 = (f32[1,512]{1,0:T(1,128)}, f32[1,512]{1,0:T(1,128)S(1)}, u32[]{:S(2)}, u32[]{:S(2)}) collective-permute-start(f32[1,512]{1,0:T(1,128)} %get-tuple-element.24), channel_id=1, source_target_pairs={{0,120},{8,0},{16,8},{24,16},{32,24},{40,32},{48,40},{56,48},{64,5... | collective-permute-start | bytes 6152 | tf_op jit(solution)/shard_map/ppermute | solution.py:568
  40.2 0.6 %collective-permute-start.5 = (f32[1,512]{1,0:T(1,128)}, f32[1,512]{1,0:T(1,128)S(1)}, u32[]{:S(2)}, u32[]{:S(2)}) collective-permute-start(f32[1,512]{1,0:T(1,128)} %get-tuple-element.25), channel_id=1, source_target_pairs={{0,7},{1,0},{2,1},{3,2},{4,3},{5,4},{6,5},{7,6},{8,15},{9,8},{10,9... | collective-permute-start | bytes 6152 | tf_op jit(solution)/shard_map/ppermute | solution.py:569
  40.9 1.0 %slice_bitcast_fusion.edge_in = f32[512,128]{1,0:T(8,128)S(1)} fusion(f32[3,512,512]{2,1,0:T(8,128)} %get-tuple-element.22.fields_in), kind=kLoop, calls=%fused_computation | loop fusion | bytes 524288 | tf_op jit(solution)/shard_map/squeeze | solution.py:527
  41.8 0.7 %slice_bitcast_fusion.1.bottom_in = f32[8,512]{1,0:T(8,128)S(1)} fusion(f32[3,512,512]{2,1,0:T(8,128)} %get-tuple-element.22.fields_in), kind=kLoop, calls=%fused_computation.2 | loop fusion | bytes 32768 | tf_op jit(solution)/shard_map/squeeze | solution.py:526
  42.6 0.0 collective-permute-done.4.hrow
  42.6 1.2 %collective-permute-done.5.hcol = f32[1,512]{1,0:T(1,128)S(1)} collective-permute-done((f32[1,512]{1,0:T(1,128)}, f32[1,512]{1,0:T(1,128)S(1)}, u32[]{:S(2)}, u32[]{:S(2)}) %collective-permute-start.5) | collective-permute-done | bytes 2080 | tf_op jit(solution)/shard_map/ppermute | solution.py:569
  43.8 0.6 %all-to-all-done.1 = f32[128,1,128]{2,1,0:T(1,128)S(1)} async-done(((f32[128,1,128]{2,1,0:T(1,128)}), f32[128,1,128]{2,1,0:T(1,128)S(1)}, u32[]{:S(2)}, u32[]{:S(2)}) %all-to-all-start.1) | async-done | bytes 65568 | tf_op jit(solution)/shard_map/all_to_all | solution.py:570
  44.3 1.0 %finish.1 = (f32[3,512,512]{2,1,0:T(8,128)}, f32[1,16]{1,0:T(1,128)}) custom-call(f32[3,512,512]{2,1,0:T(8,128)} %get-tuple-element.22.fields_in, f32[128,128]{1,0:T(8,128)S(1)} %bitcast.14, f32[1,512]{1,0:T(1,128)S(1)} %collective-permute-done.4.hrow, f32[1,512]{1,0:T(1,128)S(1)} %collective-permute-done.5.hcol, ...), custom_call_target="tpu_custom_call", output_to_operand_aliasing={{0}: (0, {})} | custom-call | flops 1048576 | bytes 1048576 | tf_op jit(solution)/shard_map/finish/pallas_call | solution.py:528
  (1 shorter events, 0.0 us)
Async XLA Ops:
  3.1 11.4 %collective-permute-start = (f32[1,8,640]{2,1,0:T(8,128)S(1)}, f32[1,8,640]{2,1,0:T(8,128)S(1)}, u32[]{:S(2)}, u32[]{:S(2)}) collective-permute-start(f32[1,8,640]{2,1,0:T(8,128)S(1)} %bitcast.15), channel_id=1, source_target_pairs={{0,4},{1,5},{2,6},{3,7},{4,0},{5,1},{6,2},{7,3},{8,12},{9,13},{10,... | collective-permute-start | bytes 61448 | tf_op jit(solution)/shard_map/ppermute | solution.py:564
  7.0 15.7 %all-to-all-start = ((f32[16,8,640]{2,1,0:T(8,128)}), f32[16,8,640]{2,1,0:T(8,128)S(1)}, u32[]{:S(2)}, u32[]{:S(2)}) async-start(f32[16,8,640]{2,1,0:T(8,128)} %get-tuple-element.15), calls=%async_computation | async-start | bytes 655360 | tf_op jit(solution)/shard_map/all_to_all | solution.py:561
  14.6 5.5 %collective-permute-start.3 = (f32[2,8,640]{2,1,0:T(8,128)S(1)}, f32[2,8,640]{2,1,0:T(8,128)S(1)}, u32[]{:S(2)}, u32[]{:S(2)}) collective-permute-start(f32[2,8,640]{2,1,0:T(8,128)S(1)} %pad_maximum_fusion.t0), channel_id=1, source_target_pairs={{0,3},{1,2},{2,1},{3,0},{4,7},{5,6},{6,5},{7,4},{8,11},{9,10},{10,... | collective-permute-start | bytes 122888 | tf_op jit(solution)/shard_map/ppermute | solution.py:565
  16.2 3.9 %collective-permute-start.2 = (f32[2,8,640]{2,1,0:T(8,128)S(1)}, f32[2,8,640]{2,1,0:T(8,128)S(1)}, u32[]{:S(2)}, u32[]{:S(2)}) collective-permute-start(f32[2,8,640]{2,1,0:T(8,128)S(1)} %pad_maximum_fusion.t0), channel_id=1, source_target_pairs={{0,2},{1,3},{2,0},{3,1},{4,6},{5,7},{6,4},{7,5},{8,10},{9,11},{10,... | collective-permute-start | bytes 122888 | tf_op jit(solution)/shard_map/ppermute | solution.py:565
  17.2 2.9 %collective-permute-start.1 = (f32[2,8,640]{2,1,0:T(8,128)S(1)}, f32[2,8,640]{2,1,0:T(8,128)S(1)}, u32[]{:S(2)}, u32[]{:S(2)}) collective-permute-start(f32[2,8,640]{2,1,0:T(8,128)S(1)} %pad_maximum_fusion.t0), channel_id=1, source_target_pairs={{0,1},{1,0},{2,3},{3,2},{4,5},{5,4},{6,7},{7,6},{8,9},{9,8},{10,11... | collective-permute-start | bytes 122888 | tf_op jit(solution)/shard_map/ppermute | solution.py:565
  29.0 15.3 %all-to-all-start.1 = ((f32[128,1,128]{2,1,0:T(1,128)}), f32[128,1,128]{2,1,0:T(1,128)S(1)}, u32[]{:S(2)}, u32[]{:S(2)}) async-start(f32[128,1,128]{2,1,0:T(1,128)} %bitcast.17), calls=%async_computation.1 | async-start | bytes 131072 | tf_op jit(solution)/shard_map/all_to_all | solution.py:570
  34.6 8.0 %collective-permute-start.4 = (f32[1,512]{1,0:T(1,128)}, f32[1,512]{1,0:T(1,128)S(1)}, u32[]{:S(2)}, u32[]{:S(2)}) collective-permute-start(f32[1,512]{1,0:T(1,128)} %get-tuple-element.24), channel_id=1, source_target_pairs={{0,120},{8,0},{16,8},{24,16},{32,24},{40,32},{48,40},{56,48},{64,5... | collective-permute-start | bytes 6152 | tf_op jit(solution)/shard_map/ppermute | solution.py:568
  40.2 3.5 %collective-permute-start.5 = (f32[1,512]{1,0:T(1,128)}, f32[1,512]{1,0:T(1,128)S(1)}, u32[]{:S(2)}, u32[]{:S(2)}) collective-permute-start(f32[1,512]{1,0:T(1,128)} %get-tuple-element.25), channel_id=1, source_target_pairs={{0,7},{1,0},{2,1},{3,2},{4,3},{5,4},{6,5},{7,6},{8,15},{9,8},{10,9... | collective-permute-start | bytes 6152 | tf_op jit(solution)/shard_map/ppermute | solution.py:569

commit v9 on v8

--- a/solution.py
+++ b/solution.py
@@ -307,15 +307,15 @@
         pltpu.make_async_copy(at_row_in, at_row, sems.at[9]),
     ]
     fields = []
-    for r in range(steps):
-        here = pl.ds(r * K, K)
+    for r in range(steps // 2):
+        here = pl.ds(r * 2 * K, 2 * K)
         fields.append(
             [
                 pltpu.make_async_copy(adj.at[:, here, :], planes.at[:, here, :], row_sems.at[r, 0]),
                 pltpu.make_async_copy(depth.at[here, :], dep.at[here, :], row_sems.at[r, 1]),
             ]
         )
-    for group in [fields[0], first, second, fields[1], last[:1], fields[2], fields[3], last[1:]]:
+    for group in [fields[0], first, second, last[:1], fields[1], last[1:]]:
         for copy in group:
             copy.start()
     txs = halves(jnp.concatenate([tx[d][:, :cols] for d in range(tx.shape[0])], axis=0))
@@ -324,10 +324,6 @@
     devices = parts.shape[0]
     count = owner.shape[1]
     slots = count // devices
-    own = owner[...]
-    device_of = iota((devices, count), 0) == lax.shift_right_logical(own, slots.bit_length() - 1)
-    device_of = device_of.astype(f32).astype(bf16)
-    slot_of = iota((slots, count), 0) == (own & (slots - 1))
     for j in range(ty.shape[0] * ty.shape[1]):
         far = j ^ v
         tyn[j * 8 : (j + 1) * 8, :] = ty[far & (ty.shape[0] - 1), far // ty.shape[0]]
@@ -364,10 +360,10 @@
     for r in range(steps):
         here = slice(r * K, (r + 1) * K)
         if r == 0:
-            for copy in fields[0] + fields[1] + last[:1]:
+            for copy in fields[0] + last[:1]:
                 copy.wait()
         if r == 2:
-            for copy in fields[2] + fields[3]:
+            for copy in fields[1]:
                 copy.wait()
         d = dep[here, :]
         high, low = halves(planes[1, here, :])
@@ -441,6 +437,10 @@
             pieces.append(line[:, b * tiles_x : (b + 1) * tiles_x] * keep)
     high, low = halves(jnp.concatenate(pieces, axis=0))
     table = jnp.concatenate([high, low], axis=0)
+    own = owner[...]
+    device_of = iota((devices, count), 0) == lax.shift_right_logical(own, slots.bit_length() - 1)
+    device_of = device_of.astype(f32).astype(bf16)
+    slot_of = iota((slots, count), 0) == (own & (slots - 1))
     lines = tiles_y * modes
     acc = jnp.zeros((lines, count), f32)
     for step in range(2):
@@ -485,7 +485,7 @@
             pltpu.VMEM(*parts),
             *(pltpu.VMEM(*h) for h in halos),
             pltpu.SemaphoreType.DMA((17,)),
-            pltpu.SemaphoreType.DMA((steps, 2)),
+            pltpu.SemaphoreType.DMA((steps // 2, 2)),
             pltpu.SemaphoreType.DMA((steps, 3)),
         ],
         compiler_params=pltpu.CompilerParams(vmem_limit_bytes=32 << 20),

time: 45.7 us -> 45.6 us (level)
  no operation moved by 1% of the time
where the time goes in v9:
time: 45.6 us; the launch traced here: 45.3 us
  starting transfers between devices  25.9 us (57%)
  Pallas kernels  12.6 us (28%)
  waiting for transfers between devices  4.35 us (10%)
  local copies, waits for them, and re-layouts  1.69 us (4%)
  between operations  0.72 us (2%)
    all_to_all x1, starting transfers between devices, body(): tx = lax.all_to_all(px, 'gx', split_axis=0, concat_axis=0, tiled=True)  7.6 us
    pallas_call x1, Pallas kernels, elevation(): pl.pallas_call(elev_kernel, out_shape=(pltpu.HBM((3, rows, cols), f32), p...  6.26 us
    ppermute x1, starting transfers between devices, body(): hrow = lax.ppermute(erow, 'gx', previous('gx'))  5.62 us
    all_to_all x1, starting transfers between devices, body(): lax.all_to_all(parts[:, None, :], ('gx', 'gy'), split_axis=0, concat_axis...  5.57 us
    ppermute x1, starting transfers between devices, body(): lax.ppermute(ty, 'gy', partner('gy', size_y // 2))  3.82 us
    pallas_call x1, Pallas kernels, carry(): pl.pallas_call(carry_kernel, out_shape=tuple((pltpu.HBM(*result) for resu...  2.83 us
    ppermute x3, starting transfers between devices, body(): lax.ppermute(ty, 'gy', partner('gy', bits))  2.67 us
    all_to_all x1, waiting for transfers between devices, body(): tx = lax.all_to_all(px, 'gx', split_axis=0, concat_axis=0, tiled=True)  2.55 us
  transfers between devices with their start and end apart: 8, of which 3 were waited for; matrix products, arithmetic and copies ran while one was open for 4% of the time, Pallas kernels for 6%

profile of v9, /device:TPU:1, one launch (start us, length us, event | category | flops | bytes accessed | tf_op | source)
XLA Modules:
  0.0 45.3 jit_solution(9928124842558210952)
XLA Ops:
  0.6 2.5 %ends.1 = (f32[16,8,640]{2,1,0:T(8,128)}, f32[8,640]{1,0:T(8,128)S(1)}) custom-call(f32[3,512,512]{2,1,0:T(8,128)} %adj.3, f32[512,512]{1,0:T(8,128)} %depth.3, f32[64,128,128]{2,1,0:T(8,128)} %block_x.3, f32[32,128,128]{2,1,0:T(8,128)} %block_y.3), custom_call_target="tpu_custom_call" | custom-call | flops 16777216 | bytes 3145728 | tf_op jit(solution)/shard_map/ends/pallas_call | solution.py:128
  3.1 3.8 %collective-permute-start = (f32[1,8,640]{2,1,0:T(8,128)S(1)}, f32[1,8,640]{2,1,0:T(8,128)S(1)}, u32[]{:S(2)}, u32[]{:S(2)}) collective-permute-start(f32[1,8,640]{2,1,0:T(8,128)S(1)} %bitcast.15), channel_id=1, source_target_pairs={{0,4},{1,5},{2,6},{3,7},{4,0},{5,1},{6,2},{7,3},{8,12},{9,13},{10,... | collective-permute-start | bytes 61448 | tf_op jit(solution)/shard_map/ppermute | solution.py:564
  7.0 7.6 %all-to-all-start = ((f32[16,8,640]{2,1,0:T(8,128)}), f32[16,8,640]{2,1,0:T(8,128)S(1)}, u32[]{:S(2)}, u32[]{:S(2)}) async-start(f32[16,8,640]{2,1,0:T(8,128)} %get-tuple-element.15), calls=%async_computation | async-start | bytes 655360 | tf_op jit(solution)/shard_map/all_to_all | solution.py:561
  14.6 0.0 collective-permute-done
  14.6 1.6 %collective-permute-start.3 = (f32[2,8,640]{2,1,0:T(8,128)S(1)}, f32[2,8,640]{2,1,0:T(8,128)S(1)}, u32[]{:S(2)}, u32[]{:S(2)}) collective-permute-start(f32[2,8,640]{2,1,0:T(8,128)S(1)} %pad_maximum_fusion.t0), channel_id=1, source_target_pairs={{0,3},{1,2},{2,1},{3,0},{4,7},{5,6},{6,5},{7,4},{8,11},{9,10},{10,... | collective-permute-start | bytes 122888 | tf_op jit(solution)/shard_map/ppermute | solution.py:565
  16.2 1.1 %collective-permute-start.2 = (f32[2,8,640]{2,1,0:T(8,128)S(1)}, f32[2,8,640]{2,1,0:T(8,128)S(1)}, u32[]{:S(2)}, u32[]{:S(2)}) collective-permute-start(f32[2,8,640]{2,1,0:T(8,128)S(1)} %pad_maximum_fusion.t0), channel_id=1, source_target_pairs={{0,2},{1,3},{2,0},{3,1},{4,6},{5,7},{6,4},{7,5},{8,10},{9,11},{10,... | collective-permute-start | bytes 122888 | tf_op jit(solution)/shard_map/ppermute | solution.py:565
  17.2 0.0 collective-permute-start.1
  17.2 2.8 %carry.1 = (bf16[2,512,256]{2,1,0:T(8,128)(2,1)}, bf16[2,192,512]{2,1,0:T(8,128)(2,1)}, f32[8,128]{1,0:T(8,128)}, f32[2,16,2048]{2,1,0:T(8,128)}, bf16[2,16,2048]{2,1,0:T(8,128)(2,1)}) custom-call(f32[64,128,128]{2,1,0:T(8,128)} %block_x.3, f32[32,128,128]{2,1,0:T(8,128)} %block_y.3, f32[128,128]{1,0:T(8,128)} %reduced_x_hbm.1, f32[64,64]{1,0:T(8,128)} %reduced_y_hbm.1, ...), custom_call_target="tpu_custom_call" | custom-call | flops 68719476736 | bytes 2097152 | tf_op jit(solution)/shard_map/carry/pallas_call | solution.py:259
  20.1 0.0 collective-permute-done.3.t3
  20.1 0.0 collective-permute-done.2.t2
  20.1 0.0 collective-permute-done.1.t1
  20.1 2.6 %all-to-all-done.tx = f32[16,8,640]{2,1,0:T(8,128)S(1)} async-done(((f32[16,8,640]{2,1,0:T(8,128)}), f32[16,8,640]{2,1,0:T(8,128)S(1)}, u32[]{:S(2)}, u32[]{:S(2)}) %all-to-all-start) | async-done | bytes 327712 | tf_op jit(solution)/shard_map/all_to_all | solution.py:561
  22.7 6.3 %elevation.1 = (f32[3,512,512]{2,1,0:T(8,128)}, f32[128,128]{1,0:T(8,128)}, f32[1,512]{1,0:T(1,128)}, f32[1,512]{1,0:T(1,128)}) custom-call(f32[16,8,640]{2,1,0:T(8,128)S(1)} %all-to-all-done.tx, f32[2,8,640]{2,1,0:T(8,128)S(1)} %pad_maximum_fusion.t0, f32[2,8,640]{2,1,0:T(8,128)S(1)} %collective-permute-done.1.t1, ...), custom_call_target="tpu_custom_call" | custom-call | flops 402653184 | bytes 10485760 | tf_op jit(solution)/shard_map/elevation/pallas_call | solution.py:472
  28.9 5.6 %all-to-all-start.1 = ((f32[128,1,128]{2,1,0:T(1,128)}), f32[128,1,128]{2,1,0:T(1,128)S(1)}, u32[]{:S(2)}, u32[]{:S(2)}) async-start(f32[128,1,128]{2,1,0:T(1,128)} %bitcast.17), calls=%async_computation.1 | async-start | bytes 131072 | tf_op jit(solution)/shard_map/all_to_all | solution.py:570
  34.5 5.6 %collective-permute-start.4 = (f32[1,512]{1,0:T(1,128)}, f32[1,512]{1,0:T(1,128)S(1)}, u32[]{:S(2)}, u32[]{:S(2)}) collective-permute-start(f32[1,512]{1,0:T(1,128)} %get-tuple-element.24), channel_id=1, source_target_pairs={{0,120},{8,0},{16,8},{24,16},{32,24},{40,32},{48,40},{56,48},{64,5... | collective-permute-start | bytes 6152 | tf_op jit(solution)/shard_map/ppermute | solution.py:568
  40.1 0.6 %collective-permute-start.5 = (f32[1,512]{1,0:T(1,128)}, f32[1,512]{1,0:T(1,128)S(1)}, u32[]{:S(2)}, u32[]{:S(2)}) collective-permute-start(f32[1,512]{1,0:T(1,128)} %get-tuple-element.25), channel_id=1, source_target_pairs={{0,7},{1,0},{2,1},{3,2},{4,3},{5,4},{6,5},{7,6},{8,15},{9,8},{10,9... | collective-permute-start | bytes 6152 | tf_op jit(solution)/shard_map/ppermute | solution.py:569
  40.8 1.0 %slice_bitcast_fusion.edge_in = f32[512,128]{1,0:T(8,128)S(1)} fusion(f32[3,512,512]{2,1,0:T(8,128)} %get-tuple-element.22.fields_in), kind=kLoop, calls=%fused_computation | loop fusion | bytes 524288 | tf_op jit(solution)/shard_map/squeeze | solution.py:527
  41.8 0.7 %slice_bitcast_fusion.1.bottom_in = f32[8,512]{1,0:T(8,128)S(1)} fusion(f32[3,512,512]{2,1,0:T(8,128)} %get-tuple-element.22.fields_in), kind=kLoop, calls=%fused_computation.2 | loop fusion | bytes 32768 | tf_op jit(solution)/shard_map/squeeze | solution.py:526
  42.5 0.0 collective-permute-done.4.hrow
  42.5 1.2 %collective-permute-done.5.hcol = f32[1,512]{1,0:T(1,128)S(1)} collective-permute-done((f32[1,512]{1,0:T(1,128)}, f32[1,512]{1,0:T(1,128)S(1)}, u32[]{:S(2)}, u32[]{:S(2)}) %collective-permute-start.5) | collective-permute-done | bytes 2080 | tf_op jit(solution)/shard_map/ppermute | solution.py:569
  43.7 0.6 %all-to-all-done.1 = f32[128,1,128]{2,1,0:T(1,128)S(1)} async-done(((f32[128,1,128]{2,1,0:T(1,128)}), f32[128,1,128]{2,1,0:T(1,128)S(1)}, u32[]{:S(2)}, u32[]{:S(2)}) %all-to-all-start.1) | async-done | bytes 65568 | tf_op jit(solution)/shard_map/all_to_all | solution.py:570
  44.3 1.0 %finish.1 = (f32[3,512,512]{2,1,0:T(8,128)}, f32[1,16]{1,0:T(1,128)}) custom-call(f32[3,512,512]{2,1,0:T(8,128)} %get-tuple-element.22.fields_in, f32[128,128]{1,0:T(8,128)S(1)} %bitcast.14, f32[1,512]{1,0:T(1,128)S(1)} %collective-permute-done.4.hrow, f32[1,512]{1,0:T(1,128)S(1)} %collective-permute-done.5.hcol, ...), custom_call_target="tpu_custom_call", output_to_operand_aliasing={{0}: (0, {})} | custom-call | flops 1048576 | bytes 1048576 | tf_op jit(solution)/shard_map/finish/pallas_call | solution.py:528
  (1 shorter events, 0.0 us)
Async XLA Ops:
  3.1 11.4 %collective-permute-start = (f32[1,8,640]{2,1,0:T(8,128)S(1)}, f32[1,8,640]{2,1,0:T(8,128)S(1)}, u32[]{:S(2)}, u32[]{:S(2)}) collective-permute-start(f32[1,8,640]{2,1,0:T(8,128)S(1)} %bitcast.15), channel_id=1, source_target_pairs={{0,4},{1,5},{2,6},{3,7},{4,0},{5,1},{6,2},{7,3},{8,12},{9,13},{10,... | collective-permute-start | bytes 61448 | tf_op jit(solution)/shard_map/ppermute | solution.py:564
  7.0 15.7 %all-to-all-start = ((f32[16,8,640]{2,1,0:T(8,128)}), f32[16,8,640]{2,1,0:T(8,128)S(1)}, u32[]{:S(2)}, u32[]{:S(2)}) async-start(f32[16,8,640]{2,1,0:T(8,128)} %get-tuple-element.15), calls=%async_computation | async-start | bytes 655360 | tf_op jit(solution)/shard_map/all_to_all | solution.py:561
  14.6 5.5 %collective-permute-start.3 = (f32[2,8,640]{2,1,0:T(8,128)S(1)}, f32[2,8,640]{2,1,0:T(8,128)S(1)}, u32[]{:S(2)}, u32[]{:S(2)}) collective-permute-start(f32[2,8,640]{2,1,0:T(8,128)S(1)} %pad_maximum_fusion.t0), channel_id=1, source_target_pairs={{0,3},{1,2},{2,1},{3,0},{4,7},{5,6},{6,5},{7,4},{8,11},{9,10},{10,... | collective-permute-start | bytes 122888 | tf_op jit(solution)/shard_map/ppermute | solution.py:565
  16.2 3.9 %collective-permute-start.2 = (f32[2,8,640]{2,1,0:T(8,128)S(1)}, f32[2,8,640]{2,1,0:T(8,128)S(1)}, u32[]{:S(2)}, u32[]{:S(2)}) collective-permute-start(f32[2,8,640]{2,1,0:T(8,128)S(1)} %pad_maximum_fusion.t0), channel_id=1, source_target_pairs={{0,2},{1,3},{2,0},{3,1},{4,6},{5,7},{6,4},{7,5},{8,10},{9,11},{10,... | collective-permute-start | bytes 122888 | tf_op jit(solution)/shard_map/ppermute | solution.py:565
  17.2 2.9 %collective-permute-start.1 = (f32[2,8,640]{2,1,0:T(8,128)S(1)}, f32[2,8,640]{2,1,0:T(8,128)S(1)}, u32[]{:S(2)}, u32[]{:S(2)}) collective-permute-start(f32[2,8,640]{2,1,0:T(8,128)S(1)} %pad_maximum_fusion.t0), channel_id=1, source_target_pairs={{0,1},{1,0},{2,3},{3,2},{4,5},{5,4},{6,7},{7,6},{8,9},{9,8},{10,11... | collective-permute-start | bytes 122888 | tf_op jit(solution)/shard_map/ppermute | solution.py:565
  28.9 15.3 %all-to-all-start.1 = ((f32[128,1,128]{2,1,0:T(1,128)}), f32[128,1,128]{2,1,0:T(1,128)S(1)}, u32[]{:S(2)}, u32[]{:S(2)}) async-start(f32[128,1,128]{2,1,0:T(1,128)} %bitcast.17), calls=%async_computation.1 | async-start | bytes 131072 | tf_op jit(solution)/shard_map/all_to_all | solution.py:570
  34.5 8.0 %collective-permute-start.4 = (f32[1,512]{1,0:T(1,128)}, f32[1,512]{1,0:T(1,128)S(1)}, u32[]{:S(2)}, u32[]{:S(2)}) collective-permute-start(f32[1,512]{1,0:T(1,128)} %get-tuple-element.24), channel_id=1, source_target_pairs={{0,120},{8,0},{16,8},{24,16},{32,24},{40,32},{48,40},{56,48},{64,5... | collective-permute-start | bytes 6152 | tf_op jit(solution)/shard_map/ppermute | solution.py:568
  40.1 3.5 %collective-permute-start.5 = (f32[1,512]{1,0:T(1,128)}, f32[1,512]{1,0:T(1,128)S(1)}, u32[]{:S(2)}, u32[]{:S(2)}) collective-permute-start(f32[1,512]{1,0:T(1,128)} %get-tuple-element.25), channel_id=1, source_target_pairs={{0,7},{1,0},{2,1},{3,2},{4,3},{5,4},{6,5},{7,6},{8,15},{9,8},{10,9... | collective-permute-start | bytes 6152 | tf_op jit(solution)/shard_map/ppermute | solution.py:569

commit v10 on v9

--- a/solution.py
+++ b/solution.py
@@ -282,9 +282,9 @@
 
 def elev_kernel(
     tx, t0, t1, t2, t3, mx_in, my_in, gside_in, share_in, at_row_in, adj, depth, basis_in, wet_in, owner_in,
-    fields_out, parts_out, erow_out, ecol_out,
+    fields_out, parts_out, erow, ecol,
     ty, mx, my, gside, share, at_row, planes, dep, basis, wet, owner,
-    elev, fx, fy, tyn, mom, parts, erow, ecol, sems, row_sems, out_sems,
+    elev, fx, fy, tyn, mom, parts, sems, row_sems, out_sems,
 ):
     u = lax.axis_index("gx")
     v = lax.axis_index("gy")
@@ -410,8 +410,6 @@
             send(1, fx, r - 1)
         if r == 0:
             erow[...] = e[0:1, :]
-            outs.append(pltpu.make_async_copy(erow, erow_out, sems.at[11]))
-            outs[-1].start()
         ecol[:, here] = e[:, :K].T[0:1, :]
         for a in range(per):
             for w in range(cols // tile_w):
@@ -422,8 +420,6 @@
                         tile * basis[b], axis=0, keepdims=True
                     )
     send(1, fx, steps - 1)
-    outs.append(pltpu.make_async_copy(ecol, ecol_out, sems.at[12]))
-    outs[-1].start()
     for copy in last[1:]:
         copy.wait()
     tiles_y, tiles_x = wet.shape
@@ -471,9 +467,13 @@
     like = lambda *arrays: [pltpu.VMEM(a.shape, a.dtype) for a in arrays]
     return pl.pallas_call(
         elev_kernel,
-        out_shape=(pltpu.HBM((3, rows, cols), f32), pltpu.HBM(*parts), *(pltpu.HBM(*h) for h in halos)),
+        out_shape=(
+            pltpu.HBM((3, rows, cols), f32),
+            pltpu.HBM(*parts),
+            *(jax.ShapeDtypeStruct(*h) for h in halos),
+        ),
         in_specs=[vmem_spec()] + [pl.BlockSpec(memory_space=pl.ANY)] * 4 + [hbm_spec()] * 10,
-        out_specs=(hbm_spec(),) * 4,
+        out_specs=(hbm_spec(), hbm_spec(), vmem_spec(), vmem_spec()),
         scratch_shapes=[pltpu.VMEM(far, f32)]
         + like(*carried)
         + [pltpu.VMEM((3, rows, cols), f32), pltpu.VMEM(*field)]
@@ -483,7 +483,6 @@
             pltpu.VMEM((far[0] * far[1] * 8, far[3]), f32),
             pltpu.VMEM((rows // tile_h * modes, cols), f32),
             pltpu.VMEM(*parts),
-            *(pltpu.VMEM(*h) for h in halos),
             pltpu.SemaphoreType.DMA((17,)),
             pltpu.SemaphoreType.DMA((steps // 2, 2)),
             pltpu.SemaphoreType.DMA((steps, 3)),

time: 45.6 us -> 45.6 us (level)
  no operation moved by 1% of the time
where the time goes in v10:
time: 45.6 us; the launch traced here: 45.3 us
  starting transfers between devices  25.9 us (57%)
  Pallas kernels  12.6 us (28%)
  waiting for transfers between devices  4.35 us (10%)
  local copies, waits for them, and re-layouts  1.69 us (4%)
  between operations  0.72 us (2%)
    all_to_all x1, starting transfers between devices, body(): tx = lax.all_to_all(px, 'gx', split_axis=0, concat_axis=0, tiled=True)  7.6 us
    pallas_call x1, Pallas kernels, elevation(): pl.pallas_call(elev_kernel, out_shape=(pltpu.HBM((3, rows, cols), f32), p...  6.26 us
    ppermute x1, starting transfers between devices, body(): hrow = lax.ppermute(erow, 'gx', previous('gx'))  5.62 us
    all_to_all x1, starting transfers between devices, body(): lax.all_to_all(parts[:, None, :], ('gx', 'gy'), split_axis=0, concat_axis...  5.58 us
    ppermute x1, starting transfers between devices, body(): lax.ppermute(ty, 'gy', partner('gy', size_y // 2))  3.82 us
    pallas_call x1, Pallas kernels, carry(): pl.pallas_call(carry_kernel, out_shape=tuple((pltpu.HBM(*result) for resu...  2.83 us
    ppermute x3, starting transfers between devices, body(): lax.ppermute(ty, 'gy', partner('gy', bits))  2.67 us
    all_to_all x1, waiting for transfers between devices, body(): tx = lax.all_to_all(px, 'gx', split_axis=0, concat_axis=0, tiled=True)  2.55 us
  transfers between devices with their start and end apart: 8, of which 3 were waited for; matrix products, arithmetic and copies ran while one was open for 4% of the time, Pallas kernels for 6%

profile of v10, /device:TPU:1, one launch (start us, length us, event | category | flops | bytes accessed | tf_op | source)
XLA Modules:
  0.0 45.3 jit_solution(12810296645627455957)
XLA Ops:
  0.6 2.5 %ends.1 = (f32[16,8,640]{2,1,0:T(8,128)}, f32[8,640]{1,0:T(8,128)S(1)}) custom-call(f32[3,512,512]{2,1,0:T(8,128)} %adj.3, f32[512,512]{1,0:T(8,128)} %depth.3, f32[64,128,128]{2,1,0:T(8,128)} %block_x.3, f32[32,128,128]{2,1,0:T(8,128)} %block_y.3), custom_call_target="tpu_custom_call" | custom-call | flops 16777216 | bytes 3145728 | tf_op jit(solution)/shard_map/ends/pallas_call | solution.py:128
  3.1 3.8 %collective-permute-start = (f32[1,8,640]{2,1,0:T(8,128)S(1)}, f32[1,8,640]{2,1,0:T(8,128)S(1)}, u32[]{:S(2)}, u32[]{:S(2)}) collective-permute-start(f32[1,8,640]{2,1,0:T(8,128)S(1)} %bitcast.15), channel_id=1, source_target_pairs={{0,4},{1,5},{2,6},{3,7},{4,0},{5,1},{6,2},{7,3},{8,12},{9,13},{10,... | collective-permute-start | bytes 61448 | tf_op jit(solution)/shard_map/ppermute | solution.py:563
  7.0 7.6 %all-to-all-start = ((f32[16,8,640]{2,1,0:T(8,128)}), f32[16,8,640]{2,1,0:T(8,128)S(1)}, u32[]{:S(2)}, u32[]{:S(2)}) async-start(f32[16,8,640]{2,1,0:T(8,128)} %get-tuple-element.15), calls=%async_computation | async-start | bytes 655360 | tf_op jit(solution)/shard_map/all_to_all | solution.py:560
  14.6 0.0 collective-permute-done
  14.6 1.6 %collective-permute-start.3 = (f32[2,8,640]{2,1,0:T(8,128)S(1)}, f32[2,8,640]{2,1,0:T(8,128)S(1)}, u32[]{:S(2)}, u32[]{:S(2)}) collective-permute-start(f32[2,8,640]{2,1,0:T(8,128)S(1)} %pad_maximum_fusion.t0), channel_id=1, source_target_pairs={{0,3},{1,2},{2,1},{3,0},{4,7},{5,6},{6,5},{7,4},{8,11},{9,10},{10,... | collective-permute-start | bytes 122888 | tf_op jit(solution)/shard_map/ppermute | solution.py:564
  16.2 1.1 %collective-permute-start.2 = (f32[2,8,640]{2,1,0:T(8,128)S(1)}, f32[2,8,640]{2,1,0:T(8,128)S(1)}, u32[]{:S(2)}, u32[]{:S(2)}) collective-permute-start(f32[2,8,640]{2,1,0:T(8,128)S(1)} %pad_maximum_fusion.t0), channel_id=1, source_target_pairs={{0,2},{1,3},{2,0},{3,1},{4,6},{5,7},{6,4},{7,5},{8,10},{9,11},{10,... | collective-permute-start | bytes 122888 | tf_op jit(solution)/shard_map/ppermute | solution.py:564
  17.2 0.0 collective-permute-start.1
  17.2 2.8 %carry.1 = (bf16[2,512,256]{2,1,0:T(8,128)(2,1)}, bf16[2,192,512]{2,1,0:T(8,128)(2,1)}, f32[8,128]{1,0:T(8,128)}, f32[2,16,2048]{2,1,0:T(8,128)}, bf16[2,16,2048]{2,1,0:T(8,128)(2,1)}) custom-call(f32[64,128,128]{2,1,0:T(8,128)} %block_x.3, f32[32,128,128]{2,1,0:T(8,128)} %block_y.3, f32[128,128]{1,0:T(8,128)} %reduced_x_hbm.1, f32[64,64]{1,0:T(8,128)} %reduced_y_hbm.1, ...), custom_call_target="tpu_custom_call" | custom-call | flops 68719476736 | bytes 2097152 | tf_op jit(solution)/shard_map/carry/pallas_call | solution.py:259
  20.1 0.0 collective-permute-done.3.t3
  20.1 0.0 collective-permute-done.2.t2
  20.1 0.0 collective-permute-done.1.t1
  20.1 2.6 %all-to-all-done.tx = f32[16,8,640]{2,1,0:T(8,128)S(1)} async-done(((f32[16,8,640]{2,1,0:T(8,128)}), f32[16,8,640]{2,1,0:T(8,128)S(1)}, u32[]{:S(2)}, u32[]{:S(2)}) %all-to-all-start) | async-done | bytes 327712 | tf_op jit(solution)/shard_map/all_to_all | solution.py:560
  22.7 6.3 %elevation.1 = (f32[3,512,512]{2,1,0:T(8,128)}, f32[128,128]{1,0:T(8,128)}, f32[1,512]{1,0:T(1,128)S(1)}, f32[1,512]{1,0:T(1,128)S(1)}) custom-call(f32[16,8,640]{2,1,0:T(8,128)S(1)} %all-to-all-done.tx, f32[2,8,640]{2,1,0:T(8,128)S(1)} %pad_maximum_fusion.t0, f32[2,8,640]{2,1,0:T(8,128)S(1)} %collective-permute-done.1.t1, ...), custom_call_target="tpu_custom_call" | custom-call | flops 402653184 | bytes 10485760 | tf_op jit(solution)/shard_map/elevation/pallas_call | solution.py:468
  28.9 5.6 %all-to-all-start.1 = ((f32[128,1,128]{2,1,0:T(1,128)}), f32[128,1,128]{2,1,0:T(1,128)S(1)}, u32[]{:S(2)}, u32[]{:S(2)}) async-start(f32[128,1,128]{2,1,0:T(1,128)} %bitcast.17), calls=%async_computation.1 | async-start | bytes 131072 | tf_op jit(solution)/shard_map/all_to_all | solution.py:569
  34.5 5.6 %collective-permute-start.4 = (f32[1,512]{1,0:T(1,128)S(1)}, f32[1,512]{1,0:T(1,128)S(1)}, u32[]{:S(2)}, u32[]{:S(2)}) collective-permute-start(f32[1,512]{1,0:T(1,128)S(1)} %get-tuple-element.24), channel_id=1, source_target_pairs={{0,120},{8,0},{16,8},{24,16},{32,24},{40,32},{48,40},{56,48},{64,5... | collective-permute-start | bytes 6152 | tf_op jit(solution)/shard_map/ppermute | solution.py:567
  40.2 0.6 %collective-permute-start.5 = (f32[1,512]{1,0:T(1,128)S(1)}, f32[1,512]{1,0:T(1,128)S(1)}, u32[]{:S(2)}, u32[]{:S(2)}) collective-permute-start(f32[1,512]{1,0:T(1,128)S(1)} %get-tuple-element.25), channel_id=1, source_target_pairs={{0,7},{1,0},{2,1},{3,2},{4,3},{5,4},{6,5},{7,6},{8,15},{9,8},{10,9... | collective-permute-start | bytes 6152 | tf_op jit(solution)/shard_map/ppermute | solution.py:568
  40.8 1.0 %slice_bitcast_fusion.edge_in = f32[512,128]{1,0:T(8,128)S(1)} fusion(f32[3,512,512]{2,1,0:T(8,128)} %get-tuple-element.22.fields_in), kind=kLoop, calls=%fused_computation | loop fusion | bytes 524288 | tf_op jit(solution)/shard_map/squeeze | solution.py:526
  41.8 0.7 %slice_bitcast_fusion.1.bottom_in = f32[8,512]{1,0:T(8,128)S(1)} fusion(f32[3,512,512]{2,1,0:T(8,128)} %get-tuple-element.22.fields_in), kind=kLoop, calls=%fused_computation.2 | loop fusion | bytes 32768 | tf_op jit(solution)/shard_map/squeeze | solution.py:525
  42.5 0.0 collective-permute-done.4.hrow
  42.5 1.0 %collective-permute-done.5.hcol = f32[1,512]{1,0:T(1,128)S(1)} collective-permute-done((f32[1,512]{1,0:T(1,128)S(1)}, f32[1,512]{1,0:T(1,128)S(1)}, u32[]{:S(2)}, u32[]{:S(2)}) %collective-permute-start.5) | collective-permute-done | bytes 2080 | tf_op jit(solution)/shard_map/ppermute | solution.py:568
  43.5 0.8 %all-to-all-done.1 = f32[128,1,128]{2,1,0:T(1,128)S(1)} async-done(((f32[128,1,128]{2,1,0:T(1,128)}), f32[128,1,128]{2,1,0:T(1,128)S(1)}, u32[]{:S(2)}, u32[]{:S(2)}) %all-to-all-start.1) | async-done | bytes 65568 | tf_op jit(solution)/shard_map/all_to_all | solution.py:569
  44.3 1.0 %finish.1 = (f32[3,512,512]{2,1,0:T(8,128)}, f32[1,16]{1,0:T(1,128)}) custom-call(f32[3,512,512]{2,1,0:T(8,128)} %get-tuple-element.22.fields_in, f32[128,128]{1,0:T(8,128)S(1)} %bitcast.14, f32[1,512]{1,0:T(1,128)S(1)} %collective-permute-done.4.hrow, f32[1,512]{1,0:T(1,128)S(1)} %collective-permute-done.5.hcol, ...), custom_call_target="tpu_custom_call", output_to_operand_aliasing={{0}: (0, {})} | custom-call | flops 1048576 | bytes 1048576 | tf_op jit(solution)/shard_map/finish/pallas_call | solution.py:527
  (1 shorter events, 0.0 us)
Async XLA Ops:
  3.1 11.4 %collective-permute-start = (f32[1,8,640]{2,1,0:T(8,128)S(1)}, f32[1,8,640]{2,1,0:T(8,128)S(1)}, u32[]{:S(2)}, u32[]{:S(2)}) collective-permute-start(f32[1,8,640]{2,1,0:T(8,128)S(1)} %bitcast.15), channel_id=1, source_target_pairs={{0,4},{1,5},{2,6},{3,7},{4,0},{5,1},{6,2},{7,3},{8,12},{9,13},{10,... | collective-permute-start | bytes 61448 | tf_op jit(solution)/shard_map/ppermute | solution.py:563
  7.0 15.7 %all-to-all-start = ((f32[16,8,640]{2,1,0:T(8,128)}), f32[16,8,640]{2,1,0:T(8,128)S(1)}, u32[]{:S(2)}, u32[]{:S(2)}) async-start(f32[16,8,640]{2,1,0:T(8,128)} %get-tuple-element.15), calls=%async_computation | async-start | bytes 655360 | tf_op jit(solution)/shard_map/all_to_all | solution.py:560
  14.6 5.5 %collective-permute-start.3 = (f32[2,8,640]{2,1,0:T(8,128)S(1)}, f32[2,8,640]{2,1,0:T(8,128)S(1)}, u32[]{:S(2)}, u32[]{:S(2)}) collective-permute-start(f32[2,8,640]{2,1,0:T(8,128)S(1)} %pad_maximum_fusion.t0), channel_id=1, source_target_pairs={{0,3},{1,2},{2,1},{3,0},{4,7},{5,6},{6,5},{7,4},{8,11},{9,10},{10,... | collective-permute-start | bytes 122888 | tf_op jit(solution)/shard_map/ppermute | solution.py:564
  16.2 3.9 %collective-permute-start.2 = (f32[2,8,640]{2,1,0:T(8,128)S(1)}, f32[2,8,640]{2,1,0:T(8,128)S(1)}, u32[]{:S(2)}, u32[]{:S(2)}) collective-permute-start(f32[2,8,640]{2,1,0:T(8,128)S(1)} %pad_maximum_fusion.t0), channel_id=1, source_target_pairs={{0,2},{1,3},{2,0},{3,1},{4,6},{5,7},{6,4},{7,5},{8,10},{9,11},{10,... | collective-permute-start | bytes 122888 | tf_op jit(solution)/shard_map/ppermute | solution.py:564
  17.2 2.9 %collective-permute-start.1 = (f32[2,8,640]{2,1,0:T(8,128)S(1)}, f32[2,8,640]{2,1,0:T(8,128)S(1)}, u32[]{:S(2)}, u32[]{:S(2)}) collective-permute-start(f32[2,8,640]{2,1,0:T(8,128)S(1)} %pad_maximum_fusion.t0), channel_id=1, source_target_pairs={{0,1},{1,0},{2,3},{3,2},{4,5},{5,4},{6,7},{7,6},{8,9},{9,8},{10,11... | collective-permute-start | bytes 122888 | tf_op jit(solution)/shard_map/ppermute | solution.py:564
  28.9 15.3 %all-to-all-start.1 = ((f32[128,1,128]{2,1,0:T(1,128)}), f32[128,1,128]{2,1,0:T(1,128)S(1)}, u32[]{:S(2)}, u32[]{:S(2)}) async-start(f32[128,1,128]{2,1,0:T(1,128)} %bitcast.17), calls=%async_computation.1 | async-start | bytes 131072 | tf_op jit(solution)/shard_map/all_to_all | solution.py:569
  34.5 8.0 %collective-permute-start.4 = (f32[1,512]{1,0:T(1,128)S(1)}, f32[1,512]{1,0:T(1,128)S(1)}, u32[]{:S(2)}, u32[]{:S(2)}) collective-permute-start(f32[1,512]{1,0:T(1,128)S(1)} %get-tuple-element.24), channel_id=1, source_target_pairs={{0,120},{8,0},{16,8},{24,16},{32,24},{40,32},{48,40},{56,48},{64,5... | collective-permute-start | bytes 6152 | tf_op jit(solution)/shard_map/ppermute | solution.py:567
  40.2 3.3 %collective-permute-start.5 = (f32[1,512]{1,0:T(1,128)S(1)}, f32[1,512]{1,0:T(1,128)S(1)}, u32[]{:S(2)}, u32[]{:S(2)}) collective-permute-start(f32[1,512]{1,0:T(1,128)S(1)} %get-tuple-element.25), channel_id=1, source_target_pairs={{0,7},{1,0},{2,1},{3,2},{4,3},{5,4},{6,5},{7,6},{8,15},{9,8},{10,9... | collective-permute-start | bytes 6152 | tf_op jit(solution)/shard_map/ppermute | solution.py:568

commit v11 on v10

--- a/solution.py
+++ b/solution.py
@@ -204,7 +204,7 @@
         share[step] = acc
     for copy in outs[:2]:
         copy.start()
-    for copy in copies[2:4]:
+    for copy in copies[2:]:
         copy.wait()
     own_x = reduced_x[pl.ds(pl.multiple_of(u * 8, 8), 8), :]
     prev_x = reduced_x[pl.ds(pl.multiple_of(jnp.maximum(u - 1, 0) * 8, 8), 8), :]
@@ -214,8 +214,6 @@
         for i, part in enumerate(zip(halves(w), halves(g))):
             mx[i, c * K : (c + 1) * K, :] = jnp.concatenate(part, axis=1)
     outs[2].start()
-    for copy in copies[4:]:
-        copy.wait()
     own_y = halves(reduced_y[pl.ds(pl.multiple_of(v * 8, 8), 8), :])
     prev_y = reduced_y[pl.ds(pl.multiple_of(jnp.maximum(v - 1, 0) * 8, 8), 8), :]
     sub = iota((8, K), 0)

time: 45.6 us -> 45.6 us (level)
  no operation moved by 1% of the time
where the time goes in v11:
time: 45.6 us; the launch traced here: 45.3 us
  starting transfers between devices  25.9 us (57%)
  Pallas kernels  12.6 us (28%)
  waiting for transfers between devices  4.35 us (10%)
  local copies, waits for them, and re-layouts  1.69 us (4%)
  between operations  0.72 us (2%)
    all_to_all x1, starting transfers between devices, body(): tx = lax.all_to_all(px, 'gx', split_axis=0, concat_axis=0, tiled=True)  7.6 us
    pallas_call x1, Pallas kernels, elevation(): pl.pallas_call(elev_kernel, out_shape=(pltpu.HBM((3, rows, cols), f32), p...  6.26 us
    ppermute x1, starting transfers between devices, body(): hrow = lax.ppermute(erow, 'gx', previous('gx'))  5.62 us
    all_to_all x1, starting transfers between devices, body(): lax.all_to_all(parts[:, None, :], ('gx', 'gy'), split_axis=0, concat_axis...  5.58 us
    ppermute x1, starting transfers between devices, body(): lax.ppermute(ty, 'gy', partner('gy', size_y // 2))  3.82 us
    pallas_call x1, Pallas kernels, carry(): pl.pallas_call(carry_kernel, out_shape=tuple((pltpu.HBM(*result) for resu...  2.83 us
    ppermute x3, starting transfers between devices, body(): lax.ppermute(ty, 'gy', partner('gy', bits))  2.67 us
    all_to_all x1, waiting for transfers between devices, body(): tx = lax.all_to_all(px, 'gx', split_axis=0, concat_axis=0, tiled=True)  2.55 us
  transfers between devices with their start and end apart: 8, of which 3 were waited for; matrix products, arithmetic and copies ran while one was open for 4% of the time, Pallas kernels for 6%

profile of v11, /device:TPU:1, one launch (start us, length us, event | category | flops | bytes accessed | tf_op | source)
XLA Modules:
  0.0 45.3 jit_solution(6869770142636632728)
XLA Ops:
  0.6 2.5 %ends.1 = (f32[16,8,640]{2,1,0:T(8,128)}, f32[8,640]{1,0:T(8,128)S(1)}) custom-call(f32[3,512,512]{2,1,0:T(8,128)} %adj.3, f32[512,512]{1,0:T(8,128)} %depth.3, f32[64,128,128]{2,1,0:T(8,128)} %block_x.3, f32[32,128,128]{2,1,0:T(8,128)} %block_y.3), custom_call_target="tpu_custom_call" | custom-call | flops 16777216 | bytes 3145728 | tf_op jit(solution)/shard_map/ends/pallas_call | solution.py:128
  3.1 3.8 %collective-permute-start = (f32[1,8,640]{2,1,0:T(8,128)S(1)}, f32[1,8,640]{2,1,0:T(8,128)S(1)}, u32[]{:S(2)}, u32[]{:S(2)}) collective-permute-start(f32[1,8,640]{2,1,0:T(8,128)S(1)} %bitcast.15), channel_id=1, source_target_pairs={{0,4},{1,5},{2,6},{3,7},{4,0},{5,1},{6,2},{7,3},{8,12},{9,13},{10,... | collective-permute-start | bytes 61448 | tf_op jit(solution)/shard_map/ppermute | solution.py:561
  7.0 7.6 %all-to-all-start = ((f32[16,8,640]{2,1,0:T(8,128)}), f32[16,8,640]{2,1,0:T(8,128)S(1)}, u32[]{:S(2)}, u32[]{:S(2)}) async-start(f32[16,8,640]{2,1,0:T(8,128)} %get-tuple-element.15), calls=%async_computation | async-start | bytes 655360 | tf_op jit(solution)/shard_map/all_to_all | solution.py:558
  14.6 0.0 collective-permute-done
  14.6 1.6 %collective-permute-start.3 = (f32[2,8,640]{2,1,0:T(8,128)S(1)}, f32[2,8,640]{2,1,0:T(8,128)S(1)}, u32[]{:S(2)}, u32[]{:S(2)}) collective-permute-start(f32[2,8,640]{2,1,0:T(8,128)S(1)} %pad_maximum_fusion.t0), channel_id=1, source_target_pairs={{0,3},{1,2},{2,1},{3,0},{4,7},{5,6},{6,5},{7,4},{8,11},{9,10},{10,... | collective-permute-start | bytes 122888 | tf_op jit(solution)/shard_map/ppermute | solution.py:562
  16.2 1.1 %collective-permute-start.2 = (f32[2,8,640]{2,1,0:T(8,128)S(1)}, f32[2,8,640]{2,1,0:T(8,128)S(1)}, u32[]{:S(2)}, u32[]{:S(2)}) collective-permute-start(f32[2,8,640]{2,1,0:T(8,128)S(1)} %pad_maximum_fusion.t0), channel_id=1, source_target_pairs={{0,2},{1,3},{2,0},{3,1},{4,6},{5,7},{6,4},{7,5},{8,10},{9,11},{10,... | collective-permute-start | bytes 122888 | tf_op jit(solution)/shard_map/ppermute | solution.py:562
  17.2 0.0 collective-permute-start.1
  17.2 2.8 %carry.1 = (bf16[2,512,256]{2,1,0:T(8,128)(2,1)}, bf16[2,192,512]{2,1,0:T(8,128)(2,1)}, f32[8,128]{1,0:T(8,128)}, f32[2,16,2048]{2,1,0:T(8,128)}, bf16[2,16,2048]{2,1,0:T(8,128)(2,1)}) custom-call(f32[64,128,128]{2,1,0:T(8,128)} %block_x.3, f32[32,128,128]{2,1,0:T(8,128)} %block_y.3, f32[128,128]{1,0:T(8,128)} %reduced_x_hbm.1, f32[64,64]{1,0:T(8,128)} %reduced_y_hbm.1, ...), custom_call_target="tpu_custom_call" | custom-call | flops 68719476736 | bytes 2097152 | tf_op jit(solution)/shard_map/carry/pallas_call | solution.py:257
  20.1 0.0 collective-permute-done.3.t3
  20.1 0.0 collective-permute-done.2.t2
  20.1 0.0 collective-permute-done.1.t1
  20.1 2.5 %all-to-all-done.tx = f32[16,8,640]{2,1,0:T(8,128)S(1)} async-done(((f32[16,8,640]{2,1,0:T(8,128)}), f32[16,8,640]{2,1,0:T(8,128)S(1)}, u32[]{:S(2)}, u32[]{:S(2)}) %all-to-all-start) | async-done | bytes 327712 | tf_op jit(solution)/shard_map/all_to_all | solution.py:558
  22.7 6.3 %elevation.1 = (f32[3,512,512]{2,1,0:T(8,128)}, f32[128,128]{1,0:T(8,128)}, f32[1,512]{1,0:T(1,128)S(1)}, f32[1,512]{1,0:T(1,128)S(1)}) custom-call(f32[16,8,640]{2,1,0:T(8,128)S(1)} %all-to-all-done.tx, f32[2,8,640]{2,1,0:T(8,128)S(1)} %pad_maximum_fusion.t0, f32[2,8,640]{2,1,0:T(8,128)S(1)} %collective-permute-done.1.t1, ...), custom_call_target="tpu_custom_call" | custom-call | flops 402653184 | bytes 10485760 | tf_op jit(solution)/shard_map/elevation/pallas_call | solution.py:466
  28.9 5.6 %all-to-all-start.1 = ((f32[128,1,128]{2,1,0:T(1,128)}), f32[128,1,128]{2,1,0:T(1,128)S(1)}, u32[]{:S(2)}, u32[]{:S(2)}) async-start(f32[128,1,128]{2,1,0:T(1,128)} %bitcast.17), calls=%async_computation.1 | async-start | bytes 131072 | tf_op jit(solution)/shard_map/all_to_all | solution.py:567
  34.5 5.6 %collective-permute-start.4 = (f32[1,512]{1,0:T(1,128)S(1)}, f32[1,512]{1,0:T(1,128)S(1)}, u32[]{:S(2)}, u32[]{:S(2)}) collective-permute-start(f32[1,512]{1,0:T(1,128)S(1)} %get-tuple-element.24), channel_id=1, source_target_pairs={{0,120},{8,0},{16,8},{24,16},{32,24},{40,32},{48,40},{56,48},{64,5... | collective-permute-start | bytes 6152 | tf_op jit(solution)/shard_map/ppermute | solution.py:565
  40.2 0.6 %collective-permute-start.5 = (f32[1,512]{1,0:T(1,128)S(1)}, f32[1,512]{1,0:T(1,128)S(1)}, u32[]{:S(2)}, u32[]{:S(2)}) collective-permute-start(f32[1,512]{1,0:T(1,128)S(1)} %get-tuple-element.25), channel_id=1, source_target_pairs={{0,7},{1,0},{2,1},{3,2},{4,3},{5,4},{6,5},{7,6},{8,15},{9,8},{10,9... | collective-permute-start | bytes 6152 | tf_op jit(solution)/shard_map/ppermute | solution.py:566
  40.8 1.0 %slice_bitcast_fusion.edge_in = f32[512,128]{1,0:T(8,128)S(1)} fusion(f32[3,512,512]{2,1,0:T(8,128)} %get-tuple-element.22.fields_in), kind=kLoop, calls=%fused_computation | loop fusion | bytes 524288 | tf_op jit(solution)/shard_map/squeeze | solution.py:524
  41.8 0.7 %slice_bitcast_fusion.1.bottom_in = f32[8,512]{1,0:T(8,128)S(1)} fusion(f32[3,512,512]{2,1,0:T(8,128)} %get-tuple-element.22.fields_in), kind=kLoop, calls=%fused_computation.2 | loop fusion | bytes 32768 | tf_op jit(solution)/shard_map/squeeze | solution.py:523
  42.5 0.0 collective-permute-done.4.hrow
  42.5 1.0 %collective-permute-done.5.hcol = f32[1,512]{1,0:T(1,128)S(1)} collective-permute-done((f32[1,512]{1,0:T(1,128)S(1)}, f32[1,512]{1,0:T(1,128)S(1)}, u32[]{:S(2)}, u32[]{:S(2)}) %collective-permute-start.5) | collective-permute-done | bytes 2080 | tf_op jit(solution)/shard_map/ppermute | solution.py:566
  43.5 0.8 %all-to-all-done.1 = f32[128,1,128]{2,1,0:T(1,128)S(1)} async-done(((f32[128,1,128]{2,1,0:T(1,128)}), f32[128,1,128]{2,1,0:T(1,128)S(1)}, u32[]{:S(2)}, u32[]{:S(2)}) %all-to-all-start.1) | async-done | bytes 65568 | tf_op jit(solution)/shard_map/all_to_all | solution.py:567
  44.3 1.0 %finish.1 = (f32[3,512,512]{2,1,0:T(8,128)}, f32[1,16]{1,0:T(1,128)}) custom-call(f32[3,512,512]{2,1,0:T(8,128)} %get-tuple-element.22.fields_in, f32[128,128]{1,0:T(8,128)S(1)} %bitcast.14, f32[1,512]{1,0:T(1,128)S(1)} %collective-permute-done.4.hrow, f32[1,512]{1,0:T(1,128)S(1)} %collective-permute-done.5.hcol, ...), custom_call_target="tpu_custom_call", output_to_operand_aliasing={{0}: (0, {})} | custom-call | flops 1048576 | bytes 1048576 | tf_op jit(solution)/shard_map/finish/pallas_call | solution.py:525
  (1 shorter events, 0.0 us)
Async XLA Ops:
  3.1 11.4 %collective-permute-start = (f32[1,8,640]{2,1,0:T(8,128)S(1)}, f32[1,8,640]{2,1,0:T(8,128)S(1)}, u32[]{:S(2)}, u32[]{:S(2)}) collective-permute-start(f32[1,8,640]{2,1,0:T(8,128)S(1)} %bitcast.15), channel_id=1, source_target_pairs={{0,4},{1,5},{2,6},{3,7},{4,0},{5,1},{6,2},{7,3},{8,12},{9,13},{10,... | collective-permute-start | bytes 61448 | tf_op jit(solution)/shard_map/ppermute | solution.py:561
  7.0 15.7 %all-to-all-start = ((f32[16,8,640]{2,1,0:T(8,128)}), f32[16,8,640]{2,1,0:T(8,128)S(1)}, u32[]{:S(2)}, u32[]{:S(2)}) async-start(f32[16,8,640]{2,1,0:T(8,128)} %get-tuple-element.15), calls=%async_computation | async-start | bytes 655360 | tf_op jit(solution)/shard_map/all_to_all | solution.py:558
  14.6 5.5 %collective-permute-start.3 = (f32[2,8,640]{2,1,0:T(8,128)S(1)}, f32[2,8,640]{2,1,0:T(8,128)S(1)}, u32[]{:S(2)}, u32[]{:S(2)}) collective-permute-start(f32[2,8,640]{2,1,0:T(8,128)S(1)} %pad_maximum_fusion.t0), channel_id=1, source_target_pairs={{0,3},{1,2},{2,1},{3,0},{4,7},{5,6},{6,5},{7,4},{8,11},{9,10},{10,... | collective-permute-start | bytes 122888 | tf_op jit(solution)/shard_map/ppermute | solution.py:562
  16.2 3.9 %collective-permute-start.2 = (f32[2,8,640]{2,1,0:T(8,128)S(1)}, f32[2,8,640]{2,1,0:T(8,128)S(1)}, u32[]{:S(2)}, u32[]{:S(2)}) collective-permute-start(f32[2,8,640]{2,1,0:T(8,128)S(1)} %pad_maximum_fusion.t0), channel_id=1, source_target_pairs={{0,2},{1,3},{2,0},{3,1},{4,6},{5,7},{6,4},{7,5},{8,10},{9,11},{10,... | collective-permute-start | bytes 122888 | tf_op jit(solution)/shard_map/ppermute | solution.py:562
  17.2 2.9 %collective-permute-start.1 = (f32[2,8,640]{2,1,0:T(8,128)S(1)}, f32[2,8,640]{2,1,0:T(8,128)S(1)}, u32[]{:S(2)}, u32[]{:S(2)}) collective-permute-start(f32[2,8,640]{2,1,0:T(8,128)S(1)} %pad_maximum_fusion.t0), channel_id=1, source_target_pairs={{0,1},{1,0},{2,3},{3,2},{4,5},{5,4},{6,7},{7,6},{8,9},{9,8},{10,11... | collective-permute-start | bytes 122888 | tf_op jit(solution)/shard_map/ppermute | solution.py:562
  28.9 15.3 %all-to-all-start.1 = ((f32[128,1,128]{2,1,0:T(1,128)}), f32[128,1,128]{2,1,0:T(1,128)S(1)}, u32[]{:S(2)}, u32[]{:S(2)}) async-start(f32[128,1,128]{2,1,0:T(1,128)} %bitcast.17), calls=%async_computation.1 | async-start | bytes 131072 | tf_op jit(solution)/shard_map/all_to_all | solution.py:567
  34.5 8.0 %collective-permute-start.4 = (f32[1,512]{1,0:T(1,128)S(1)}, f32[1,512]{1,0:T(1,128)S(1)}, u32[]{:S(2)}, u32[]{:S(2)}) collective-permute-start(f32[1,512]{1,0:T(1,128)S(1)} %get-tuple-element.24), channel_id=1, source_target_pairs={{0,120},{8,0},{16,8},{24,16},{32,24},{40,32},{48,40},{56,48},{64,5... | collective-permute-start | bytes 6152 | tf_op jit(solution)/shard_map/ppermute | solution.py:565
  40.2 3.3 %collective-permute-start.5 = (f32[1,512]{1,0:T(1,128)S(1)}, f32[1,512]{1,0:T(1,128)S(1)}, u32[]{:S(2)}, u32[]{:S(2)}) collective-permute-start(f32[1,512]{1,0:T(1,128)S(1)} %get-tuple-element.25), channel_id=1, source_target_pairs={{0,7},{1,0},{2,1},{3,2},{4,3},{5,4},{6,5},{7,6},{8,15},{9,8},{10,9... | collective-permute-start | bytes 6152 | tf_op jit(solution)/shard_map/ppermute | solution.py:566
